TPU v7x, 128 devices: a whole 4x4x4 slice. The times are simulated.
128 devices in a mesh: rows: 16 (over y, x), pb: 8 (over z, core).
Axes of the slice: x: 4, y: 4, z: 4, core: 2. Of those that a mesh axis runs over, the one named last changes fastest.
Arguments:
- lower_panel: bfloat16 [2, 16384, 2048], P(None, 'rows'), may hold values from -0.1875 to 0.1875
- sparse_desc: bfloat16 [2, 16384, 1024], P(None, 'rows', 'pb'), may hold values from -6 to 6
- query_desc: bfloat16 [8192, 1024], P('pb', 'rows'), may hold values from -6 to 6
- diag_inv: bfloat16 [2, 1024, 1024], replicated, may hold values from -0.1875 to 0.1875
Outputs:
- partial_solve: bfloat16 [2, 16384, 8192], P(None, 'rows', 'pb')
All inputs are finite; a program needn't handle non-finite values.
Results may differ from a plain program's by a relative error of at most 0.006.
Values may be sent and summed in bfloat16 or wider, within the bound.
No kernel may reach another device: no remote copies, remote signals or barrier semaphores. Data moves between devices by JAX's collectives and lax.ppermute only.
A program may use at most 128 MiB of HBM per device.

v0:
```python
import jax
import jax.numpy as jnp
from jax import lax
from jax.sharding import PartitionSpec as P


def spread(block, axis, holder):
    block = jnp.where(lax.axis_index(axis) == holder, block, jnp.zeros_like(block))
    return lax.psum(block, axis)


def per_device(lower_panel, sparse_desc, query_desc, diag_inv):
    width = diag_inv.shape[1]
    queries = query_desc.shape[0]
    whole_query = lax.all_gather(query_desc, "rows", axis=1, tiled=True)
    feats = whole_query.shape[1]
    here = lax.axis_index("rows")
    dots = jnp.einsum(
        "sbf,qf->sbq",
        lax.all_gather(sparse_desc, "pb", axis=2, tiled=True),
        whole_query,
        preferred_element_type=jnp.float32,
    )
    scaled = dots / jnp.sqrt(jnp.float32(feats))
    kstar = scaled * scaled
    blank = jnp.zeros((width, queries), jnp.bfloat16)

    def solve(which, rhs):
        return jnp.dot(
            diag_inv[which], rhs.astype(jnp.bfloat16), preferred_element_type=jnp.float32
        ).astype(jnp.bfloat16)

    own_first = lax.cond(here == 0, lambda: solve(0, kstar[0]), lambda: blank)
    solved0 = spread(own_first, "rows", 0)
    resid = kstar - jnp.einsum(
        "sbk,kq->sbq", lower_panel[:, :, :width], solved0, preferred_element_type=jnp.float32
    )
    own_second = lax.cond(here == 1, lambda: solve(1, resid[0]), lambda: blank)
    solved1 = spread(own_second, "rows", 1)
    resid = resid - jnp.einsum(
        "sbk,kq->sbq", lower_panel[:, :, width:], solved1, preferred_element_type=jnp.float32
    )
    output = resid.astype(jnp.bfloat16)
    first_row = jnp.where(here == 0, solved0, jnp.where(here == 1, solved1, output[0]))
    return output.at[0].set(first_row)


def solution(mesh):
    return jax.shard_map(
        per_device,
        mesh=mesh,
        in_specs=(P(None, "rows", None), P(None, "rows", "pb"), P("pb", "rows"), P()),
        out_specs=P(None, "rows", "pb"),
        check_vma=False,
    )
```

profile of v0, /device:TPU:6, one launch (start us, length us, event | category | flops | bytes accessed | tf_op | source)
XLA Modules:
  0.0 326.9 jit_solution(209369793626751538)
XLA Ops:
  6.5 0.0 all-gather.5.cloned.1.call-start
  6.5 0.7 all-gather.5.cloned.1.call-update
  7.3 0.0 all-gather.3.cloned.1.call-start
  7.3 0.7 all-gather.3.cloned.1.call-update
  8.0 0.0 all-reduce.3.cloned.1.call-start
  8.1 48.3 %all-gather.5.cloned.1.call-done = bf16[1024,1024]{0,1:T(8,128)(2,1)} async-done(((bf16[1024,64]{0,1:T(8,128)(2,1)}), bf16[1024,1024]{0,1:T(8,128)(2,1)}) %all-gather.5.cloned.1.call-update) | async-done | bytes 2097168 | tf_op jit(solution)/shard_map/all_gather | solution.py:15
  56.3 37.7 %all-gather.3.cloned.1.call-done = bf16[2,1024,1024]{2,1,0:T(8,128)(2,1)} async-done(((bf16[2,1024,128]{2,1,0:T(8,128)(2,1)}), bf16[2,1024,1024]{2,1,0:T(8,128)(2,1)}) %all-gather.3.cloned.1.call-update) | async-done | bytes 4194320 | tf_op jit(solution)/shard_map/all_gather | solution.py:20
  94.0 10.6 %multiply_multiply_fusion = f32[2,1024,1024]{2,1,0:T(8,128)} fusion(bf16[2,1024,1024]{2,1,0:T(8,128)(2,1)} %all-gather.3.cloned.1.call-done, bf16[1024,1024]{0,1:T(8,128)(2,1)} %all-gather.5.cloned.1.call-done), kind=kOutput, calls=%fused_computation.15 | convolution fusion | flops 4299161600 | bytes 14680064 | tf_op jit(solution)/shard_map/sbf,qf->sbq/dot_general | solution.py:18
  104.6 0.3 conditional.2
  104.6 0.3 broadcast.32
  104.9 1.5 broadcast_select_fusion.1
  106.4 0.0 all-reduce.3.cloned.1.call-update
  106.4 0.0 all-reduce.5.cloned.1.call-start
  106.4 90.7 %all-reduce.3.cloned.1.call-done = bf16[1024,1024]{1,0:T(8,128)(2,1)} async-done(((bf16[1024,1024]{1,0:T(8,128)(2,1)}), bf16[1024,1024]{1,0:T(8,128)(2,1)}) %all-reduce.3.cloned.1.call-update) | async-done | bytes 2097168 | tf_op jit(solution)/shard_map/psum | solution.py:9
  197.2 13.0 %bitcast_subtract_fusion.1 = f32[2,1024,1024]{2,1,0:T(8,128)} fusion(f32[2,1024,1024]{2,1,0:T(8,128)} %multiply_multiply_fusion, bf16[2,1024,2048]{2,1,0:T(8,128)(2,1)} %param.10, bf16[1024,1024]{1,0:T(8,128)(2,1)} %all-reduce.3.cloned.1.call-done), kind=kOutput, calls=%fused_computation.14 | convolution fusion | flops 4297064448 | bytes 23068672 | tf_op jit(solution)/shard_map/sbk,kq->sbq/dot_general | solution.py:35
  210.1 0.4 conditional.3
  210.1 0.3 broadcast.33
  210.6 1.5 broadcast_select_fusion
  212.1 0.0 all-reduce.5.cloned.1.call-update
  212.1 0.0 copy-start
  212.1 91.9 %all-reduce.5.cloned.1.call-done = bf16[1024,1024]{1,0:T(8,128)(2,1)} async-done(((bf16[1024,1024]{1,0:T(8,128)(2,1)}), bf16[1024,1024]{1,0:T(8,128)(2,1)}) %all-reduce.5.cloned.1.call-update) | async-done | bytes 2097168 | tf_op jit(solution)/shard_map/psum | solution.py:9
  304.0 0.0 copy-start.1
  304.0 11.9 %fusion.20 = bf16[2,1024,1024]{2,1,0:T(8,128)(2,1)} fusion(f32[2,1024,1024]{2,1,0:T(8,128)} %bitcast_subtract_fusion.1, bf16[2,1024,2048]{2,1,0:T(8,128)(2,1)} %param.10, bf16[1024,1024]{1,0:T(8,128)(2,1)} %all-reduce.5.cloned.1.call-done), kind=kOutput, calls=%fused_computation.13 | convolution fusion | flops 4299161600 | bytes 18874368 | tf_op jit(solution)/shard_map/sbk,kq->sbq/dot_general | solution.py:40
  315.9 0.0 copy-done
  315.9 0.0 copy-done.1
  315.9 4.4 %fusion.32 = bf16[2,1024,1024]{2,1,0:T(8,128)(2,1)} fusion(bf16[2,1024,1024]{2,1,0:T(8,128)(2,1)} %fusion.20, bf16[1024,1024]{1,0:T(8,128)(2,1)S(1)} %copy-done, bf16[1024,1024]{1,0:T(8,128)(2,1)S(1)} %copy-done.1, pred[]{:T(512)S(6)} %eq.5, pred[]{:T(512)S(6)} %eq.4), kind=kLoop, calls=%fused_computation.24 | loop fusion | flops 2097152 | bytes 8388610 | tf_op jit(solution)/shard_map/scatter | solution.py:45
Async XLA Ops:
  6.5 49.8 %all-gather.5.cloned.1.call-start = ((), (), s32[]{:S(2)}) async-start(), calls=%async_computation.1 | async-start | bytes 2228224 | tf_op jit(solution)/shard_map/all_gather | solution.py:15
  7.3 86.8 %all-gather.3.cloned.1.call-start = ((), (), s32[]{:S(2)}) async-start(), calls=%async_computation | async-start | bytes 4718592 | tf_op jit(solution)/shard_map/all_gather | solution.py:20
  8.0 189.2 %all-reduce.3.cloned.1.call-start = ((), (), s32[]{:S(2)}) async-start(), calls=%async_computation.2 | async-start | bytes 4194304 | tf_op jit(solution)/shard_map/psum | solution.py:9
  106.4 197.6 %all-reduce.5.cloned.1.call-start = ((), (), s32[]{:S(2)}) async-start(), calls=%async_computation.3 | async-start | bytes 4194304 | tf_op jit(solution)/shard_map/psum | solution.py:9
  212.1 103.8 %copy-start = (bf16[1024,1024]{1,0:T(8,128)(2,1)S(1)}, bf16[1024,1024]{1,0:T(8,128)(2,1)}, u32[]{:S(2)}) copy-start(bf16[1024,1024]{1,0:T(8,128)(2,1)} %all-reduce.3.cloned.1.call-done) | copy-start | bytes 6291460
  304.0 11.9 %copy-start.1 = (bf16[1024,1024]{1,0:T(8,128)(2,1)S(1)}, bf16[1024,1024]{1,0:T(8,128)(2,1)}, u32[]{:S(2)}) copy-start(bf16[1024,1024]{1,0:T(8,128)(2,1)} %all-reduce.5.cloned.1.call-done) | copy-start | bytes 6291460
Sparse Core Ops, SparseCore 0:
  9.5 46.7 all-gather.4
  58.0 35.9 all-gather.2
  106.5 90.6 all-reduce.2
  212.2 91.7 all-reduce.4
where the time goes:
time: 327 us
  waiting for transfers between devices  270 us (83%)
  matrix products  35.5 us (11%)
  between operations  13.2 us (4%)
  other arithmetic  7.34 us (2%)
    psum x2, waiting for transfers between devices, spread(): return lax.psum(block, axis)  183 us
    all_gather x1, waiting for transfers between devices, per_device(): whole_query = lax.all_gather(query_desc, 'rows', axis=1, tiled=True)  48.3 us
    all_gather x1, waiting for transfers between devices, per_device(): lax.all_gather(sparse_desc, 'pb', axis=2, tiled=True)  37.7 us
    dot_general x1, matrix products, per_device(): jnp.einsum('sbk,kq->sbq', lower_panel[:, :, :width], solved0, preferred_e...  13 us
    dot_general x1, matrix products, per_device(): jnp.einsum('sbk,kq->sbq', lower_panel[:, :, width:], solved1, preferred_e...  11.9 us
    dot_general x1, matrix products, per_device(): jnp.einsum('sbf,qf->sbq', lax.all_gather(sparse_desc, 'pb', axis=2, tiled...  10.6 us
  transfers between devices with their start and end apart: 4, of which 4 were waited for; matrix products, arithmetic and copies ran while one was open for 0% of the time, Pallas kernels for 0%

commit v1 on v0

v1 whole, which is shorter than its diff:
```python
import jax
import jax.numpy as jnp
from jax import lax
from jax.experimental import pallas as pl
from jax.experimental.pallas import tpu as pltpu
from jax.sharding import PartitionSpec as P

BF16, F32 = jnp.bfloat16, jnp.float32
VMEM_BYTES = 56 * 1024 * 1024
N = 4
TILE = 256


def x_perm(d):
    return [(r, (r // N) * N + (r % N + d) % N) for r in range(N * N)]


def y_perm(d):
    return [(r, ((r // N + d) % N) * N + r % N) for r in range(N * N)]


def z_perm(d):
    return [(p, ((p // 2 + d) % N) * 2 + p % 2) for p in range(2 * N)]


SWAP = [(p, p ^ 1) for p in range(2 * N)]


def pick(index, choices):
    out = choices[0]
    for i in range(1, len(choices)):
        out = jnp.where(index == i, choices[i], out)
    return out


def after(value, *others):
    return lax.optimization_barrier((value,) + others)[0]


def params(**kw):
    return pltpu.CompilerParams(vmem_limit_bytes=VMEM_BYTES, **kw)


def cost(flops, moved):
    return pl.CostEstimate(flops=int(flops), bytes_accessed=int(moved), transcendentals=0)


def whole():
    return pl.BlockSpec(memory_space=pltpu.VMEM)


def place_features(at, refs, dst, rows=None):
    z, core = at[2], at[3]
    for i, ref in enumerate(refs):
        zz = lax.rem(z + (0, 3, 1, 2)[i % 4], 4)
        cc = core if i < 4 else 1 - core
        off = pl.multiple_of((zz * 2 + cc) * 128, 128)
        dst[:, pl.ds(off, 128)] = ref[...]


def kernel_slices(at, qt, s0, s1, s2, s3, s4, s5, s6, s7, k0, k1, feats):
    place_features(at, (s0, s1, s2, s3, s4, s5, s6, s7), feats)
    half = k0.shape[0]
    scale = 1.0 / (qt.shape[0] ** 0.5)

    def step(i, _):
        cols = pl.ds(pl.multiple_of(i * TILE, TILE), TILE)
        dots = jnp.dot(feats[...], qt[:, cols], preferred_element_type=F32) * scale
        k = dots * dots
        k0[:, cols] = k[:half].astype(BF16)
        k1[:, cols] = k[half:]
        return 0

    lax.fori_loop(0, qt.shape[1] // TILE, step, 0)


def place_rows(at, refs, dst):
    color = lax.rem(at[0] + 2 * at[1], 4)
    for add, ref in zip((0, 1, 3, 2), refs):
        off = pl.multiple_of(lax.rem(color + add, 4) * ref.shape[0], ref.shape[0])
        dst[pl.ds(off, ref.shape[0]), :] = ref[...]


def first_solve(at, a, b, c, d, inv, la, lb, k1, s0, t, rhs):
    place_rows(at, (a, b, c, d), rhs)
    core = at[3]
    half = la.shape[1]
    off_a = pl.multiple_of(core * half, half)
    off_b = pl.multiple_of((1 - core) * half, half)

    def step(i, _):
        cols = pl.ds(pl.multiple_of(i * TILE, TILE), TILE)
        s0[:, cols] = jnp.dot(inv[...], rhs[:, cols], preferred_element_type=F32).astype(BF16)
        low = jnp.dot(la[...], s0[pl.ds(off_a, half), cols], preferred_element_type=F32)
        low = low + jnp.dot(lb[...], s0[pl.ds(off_b, half), cols], preferred_element_type=F32)
        t[:, cols] = (k1[:, cols] - low).astype(BF16)
        return 0

    lax.fori_loop(0, rhs.shape[1] // TILE, step, 0)


def residual(at, qt, s0, low, p0, p1, p2, p3, p4, p5, p6, p7, out, feats):
    place_features(at, (p0, p1, p2, p3, p4, p5, p6, p7), feats)
    scale = 1.0 / (qt.shape[0] ** 0.5)
    dots = jnp.dot(feats[...], qt[...], preferred_element_type=F32) * scale
    out[...] = dots * dots - jnp.dot(low[...], s0[...], preferred_element_type=F32)


def last_step(at, a, b, c, d, inv, s0, low, res, out, rhs, s1):
    i = pl.program_id(0)
    here = at[0] + 4 * at[1]
    bm = out.shape[0]
    per_block = s1.shape[0] // bm

    @pl.when(i == 0)
    def _():
        place_rows(at, (a, b, c, d), rhs)

        def step(j, _):
            cols = pl.ds(pl.multiple_of(j * TILE, TILE), TILE)
            s1[:, cols] = jnp.dot(inv[...], rhs[:, cols], preferred_element_type=F32).astype(BF16)
            return 0

        lax.fori_loop(0, rhs.shape[1] // TILE, step, 0)

    rows = pl.ds(pl.multiple_of(lax.rem(i, per_block) * bm, bm), bm)
    first = i < per_block

    @pl.when(jnp.logical_and(first, here == 0))
    def _():
        out[...] = s0[rows, :]

    @pl.when(jnp.logical_and(first, here == 1))
    def _():
        out[...] = s1[rows, :]

    @pl.when(jnp.logical_not(jnp.logical_and(first, here < 2)))
    def _():
        out[...] = (res[...] - jnp.dot(low[...], s1[...], preferred_element_type=F32)).astype(BF16)


def per_device(lower_panel, sparse_desc, query_desc, diag_inv):
    blocks, width, _ = lower_panel.shape
    queries = query_desc.shape[0]
    here, part = lax.axis_index("rows"), lax.axis_index("pb")
    x, y = here % N, here // N
    z, core = part // 2, part % 2
    at = jnp.stack([x, y, z, core]).astype(jnp.int32)
    smem = pl.BlockSpec(memory_space=pltpu.SMEM)
    quarter = width // 4
    piece = sparse_desc.shape[2]
    feats = piece * 2 * N

    qt = query_desc.T
    qt = jnp.broadcast_to(qt[None], (N * N,) + qt.shape)
    qt = lax.all_to_all(qt, "rows", 0, 0, tiled=True).reshape(feats, queries)

    first = sparse_desc[0].reshape(4, quarter, piece)

    def two(d):
        return jnp.concatenate(
            [lax.dynamic_index_in_dim(first, (x + d + e) % 4, 0, False) for e in (0, 2)]
        )

    got = [two(0)] + [
        lax.ppermute(two(d), "rows", [(0, d), (1, (1 + d) % N)]) for d in (1, 2, 3)
    ]
    from0 = pick(x, got)
    from1 = pick((x + 3) % N, got)
    even = jnp.concatenate([from0[:quarter], from1[:quarter]])
    odd = jnp.concatenate([from0[quarter:], from1[quarter:]])
    got_y = [even] + [
        lax.ppermute(even if d == 2 else odd, "rows", [(c, d * N + c) for c in range(N)])
        for d in (1, 2, 3)
    ]
    mine = pick(y, got_y)
    slices = [mine] + [lax.ppermute(mine, "pb", z_perm(d)) for d in (1, -1, 2)]
    slices = slices + [lax.ppermute(v, "pb", SWAP) for v in slices]

    low = lax.dynamic_slice_in_dim(lower_panel[0], core * (width // 2), width // 2, 1)
    low = low.reshape(4, quarter, width // 2)
    low = after(low, got[1], got[2], got[3])

    def two_low(d):
        return jnp.concatenate([low[(1 + d) % 4], low[(3 + d) % 4]])

    got_l = [two_low(0)] + [
        lax.ppermute(two_low(d), "rows", [(1, (1 + d) % N)]) for d in (1, 2, 3)
    ]
    from_l = pick((x + 3) % N, got_l)
    even_l, odd_l = from_l[:quarter], from_l[quarter:]
    got_ly = [even_l] + [
        lax.ppermute(even_l if d == 2 else odd_l, "rows", [(c, d * N + c) for c in range(N)])
        for d in (1, 2, 3)
    ]
    low_a = pick(y, got_ly)
    low_b = lax.ppermute(low_a, "pb", SWAP)

    own = sparse_desc.reshape(blocks * width, piece)
    own_z = after(own, slices[1], slices[2], slices[3])
    envs = [own] + [lax.ppermute(own_z, "pb", z_perm(d)) for d in (1, -1, 2)]
    envs = envs + [lax.ppermute(v, "pb", SWAP) for v in envs]

    unit = 2 * width * feats * queries
    k0, k1 = pl.pallas_call(
        kernel_slices,
        out_shape=(
            jax.ShapeDtypeStruct((quarter, queries), BF16),
            jax.ShapeDtypeStruct((quarter, queries), F32),
        ),
        in_specs=[smem] + [whole()] * 9,
        out_specs=(whole(), whole()),
        scratch_shapes=[pltpu.VMEM((2 * quarter, feats), BF16)],
        compiler_params=params(),
        cost_estimate=cost(unit / 2, 5e6),
    )(at, qt, *slices)

    def neighbours(v):
        return (
            v,
            lax.ppermute(v, "rows", x_perm(-1)),
            lax.ppermute(v, "rows", x_perm(1)),
            lax.ppermute(v, "rows", y_perm(-1)),
        )

    block = pl.BlockSpec((None, width, width), lambda *_: (0, 0, 0), memory_space=pltpu.VMEM)
    s0, t = pl.pallas_call(
        first_solve,
        grid=(1,),
        out_shape=(
            jax.ShapeDtypeStruct((width, queries), BF16),
            jax.ShapeDtypeStruct((quarter, queries), BF16),
        ),
        in_specs=[smem] + [whole()] * 4 + [block] + [whole()] * 3,
        out_specs=(whole(), whole()),
        scratch_shapes=[pltpu.VMEM((width, queries), BF16)],
        compiler_params=params(),
        cost_estimate=cost(unit * 1.25, 8e6),
    )(at, *neighbours(k0), diag_inv, low_a, low_b, k1)

    bm = TILE
    rows = blocks * width
    panel = lower_panel.reshape(rows, 2 * width)
    res = pl.pallas_call(
        residual,
        grid=(rows // bm,),
        out_shape=jax.ShapeDtypeStruct((rows, queries), F32),
        in_specs=[smem, whole(), whole(), pl.BlockSpec((bm, width), lambda i: (i, 0))]
        + [pl.BlockSpec((bm, piece), lambda i: (i, 0))] * 8,
        out_specs=pl.BlockSpec((bm, queries), lambda i: (i, 0)),
        scratch_shapes=[pltpu.VMEM((bm, feats), BF16)],
        compiler_params=params(),
        cost_estimate=cost(unit * 4, 22e6),
    )(at, qt, s0, panel, *envs)

    block1 = pl.BlockSpec((None, width, width), lambda *_: (1, 0, 0), memory_space=pltpu.VMEM)
    out = pl.pallas_call(
        last_step,
        grid=(rows // bm,),
        out_shape=jax.ShapeDtypeStruct((rows, queries), BF16),
        in_specs=[smem]
        + [whole()] * 4
        + [
            block1,
            whole(),
            pl.BlockSpec((bm, width), lambda i: (i, 1)),
            pl.BlockSpec((bm, queries), lambda i: (i, 0)),
        ],
        out_specs=pl.BlockSpec((bm, queries), lambda i: (i, 0)),
        scratch_shapes=[pltpu.VMEM((width, queries), BF16), pltpu.VMEM((width, queries), BF16)],
        compiler_params=params(),
        cost_estimate=cost(unit * 3, 20e6),
    )(at, *neighbours(t), diag_inv, s0, panel, res)
    return out.reshape(blocks, width, queries)


def solution(mesh):
    return jax.shard_map(
        per_device,
        mesh=mesh,
        in_specs=(P(None, "rows", None), P(None, "rows", "pb"), P("pb", "rows"), P()),
        out_specs=P(None, "rows", "pb"),
        check_vma=False,
    )
```

time: 327 us -> 164 us (0.50)
  waiting for transfers between devices: 270 us -> 36.7 us
  starting transfers between devices: 0.12 us -> 58.9 us
  Pallas kernels: 0 us -> 45.6 us
  matrix products: 35.5 us -> 0 us
  local copies, waits for them, and re-layouts: 0.51 us -> 16.4 us
  between operations: 13.2 us -> 0.47 us
  other arithmetic: 7.34 us -> 4.06 us
    psum x2 -> x0, waiting for transfers between devices: 183 us -> none  [spread(): return lax.psum(block, axis)]
    all_gather x2 -> x0, waiting for transfers between devices: 86 us -> none  [the longest x1 48.3 us: per_device(): whole_query = lax.all_gather(query_desc, 'rows', axis=1, tiled=True)]
    ppermute x0 -> x33, starting transfers between devices: none -> 47.4 us  [the longest x2 9.92 us: neighbours(): lax.ppermute(v, 'rows', x_perm(1))]
    pallas_call x0 -> x4, Pallas kernels: none -> 45.6 us  [the longest x1 16 us: per_device(): pl.pallas_call(last_step, grid=(rows // bm,), out_shape=jax.ShapeDtypeStr...]
    ppermute x0 -> x33, waiting for transfers between devices: none -> 36.7 us  [the longest x3 11.3 us: per_device(): envs = [own] + [lax.ppermute(own_z, 'pb', z_perm(d)) for d in (1, -1, 2)]]
    dot_general x3 -> x0, matrix products: 35.5 us -> none  [the longest x1 13 us: per_device(): jnp.einsum('sbk,kq->sbq', lower_panel[:, :, :width], solved0, preferred_e...]
    all_to_all x0 -> x1, starting transfers between devices: none -> 11.5 us  [per_device(): qt = lax.all_to_all(qt, 'rows', 0, 0, tiled=True).reshape(feats, queries)]
    slice x0 -> x4, local copies, waits for them, and re-layouts: none -> 6.51 us  [the longest x1 4.79 us: per_device(): lower_panel[0]]
  transfers between devices with their start and end apart: 4 -> 34, of which waited for: 4 -> 5; matrix products, arithmetic and copies ran while one was open for 0% -> 8% of each run, Pallas kernels for 0% -> 18%
where the time goes in v1:
time: 164 us; the launch traced here: 162 us
  starting transfers between devices  58.9 us (36%)
  Pallas kernels  45.6 us (28%)
  waiting for transfers between devices  36.7 us (22%)
  local copies, waits for them, and re-layouts  16.4 us (10%)
  other arithmetic  4.06 us (2%)
    pallas_call x1, Pallas kernels, per_device(): pl.pallas_call(last_step, grid=(rows // bm,), out_shape=jax.ShapeDtypeStr...  16 us
    pallas_call x1, Pallas kernels, per_device(): pl.pallas_call(residual, grid=(rows // bm,), out_shape=jax.ShapeDtypeStru...  15.4 us
    all_to_all x1, starting transfers between devices, per_device(): qt = lax.all_to_all(qt, 'rows', 0, 0, tiled=True).reshape(feats, queries)  11.5 us
    ppermute x3, waiting for transfers between devices, per_device(): envs = [own] + [lax.ppermute(own_z, 'pb', z_perm(d)) for d in (1, -1, 2)]  11.3 us
    ppermute x2, starting transfers between devices, neighbours(): lax.ppermute(v, 'rows', x_perm(1))  9.92 us
    ppermute x3, waiting for transfers between devices, per_device(): lax.ppermute(even if d == 2 else odd, 'rows', [(c, d * N + c) for c in ra...  9.6 us
    pallas_call x1, Pallas kernels, per_device(): pl.pallas_call(first_solve, grid=(1,), out_shape=(jax.ShapeDtypeStruct((w...  8.94 us
    ppermute x3, starting transfers between devices, per_device(): lax.ppermute(even_l if d == 2 else odd_l, 'rows', [(c, d * N + c) for c i...  8.56 us
  transfers between devices with their start and end apart: 34, of which 5 were waited for; matrix products, arithmetic and copies ran while one was open for 8% of the time, Pallas kernels for 18%

profile of v1, /device:TPU:6, one launch (start us, length us, event | category | flops | bytes accessed | tf_op | source)
XLA Modules:
  0.0 162.2 jit_solution(10972728070783298547)
XLA Ops:
  1.1 1.3 collective-permute-start.1
  2.4 1.3 collective-permute-start
  4.4 2.5 %broadcast_in_dim.2 = bf16[16,64,1024]{2,1,0:T(8,128)(2,1)} broadcast(bf16[64,1024]{1,0:T(8,128)(2,1)} %bitcast.37), dimensions={1,2} | broadcast | bytes 2228224 | tf_op jit(solution)/shard_map/broadcast_in_dim | solution.py:155
  6.9 11.5 %all-to-all-start = ((bf16[16,64,1024]{2,1,0:T(8,128)(2,1)}), bf16[16,64,1024]{2,1,0:T(8,128)(2,1)S(1)}, u32[]{:S(2)}, u32[]{:S(2)}) async-start(bf16[16,64,1024]{2,1,0:T(8,128)(2,1)} %broadcast_in_dim.2), calls=%async_computation | async-start | bytes 4194304 | tf_op jit(solution)/shard_map/all_to_all | solution.py:156
  18.4 4.8 %slice.45 = bf16[1,1024,2048]{2,1,0:T(8,128)(2,1)} slice(bf16[2,1024,2048]{2,1,0:T(8,128)(2,1)} %param.4), slice={[0:1], [0:1024], [0:2048]} | slice | bytes 8388608 | tf_op jit(solution)/shard_map/slice | solution.py:180
  23.2 1.3 constant_dynamic-slice_fusion
  24.7 4.7 %collective-permute-start.3 = (bf16[512,128]{1,0:T(8,128)(2,1)S(1)}, bf16[512,128]{1,0:T(8,128)(2,1)S(1)}, u32[]{:S(2)}, u32[]{:S(2)}) collective-permute-start(bf16[512,128]{1,0:T(8,128)(2,1)S(1)} %pad_maximum_fusion.7), channel_id=1, source_target_pairs={{0,96},{8,104},{16,112},{24,120},{1,97},{9,105},{17,113},{25,121},... | collective-permute-start | bytes 393224 | tf_op jit(solution)/shard_map/ppermute | solution.py:173
  29.4 1.3 collective-permute-start.5
  32.9 1.3 collective-permute-start.4
  35.3 1.5 collective-permute-start.16
  36.7 9.6 %collective-permute-done.4 = bf16[512,128]{1,0:T(8,128)(2,1)S(1)} collective-permute-done((bf16[512,128]{1,0:T(8,128)(2,1)S(1)}, bf16[512,128]{1,0:T(8,128)(2,1)S(1)}, u32[]{:S(2)}, u32[]{:S(2)}) %collective-permute-start.4) | collective-permute-done | bytes 131104 | tf_op jit(solution)/shard_map/ppermute | solution.py:173
  46.3 1.5 collective-permute-start.18
  47.9 2.0 %collective-permute-start.6 = (bf16[512,128]{1,0:T(8,128)(2,1)S(1)}, bf16[512,128]{1,0:T(8,128)(2,1)S(1)}, u32[]{:S(2)}, u32[]{:S(2)}) collective-permute-start(bf16[512,128]{1,0:T(8,128)(2,1)S(1)} %select_select_fusion.1.s0), channel_id=1, source_target_pairs={{0,2},{1,3},{2,4},{3,5},{4,6},{5,7},{6,0},{7,1},{8,10},{9,11},{10,... | collective-permute-start | bytes 393224 | tf_op jit(solution)/shard_map/ppermute | solution.py:177
  49.9 2.2 %collective-permute-start.7 = (bf16[512,128]{1,0:T(8,128)(2,1)S(1)}, bf16[512,128]{1,0:T(8,128)(2,1)S(1)}, u32[]{:S(2)}, u32[]{:S(2)}) collective-permute-start(bf16[512,128]{1,0:T(8,128)(2,1)S(1)} %select_select_fusion.1.s0), channel_id=1, source_target_pairs={{0,6},{1,7},{2,0},{3,1},{4,2},{5,3},{6,4},{7,5},{8,14},{9,15},{10,... | collective-permute-start | bytes 393224 | tf_op jit(solution)/shard_map/ppermute | solution.py:177
  52.1 2.9 %collective-permute-done.6.s1 = bf16[512,128]{1,0:T(8,128)(2,1)S(1)} collective-permute-done((bf16[512,128]{1,0:T(8,128)(2,1)S(1)}, bf16[512,128]{1,0:T(8,128)(2,1)S(1)}, u32[]{:S(2)}, u32[]{:S(2)}) %collective-permute-start.6) | collective-permute-done | bytes 131104 | tf_op jit(solution)/shard_map/ppermute | solution.py:177
  54.9 1.9 %collective-permute-start.8 = (bf16[512,128]{1,0:T(8,128)(2,1)S(1)}, bf16[512,128]{1,0:T(8,128)(2,1)S(1)}, u32[]{:S(2)}, u32[]{:S(2)}) collective-permute-start(bf16[512,128]{1,0:T(8,128)(2,1)S(1)} %select_select_fusion.1.s0), channel_id=1, source_target_pairs={{0,4},{1,5},{2,6},{3,7},{4,0},{5,1},{6,2},{7,3},{8,12},{9,13},{10,... | collective-permute-start | bytes 393224 | tf_op jit(solution)/shard_map/ppermute | solution.py:177
  56.8 4.6 %collective-permute-done.8.s3 = bf16[512,128]{1,0:T(8,128)(2,1)S(1)} collective-permute-done((bf16[512,128]{1,0:T(8,128)(2,1)S(1)}, bf16[512,128]{1,0:T(8,128)(2,1)S(1)}, u32[]{:S(2)}, u32[]{:S(2)}) %collective-permute-start.8) | collective-permute-done | bytes 131104 | tf_op jit(solution)/shard_map/ppermute | solution.py:177
  62.0 1.3 fusion.1
  64.1 1.3 collective-permute-start.19
  66.0 5.3 %collective-permute-start.20 = (bf16[256,512]{1,0:T(8,128)(2,1)}, bf16[256,512]{1,0:T(8,128)(2,1)S(1)}, u32[]{:S(2)}, u32[]{:S(2)}) collective-permute-start(bf16[256,512]{1,0:T(8,128)(2,1)} %get-tuple-element.21), channel_id=1, source_target_pairs={{0,64},{8,72},{16,80},{24,88},{1,65},{9,73},{17,81},{25,89},{2,66}... | collective-permute-start | bytes 786440 | tf_op jit(solution)/shard_map/ppermute | solution.py:193
  71.3 2.0 %collective-permute-start.21 = (bf16[256,512]{1,0:T(8,128)(2,1)S(1)}, bf16[256,512]{1,0:T(8,128)(2,1)}, u32[]{:S(2)}, u32[]{:S(2)}) collective-permute-start(bf16[256,512]{1,0:T(8,128)(2,1)S(1)} %get-tuple-element.22), channel_id=1, source_target_pairs={{0,32},{8,40},{16,48},{24,56},{1,33},{9,41},{17,49},{25,57},{2,34}... | collective-permute-start | bytes 786440 | tf_op jit(solution)/shard_map/ppermute | solution.py:193
  74.0 2.7 %collective-permute-start.27 = (bf16[2048,128]{1,0:T(8,128)(2,1)}, bf16[2048,128]{1,0:T(8,128)(2,1)}, u32[]{:S(2)}, u32[]{:S(2)}) collective-permute-start(bf16[2048,128]{1,0:T(8,128)(2,1)} %bitcast.39), channel_id=1, source_target_pairs={{0,6},{1,7},{2,0},{3,1},{4,2},{5,3},{6,4},{7,5},{8,14},{9,15},{10,... | collective-permute-start | bytes 1572872 | tf_op jit(solution)/shard_map/ppermute | solution.py:201
  77.9 1.3 copy-done
  79.2 5.2 %shard_map.46 = (bf16[256,1024]{1,0:T(8,128)(2,1)}, f32[256,1024]{1,0:T(8,128)}) custom-call(s32[4]{0:T(128)} %pad_add_fusion.at, bf16[1024,1024]{1,0:T(8,128)(2,1)} %bitcast.34, bf16[512,128]{1,0:T(8,128)(2,1)} %copy-done.6, bf16[512,128]{1,0:T(8,128)(2,1)} %copy-done.15, bf16[512,128]{1,0:T(8,128)(2,1)} %copy-done.16, bf16[512,128]{1,0:T(8,128)(2,1)} %copy-done.17, ...), custom_call_target="tpu_custom_call" | custom-call | flops 1073741824 | bytes 5000000 | tf_op jit(solution)/shard_map/pallas_call | solution.py:205
  85.0 3.0 %collective-permute-start.14 = (bf16[256,1024]{1,0:T(8,128)(2,1)}, bf16[256,1024]{1,0:T(8,128)(2,1)S(1)}, u32[]{:S(2)}, u32[]{:S(2)}) collective-permute-start(bf16[256,1024]{1,0:T(8,128)(2,1)} %get-tuple-element.11.a), channel_id=1, source_target_pairs={{0,8},{8,16},{16,24},{24,0},{32,40},{40,48},{48,56},{56,32},{64,72... | collective-permute-start | bytes 1572872 | tf_op jit(solution)/shard_map/ppermute | solution.py:222
  88.2 11.3 %collective-permute-done.27.p2 = bf16[2048,128]{1,0:T(8,128)(2,1)} collective-permute-done((bf16[2048,128]{1,0:T(8,128)(2,1)}, bf16[2048,128]{1,0:T(8,128)(2,1)}, u32[]{:S(2)}, u32[]{:S(2)}) %collective-permute-start.27) | collective-permute-done | bytes 524320 | tf_op jit(solution)/shard_map/ppermute | solution.py:201
  100.6 8.3 %collective-permute-done.15.d = bf16[256,1024]{1,0:T(8,128)(2,1)S(1)} collective-permute-done((bf16[256,1024]{1,0:T(8,128)(2,1)}, bf16[256,1024]{1,0:T(8,128)(2,1)S(1)}, u32[]{:S(2)}, u32[]{:S(2)}) %collective-permute-start.15) | collective-permute-done | bytes 524320 | tf_op jit(solution)/shard_map/ppermute | solution.py:223
  109.7 8.9 %shard_map.47 = (bf16[1024,1024]{1,0:T(8,128)(2,1)}, bf16[256,1024]{1,0:T(8,128)(2,1)}) custom-call(s32[4]{0:T(128)} %pad_add_fusion.at, bf16[256,1024]{1,0:T(8,128)(2,1)} %get-tuple-element.11.a, bf16[256,1024]{1,0:T(8,128)(2,1)} %copy-done.7, bf16[256,1024]{1,0:T(8,128)(2,1)} %copy-done.9, bf16[256,1024]{1,0:T(8,128)(2,1)} %copy-done.13, ...), custom_call_target="tpu_custom_call" | custom-call | flops 2684354560 | bytes 8000000 | tf_op jit(solution)/shard_map/pallas_call | solution.py:227
  119.5 6.9 %collective-permute-start.24 = (bf16[256,1024]{1,0:T(8,128)(2,1)}, bf16[256,1024]{1,0:T(8,128)(2,1)S(1)}, u32[]{:S(2)}, u32[]{:S(2)}) collective-permute-start(bf16[256,1024]{1,0:T(8,128)(2,1)} %get-tuple-element.14.a), channel_id=1, source_target_pairs={{0,8},{8,16},{16,24},{24,0},{32,40},{40,48},{48,56},{56,32},{64,72... | collective-permute-start | bytes 1572872 | tf_op jit(solution)/shard_map/ppermute | solution.py:222
  126.4 1.5 collective-permute-start.25
  128.9 15.4 %shard_map.48.res = f32[2048,1024]{1,0:T(8,128)} custom-call(s32[4]{0:T(128)} %pad_add_fusion.at, bf16[1024,1024]{1,0:T(8,128)(2,1)} %bitcast.35, bf16[1024,1024]{1,0:T(8,128)(2,1)} %get-tuple-element.15.s0, bf16[2048,2048]{1,0:T(8,128)(2,1)} %bitcast.31, bf16[2048,128]{1,0:T(8,128)(2,1)} %bitcast.41, bf16[2048,128]{1,0:T(8,128)(2,1)} %collective-permute-done.26.p1, ...), custom_call_target="tpu_custom_call" | custom-call | flops 8589934592 | bytes 22000000 | tf_op jit(solution)/shard_map/pallas_call | solution.py:244
  146.1 16.0 %shard_map.49 = bf16[2048,1024]{1,0:T(8,128)(2,1)} custom-call(s32[4]{0:T(128)} %pad_add_fusion.at, bf16[256,1024]{1,0:T(8,128)(2,1)} %get-tuple-element.14.a, bf16[256,1024]{1,0:T(8,128)(2,1)} %copy-done.1, bf16[256,1024]{1,0:T(8,128)(2,1)} %copy-done.2, bf16[256,1024]{1,0:T(8,128)(2,1)} %copy-done.3, bf16[2,1024,1024]{2,1,0:T(8,128)(2,1)} %inv.3, ...), custom_call_target="tpu_custom_call" | custom-call | flops 6442450944 | bytes 20000000 | tf_op jit(solution)/shard_map/pallas_call | solution.py:257
  (103 shorter events, 15.3 us)
Async XLA Ops:
  1.1 23.4 %collective-permute-start.1 = (bf16[512,128]{1,0:T(8,128)(2,1)S(1)}, bf16[512,128]{1,0:T(8,128)(2,1)S(1)}, u32[]{:S(2)}, u32[]{:S(2)}) collective-permute-start(bf16[512,128]{1,0:T(8,128)(2,1)S(1)} %pad_maximum_fusion.4), channel_id=1, source_target_pairs={{0,16},{8,24},{1,17},{9,25},{2,18},{10,26},{3,19},{11,27},{4,20},{... | collective-permute-start | bytes 393224 | tf_op jit(solution)/shard_map/ppermute | solution.py:166
  2.4 22.1 %collective-permute-start = (bf16[512,128]{1,0:T(8,128)(2,1)S(1)}, bf16[512,128]{1,0:T(8,128)(2,1)S(1)}, u32[]{:S(2)}, u32[]{:S(2)}) collective-permute-start(bf16[512,128]{1,0:T(8,128)(2,1)S(1)} %get-tuple-element.38), channel_id=1, source_target_pairs={{0,24},{8,0},{1,25},{9,1},{2,26},{10,2},{3,27},{11,3},{4,28},{12,4... | collective-permute-start | bytes 393224 | tf_op jit(solution)/shard_map/ppermute | solution.py:166
  3.7 20.8 %collective-permute-start.2 = (bf16[512,128]{1,0:T(8,128)(2,1)S(1)}, bf16[512,128]{1,0:T(8,128)(2,1)S(1)}, u32[]{:S(2)}, u32[]{:S(2)}) collective-permute-start(bf16[512,128]{1,0:T(8,128)(2,1)S(1)} %get-tuple-element.37), channel_id=1, source_target_pairs={{0,8},{8,16},{1,9},{9,17},{2,10},{10,18},{3,11},{11,19},{4,12},{12... | collective-permute-start | bytes 393224 | tf_op jit(solution)/shard_map/ppermute | solution.py:166
  6.9 71.0 %all-to-all-start = ((bf16[16,64,1024]{2,1,0:T(8,128)(2,1)}), bf16[16,64,1024]{2,1,0:T(8,128)(2,1)S(1)}, u32[]{:S(2)}, u32[]{:S(2)}) async-start(bf16[16,64,1024]{2,1,0:T(8,128)(2,1)} %broadcast_in_dim.2), calls=%async_computation | async-start | bytes 4194304 | tf_op jit(solution)/shard_map/all_to_all | solution.py:156
  24.7 23.1 %collective-permute-start.3 = (bf16[512,128]{1,0:T(8,128)(2,1)S(1)}, bf16[512,128]{1,0:T(8,128)(2,1)S(1)}, u32[]{:S(2)}, u32[]{:S(2)}) collective-permute-start(bf16[512,128]{1,0:T(8,128)(2,1)S(1)} %pad_maximum_fusion.7), channel_id=1, source_target_pairs={{0,96},{8,104},{16,112},{24,120},{1,97},{9,105},{17,113},{25,121},... | collective-permute-start | bytes 393224 | tf_op jit(solution)/shard_map/ppermute | solution.py:173
  29.4 18.4 %collective-permute-start.5 = (bf16[512,128]{1,0:T(8,128)(2,1)S(1)}, bf16[512,128]{1,0:T(8,128)(2,1)S(1)}, u32[]{:S(2)}, u32[]{:S(2)}) collective-permute-start(bf16[512,128]{1,0:T(8,128)(2,1)S(1)} %pad_maximum_fusion.7), channel_id=1, source_target_pairs={{0,32},{8,40},{16,48},{24,56},{1,33},{9,41},{17,49},{25,57},{2,34}... | collective-permute-start | bytes 393224 | tf_op jit(solution)/shard_map/ppermute | solution.py:173
  31.6 29.8 %collective-permute-start.17 = (bf16[512,512]{1,0:T(8,128)(2,1)}, bf16[512,512]{1,0:T(8,128)(2,1)}, u32[]{:S(2)}, u32[]{:S(2)}) collective-permute-start(bf16[512,512]{1,0:T(8,128)(2,1)} %pad_maximum_fusion.1), channel_id=1, source_target_pairs={{8,24},{9,25},{10,26},{11,27},{12,28},{13,29},{14,30},{15,31}} | collective-permute-start | bytes 1572872 | tf_op jit(solution)/shard_map/ppermute | solution.py:188
  32.9 13.4 %collective-permute-start.4 = (bf16[512,128]{1,0:T(8,128)(2,1)S(1)}, bf16[512,128]{1,0:T(8,128)(2,1)S(1)}, u32[]{:S(2)}, u32[]{:S(2)}) collective-permute-start(bf16[512,128]{1,0:T(8,128)(2,1)S(1)} %pad_maximum_fusion.8), channel_id=1, source_target_pairs={{0,64},{8,72},{16,80},{24,88},{1,65},{9,73},{17,81},{25,89},{2,66}... | collective-permute-start | bytes 393224 | tf_op jit(solution)/shard_map/ppermute | solution.py:173
  35.3 26.7 %collective-permute-start.16 = (bf16[512,512]{1,0:T(8,128)(2,1)}, bf16[512,512]{1,0:T(8,128)(2,1)}, u32[]{:S(2)}, u32[]{:S(2)}) collective-permute-start(bf16[512,512]{1,0:T(8,128)(2,1)} %get-tuple-element.24), channel_id=1, source_target_pairs={{8,0},{9,1},{10,2},{11,3},{12,4},{13,5},{14,6},{15,7}} | collective-permute-start | bytes 1572872 | tf_op jit(solution)/shard_map/ppermute | solution.py:188
  46.3 15.7 %collective-permute-start.18 = (bf16[512,512]{1,0:T(8,128)(2,1)}, bf16[512,512]{1,0:T(8,128)(2,1)}, u32[]{:S(2)}, u32[]{:S(2)}) collective-permute-start(bf16[512,512]{1,0:T(8,128)(2,1)} %get-tuple-element.23), channel_id=1, source_target_pairs={{8,16},{9,17},{10,18},{11,19},{12,20},{13,21},{14,22},{15,23}} | collective-permute-start | bytes 1572872 | tf_op jit(solution)/shard_map/ppermute | solution.py:188
  47.9 7.1 %collective-permute-start.6 = (bf16[512,128]{1,0:T(8,128)(2,1)S(1)}, bf16[512,128]{1,0:T(8,128)(2,1)S(1)}, u32[]{:S(2)}, u32[]{:S(2)}) collective-permute-start(bf16[512,128]{1,0:T(8,128)(2,1)S(1)} %select_select_fusion.1.s0), channel_id=1, source_target_pairs={{0,2},{1,3},{2,4},{3,5},{4,6},{5,7},{6,0},{7,1},{8,10},{9,11},{10,... | collective-permute-start | bytes 393224 | tf_op jit(solution)/shard_map/ppermute | solution.py:177
  49.9 6.9 %collective-permute-start.7 = (bf16[512,128]{1,0:T(8,128)(2,1)S(1)}, bf16[512,128]{1,0:T(8,128)(2,1)S(1)}, u32[]{:S(2)}, u32[]{:S(2)}) collective-permute-start(bf16[512,128]{1,0:T(8,128)(2,1)S(1)} %select_select_fusion.1.s0), channel_id=1, source_target_pairs={{0,6},{1,7},{2,0},{3,1},{4,2},{5,3},{6,4},{7,5},{8,14},{9,15},{10,... | collective-permute-start | bytes 393224 | tf_op jit(solution)/shard_map/ppermute | solution.py:177
  56.8 8.6 %collective-permute-start.9 = (bf16[512,128]{1,0:T(8,128)(2,1)S(1)}, bf16[512,128]{1,0:T(8,128)(2,1)S(1)}, u32[]{:S(2)}, u32[]{:S(2)}) collective-permute-start(bf16[512,128]{1,0:T(8,128)(2,1)S(1)} %select_select_fusion.1.s0), channel_id=1, source_target_pairs={{0,1},{1,0},{2,3},{3,2},{4,5},{5,4},{6,7},{7,6},{8,9},{9,8},{10,11... | collective-permute-start | bytes 393224 | tf_op jit(solution)/shard_map/ppermute | solution.py:178
  61.4 9.9 %collective-permute-start.11 = (bf16[512,128]{1,0:T(8,128)(2,1)S(1)}, bf16[512,128]{1,0:T(8,128)(2,1)S(1)}, u32[]{:S(2)}, u32[]{:S(2)}) collective-permute-start(bf16[512,128]{1,0:T(8,128)(2,1)S(1)} %collective-permute-done.7.s2), channel_id=1, source_target_pairs={{0,1},{1,0},{2,3},{3,2},{4,5},{5,4},{6,7},{7,6},{8,9},{9,8},{10,11... | collective-permute-start | bytes 393224 | tf_op jit(solution)/shard_map/ppermute | solution.py:178
  61.9 11.4 %collective-permute-start.12 = (bf16[512,128]{1,0:T(8,128)(2,1)S(1)}, bf16[512,128]{1,0:T(8,128)(2,1)S(1)}, u32[]{:S(2)}, u32[]{:S(2)}) collective-permute-start(bf16[512,128]{1,0:T(8,128)(2,1)S(1)} %collective-permute-done.8.s3), channel_id=1, source_target_pairs={{0,1},{1,0},{2,3},{3,2},{4,5},{5,4},{6,7},{7,6},{8,9},{9,8},{10,11... | collective-permute-start | bytes 393224 | tf_op jit(solution)/shard_map/ppermute | solution.py:178
  64.1 13.2 %collective-permute-start.19 = (bf16[256,512]{1,0:T(8,128)(2,1)S(1)}, bf16[256,512]{1,0:T(8,128)(2,1)S(1)}, u32[]{:S(2)}, u32[]{:S(2)}) collective-permute-start(bf16[256,512]{1,0:T(8,128)(2,1)S(1)} %get-tuple-element.22), channel_id=1, source_target_pairs={{0,96},{8,104},{16,112},{24,120},{1,97},{9,105},{17,113},{25,121},... | collective-permute-start | bytes 786440 | tf_op jit(solution)/shard_map/ppermute | solution.py:193
  65.4 22.7 %collective-permute-start.26 = (bf16[2048,128]{1,0:T(8,128)(2,1)}, bf16[2048,128]{1,0:T(8,128)(2,1)}, u32[]{:S(2)}, u32[]{:S(2)}) collective-permute-start(bf16[2048,128]{1,0:T(8,128)(2,1)} %bitcast.38), channel_id=1, source_target_pairs={{0,2},{1,3},{2,4},{3,5},{4,6},{5,7},{6,0},{7,1},{8,10},{9,11},{10,... | collective-permute-start | bytes 1572872 | tf_op jit(solution)/shard_map/ppermute | solution.py:201
  66.0 18.4 %collective-permute-start.20 = (bf16[256,512]{1,0:T(8,128)(2,1)}, bf16[256,512]{1,0:T(8,128)(2,1)S(1)}, u32[]{:S(2)}, u32[]{:S(2)}) collective-permute-start(bf16[256,512]{1,0:T(8,128)(2,1)} %get-tuple-element.21), channel_id=1, source_target_pairs={{0,64},{8,72},{16,80},{24,88},{1,65},{9,73},{17,81},{25,89},{2,66}... | collective-permute-start | bytes 786440 | tf_op jit(solution)/shard_map/ppermute | solution.py:193
  71.3 13.7 %collective-permute-start.21 = (bf16[256,512]{1,0:T(8,128)(2,1)S(1)}, bf16[256,512]{1,0:T(8,128)(2,1)}, u32[]{:S(2)}, u32[]{:S(2)}) collective-permute-start(bf16[256,512]{1,0:T(8,128)(2,1)S(1)} %get-tuple-element.22), channel_id=1, source_target_pairs={{0,32},{8,40},{16,48},{24,56},{1,33},{9,41},{17,49},{25,57},{2,34}... | collective-permute-start | bytes 786440 | tf_op jit(solution)/shard_map/ppermute | solution.py:193
  74.0 25.5 %collective-permute-start.27 = (bf16[2048,128]{1,0:T(8,128)(2,1)}, bf16[2048,128]{1,0:T(8,128)(2,1)}, u32[]{:S(2)}, u32[]{:S(2)}) collective-permute-start(bf16[2048,128]{1,0:T(8,128)(2,1)} %bitcast.39), channel_id=1, source_target_pairs={{0,6},{1,7},{2,0},{3,1},{4,2},{5,3},{6,4},{7,5},{8,14},{9,15},{10,... | collective-permute-start | bytes 1572872 | tf_op jit(solution)/shard_map/ppermute | solution.py:201
  77.2 22.3 %collective-permute-start.28 = (bf16[2048,128]{1,0:T(8,128)(2,1)}, bf16[2048,128]{1,0:T(8,128)(2,1)}, u32[]{:S(2)}, u32[]{:S(2)}) collective-permute-start(bf16[2048,128]{1,0:T(8,128)(2,1)} %bitcast.40), channel_id=1, source_target_pairs={{0,4},{1,5},{2,6},{3,7},{4,0},{5,1},{6,2},{7,3},{8,12},{9,13},{10,... | collective-permute-start | bytes 1572872 | tf_op jit(solution)/shard_map/ppermute | solution.py:201
  84.4 15.7 %collective-permute-start.13 = (bf16[256,1024]{1,0:T(8,128)(2,1)}, bf16[256,1024]{1,0:T(8,128)(2,1)S(1)}, u32[]{:S(2)}, u32[]{:S(2)}) collective-permute-start(bf16[256,1024]{1,0:T(8,128)(2,1)} %get-tuple-element.11.a), channel_id=1, source_target_pairs={{0,24},{8,0},{16,8},{24,16},{32,56},{40,32},{48,40},{56,48},{64,88... | collective-permute-start | bytes 1572872 | tf_op jit(solution)/shard_map/ppermute | solution.py:221
  85.0 15.2 %collective-permute-start.14 = (bf16[256,1024]{1,0:T(8,128)(2,1)}, bf16[256,1024]{1,0:T(8,128)(2,1)S(1)}, u32[]{:S(2)}, u32[]{:S(2)}) collective-permute-start(bf16[256,1024]{1,0:T(8,128)(2,1)} %get-tuple-element.11.a), channel_id=1, source_target_pairs={{0,8},{8,16},{16,24},{24,0},{32,40},{40,48},{48,56},{56,32},{64,72... | collective-permute-start | bytes 1572872 | tf_op jit(solution)/shard_map/ppermute | solution.py:222
  88.1 11.5 %collective-permute-start.22 = (bf16[256,512]{1,0:T(8,128)(2,1)S(1)}, bf16[256,512]{1,0:T(8,128)(2,1)S(1)}, u32[]{:S(2)}, u32[]{:S(2)}) collective-permute-start(bf16[256,512]{1,0:T(8,128)(2,1)S(1)} %select_select_fusion.la), channel_id=1, source_target_pairs={{0,1},{1,0},{2,3},{3,2},{4,5},{5,4},{6,7},{7,6},{8,9},{9,8},{10,11... | collective-permute-start | bytes 786440 | tf_op jit(solution)/shard_map/ppermute | solution.py:197
  99.5 9.4 %collective-permute-start.15 = (bf16[256,1024]{1,0:T(8,128)(2,1)}, bf16[256,1024]{1,0:T(8,128)(2,1)S(1)}, u32[]{:S(2)}, u32[]{:S(2)}) collective-permute-start(bf16[256,1024]{1,0:T(8,128)(2,1)} %get-tuple-element.11.a), channel_id=1, source_target_pairs={{0,96},{8,104},{16,112},{24,120},{32,0},{40,8},{48,16},{56,24},{64... | collective-permute-start | bytes 1572872 | tf_op jit(solution)/shard_map/ppermute | solution.py:223
  99.5 20.0 %collective-permute-start.29 = (bf16[2048,128]{1,0:T(8,128)(2,1)S(1)}, bf16[2048,128]{1,0:T(8,128)(2,1)S(1)}, u32[]{:S(2)}, u32[]{:S(2)}) collective-permute-start(bf16[2048,128]{1,0:T(8,128)(2,1)S(1)} %bitcast.42), channel_id=1, source_target_pairs={{0,1},{1,0},{2,3},{3,2},{4,5},{5,4},{6,7},{7,6},{8,9},{9,8},{10,11... | collective-permute-start | bytes 1572872 | tf_op jit(solution)/shard_map/ppermute | solution.py:202
  99.6 26.8 %collective-permute-start.30 = (bf16[2048,128]{1,0:T(8,128)(2,1)}, bf16[2048,128]{1,0:T(8,128)(2,1)S(1)}, u32[]{:S(2)}, u32[]{:S(2)}) collective-permute-start(bf16[2048,128]{1,0:T(8,128)(2,1)} %collective-permute-done.26.p1), channel_id=1, source_target_pairs={{0,1},{1,0},{2,3},{3,2},{4,5},{5,4},{6,7},{7,6},{8,9},{9,8},{10,11... | collective-permute-start | bytes 1572872 | tf_op jit(solution)/shard_map/ppermute | solution.py:202
  100.1 27.8 %collective-permute-start.31 = (bf16[2048,128]{1,0:T(8,128)(2,1)}, bf16[2048,128]{1,0:T(8,128)(2,1)S(1)}, u32[]{:S(2)}, u32[]{:S(2)}) collective-permute-start(bf16[2048,128]{1,0:T(8,128)(2,1)} %collective-permute-done.27.p2), channel_id=1, source_target_pairs={{0,1},{1,0},{2,3},{3,2},{4,5},{5,4},{6,7},{7,6},{8,9},{9,8},{10,11... | collective-permute-start | bytes 1572872 | tf_op jit(solution)/shard_map/ppermute | solution.py:202
  100.2 27.7 %collective-permute-start.32 = (bf16[2048,128]{1,0:T(8,128)(2,1)}, bf16[2048,128]{1,0:T(8,128)(2,1)S(1)}, u32[]{:S(2)}, u32[]{:S(2)}) collective-permute-start(bf16[2048,128]{1,0:T(8,128)(2,1)} %collective-permute-done.28.p3), channel_id=1, source_target_pairs={{0,1},{1,0},{2,3},{3,2},{4,5},{5,4},{6,7},{7,6},{8,9},{9,8},{10,11... | collective-permute-start | bytes 1572872 | tf_op jit(solution)/shard_map/ppermute | solution.py:202
  118.6 25.7 %collective-permute-start.23 = (bf16[256,1024]{1,0:T(8,128)(2,1)}, bf16[256,1024]{1,0:T(8,128)(2,1)S(1)}, u32[]{:S(2)}, u32[]{:S(2)}) collective-permute-start(bf16[256,1024]{1,0:T(8,128)(2,1)} %get-tuple-element.14.a), channel_id=1, source_target_pairs={{0,24},{8,0},{16,8},{24,16},{32,56},{40,32},{48,40},{56,48},{64,88... | collective-permute-start | bytes 1572872 | tf_op jit(solution)/shard_map/ppermute | solution.py:221
  119.5 24.8 %collective-permute-start.24 = (bf16[256,1024]{1,0:T(8,128)(2,1)}, bf16[256,1024]{1,0:T(8,128)(2,1)S(1)}, u32[]{:S(2)}, u32[]{:S(2)}) collective-permute-start(bf16[256,1024]{1,0:T(8,128)(2,1)} %get-tuple-element.14.a), channel_id=1, source_target_pairs={{0,8},{8,16},{16,24},{24,0},{32,40},{40,48},{48,56},{56,32},{64,72... | collective-permute-start | bytes 1572872 | tf_op jit(solution)/shard_map/ppermute | solution.py:222
  126.4 18.0 %collective-permute-start.25 = (bf16[256,1024]{1,0:T(8,128)(2,1)}, bf16[256,1024]{1,0:T(8,128)(2,1)S(1)}, u32[]{:S(2)}, u32[]{:S(2)}) collective-permute-start(bf16[256,1024]{1,0:T(8,128)(2,1)} %get-tuple-element.14.a), channel_id=1, source_target_pairs={{0,96},{8,104},{16,112},{24,120},{32,0},{40,8},{48,16},{56,24},{64... | collective-permute-start | bytes 1572872 | tf_op jit(solution)/shard_map/ppermute | solution.py:223
  (24 other events, 175.8 us)

commit v2 on v1

v2 whole, which is shorter than its diff:
```python
import jax
import jax.numpy as jnp
from jax import lax
from jax.experimental import pallas as pl
from jax.experimental.pallas import tpu as pltpu
from jax.sharding import PartitionSpec as P

BF16, F32 = jnp.bfloat16, jnp.float32
N = 4
BM = 512


def x_perm(d):
    return [(r, (r // N) * N + (r % N + d) % N) for r in range(N * N)]


def y_perm(d):
    return [(r, ((r // N + d) % N) * N + r % N) for r in range(N * N)]


def z_perm(d):
    return [(p, ((p // 2 + d) % N) * 2 + p % 2) for p in range(2 * N)]


SWAP = [(p, p ^ 1) for p in range(2 * N)]


def pick(index, choices):
    out = choices[0]
    for i in range(1, len(choices)):
        out = jnp.where(index == i, choices[i], out)
    return out


def after(value, *others):
    return lax.optimization_barrier((value,) + others)[0]


def params(mib):
    return pltpu.CompilerParams(vmem_limit_bytes=mib * 1024 * 1024)


def cost(flops, moved):
    return pl.CostEstimate(flops=int(flops), bytes_accessed=int(moved), transcendentals=0)


def whole():
    return pl.BlockSpec(memory_space=pltpu.VMEM)


def place_features(at, refs, dst, rows=None):
    z, core = at[2], at[3]
    for i, ref in enumerate(refs):
        zz = lax.rem(z + (0, 3, 1, 2)[i % 4], 4)
        cc = core if i < 4 else 1 - core
        off = pl.multiple_of((zz * 2 + cc) * 128, 128)
        dst[:, pl.ds(off, 128)] = ref[...]


def pack(at, env, low, p0, p1, p2, p3):
    n = env.shape[0] // 4
    for d, out in enumerate((p0, p1, p2, p3)):
        for i, add in enumerate((d, d + 2)):
            src = pl.ds(pl.multiple_of(lax.rem(at[0] + add, 4) * n, n), n)
            out[i * n : (i + 1) * n, :] = env[src, :]
            out[(i + 2) * n : (i + 3) * n, :] = low[src, :]


def kernel_slices(at, qt, s0, s1, s2, s3, s4, s5, s6, s7, k0, k1, low, feats):
    place_features(at, (s0, s1, s2, s3, s4, s5, s6, s7), feats)
    n = k0.shape[0]
    low[...] = feats[2 * n :, :]
    scale = 1.0 / (qt.shape[0] ** 0.5)
    dots = jnp.dot(feats[: 2 * n, :], qt[...], preferred_element_type=F32) * scale
    k = dots * dots
    k0[...] = k[:n].astype(BF16)
    k1[...] = k[n:]


def place_rows(at, refs, dst):
    color = lax.rem(at[0] + 2 * at[1], 4)
    for add, ref in zip((0, 1, 3, 2), refs):
        off = pl.multiple_of(lax.rem(color + add, 4) * ref.shape[0], ref.shape[0])
        dst[pl.ds(off, ref.shape[0]), :] = ref[...]


def first_solve(at, a, b, c, d, inv, low, k1, s0, t, rhs):
    place_rows(at, (a, b, c, d), rhs)
    s0[...] = jnp.dot(inv[...], rhs[...], preferred_element_type=F32).astype(BF16)
    t[...] = (k1[...] - jnp.dot(low[...], s0[...], preferred_element_type=F32)).astype(BF16)


def kernel_rows(at, qt, p0, p1, p2, p3, p4, p5, p6, p7, out, feats):
    place_features(at, (p0, p1, p2, p3, p4, p5, p6, p7), feats)
    scale = 1.0 / (qt.shape[0] ** 0.5)
    dots = jnp.dot(feats[...], qt[...], preferred_element_type=F32) * scale
    out[...] = dots * dots


def update(s0, low, k, out):
    out[...] = k[...] - jnp.dot(low[...], s0[...], preferred_element_type=F32)


def last_step(at, a, b, c, d, inv, s0, low, res, out, rhs, s1):
    i = pl.program_id(0)
    here = at[0] + 4 * at[1]
    bm = out.shape[0]
    per_block = s1.shape[0] // bm

    @pl.when(i == 0)
    def _():
        place_rows(at, (a, b, c, d), rhs)

        s1[...] = jnp.dot(inv[...], rhs[...], preferred_element_type=F32).astype(BF16)

    rows = pl.ds(pl.multiple_of(lax.rem(i, per_block) * bm, bm), bm)
    first = i < per_block

    @pl.when(jnp.logical_and(first, here == 0))
    def _():
        out[...] = s0[rows, :]

    @pl.when(jnp.logical_and(first, here == 1))
    def _():
        out[...] = s1[rows, :]

    @pl.when(jnp.logical_not(jnp.logical_and(first, here < 2)))
    def _():
        out[...] = (res[...] - jnp.dot(low[...], s1[...], preferred_element_type=F32)).astype(BF16)


def per_device(lower_panel, sparse_desc, query_desc, diag_inv):
    blocks, width, _ = lower_panel.shape
    queries = query_desc.shape[0]
    here, part = lax.axis_index("rows"), lax.axis_index("pb")
    x, y = here % N, here // N
    z, core = part // 2, part % 2
    at = jnp.stack([x, y, z, core]).astype(jnp.int32)
    smem = pl.BlockSpec(memory_space=pltpu.SMEM)
    quarter = width // 4
    piece = sparse_desc.shape[2]
    feats = piece * 2 * N

    qt = query_desc.T
    spread = jnp.broadcast_to(qt[None], (N * N,) + qt.shape)
    qt = lax.all_to_all(spread, "rows", 0, 0, tiled=True).reshape(feats, queries)

    got = pl.pallas_call(
        pack,
        grid_spec=pltpu.PrefetchScalarGridSpec(
            num_scalar_prefetch=1,
            grid=(1,),
            in_specs=[
                pl.BlockSpec((None, width, piece), lambda i, at: (0, 0, 0)),
                pl.BlockSpec((None, width, piece), lambda i, at: (0, 0, at[2] * 2 + at[3])),
            ],
            out_specs=[pl.BlockSpec((width, piece), lambda i, at: (0, 0))] * 4,
        ),
        out_shape=[jax.ShapeDtypeStruct((width, piece), BF16)] * 4,
        compiler_params=params(16),
    )(after(at, spread), sparse_desc, lower_panel)
    got = [got[0]] + [
        lax.ppermute(got[d], "rows", [(0, d), (1, (1 + d) % N)]) for d in (1, 2, 3)
    ]
    from0 = pick(x, got)
    from1 = pick((x + 3) % N, got)
    n = quarter
    even = jnp.concatenate([from0[:n], from1[:n], from1[2 * n : 3 * n]])
    odd = jnp.concatenate([from0[n : 2 * n], from1[n : 2 * n], from1[3 * n :]])
    got_y = [even] + [
        lax.ppermute(even if d == 2 else odd, "rows", [(c, d * N + c) for c in range(N)])
        for d in (1, 2, 3)
    ]
    mine = pick(y, got_y)
    slices = [mine] + [lax.ppermute(mine, "pb", z_perm(d)) for d in (1, -1, 2)]
    slices = slices + [lax.ppermute(v, "pb", SWAP) for v in slices]

    own = sparse_desc.reshape(blocks * width, piece)
    envs = [own] + [lax.ppermute(own, "pb", z_perm(d)) for d in (1, -1)]
    envs = envs + [lax.ppermute(after(own, envs[1]), "pb", z_perm(2))]
    envs = envs + [lax.ppermute(v, "pb", SWAP) for v in envs]

    unit = 2 * width * feats * queries
    k0, k1, low = pl.pallas_call(
        kernel_slices,
        out_shape=(
            jax.ShapeDtypeStruct((quarter, queries), BF16),
            jax.ShapeDtypeStruct((quarter, queries), F32),
            jax.ShapeDtypeStruct((quarter, width), BF16),
        ),
        in_specs=[smem] + [whole()] * 9,
        out_specs=(whole(),) * 3,
        scratch_shapes=[pltpu.VMEM((3 * quarter, feats), BF16)],
        compiler_params=params(16),
        cost_estimate=cost(unit / 2, 5e6),
    )(at, qt, *slices)

    def neighbours(v):
        return (
            v,
            lax.ppermute(v, "rows", x_perm(-1)),
            lax.ppermute(v, "rows", x_perm(1)),
            lax.ppermute(v, "rows", y_perm(-1)),
        )

    block = pl.BlockSpec((None, width, width), lambda *_: (0, 0, 0), memory_space=pltpu.VMEM)
    s0, t = pl.pallas_call(
        first_solve,
        grid=(1,),
        out_shape=(
            jax.ShapeDtypeStruct((width, queries), BF16),
            jax.ShapeDtypeStruct((quarter, queries), BF16),
        ),
        in_specs=[smem] + [whole()] * 4 + [block] + [whole()] * 2,
        out_specs=(whole(), whole()),
        scratch_shapes=[pltpu.VMEM((width, queries), BF16)],
        compiler_params=params(20),
        cost_estimate=cost(unit * 1.25, 8e6),
    )(at, *neighbours(k0), diag_inv, low, k1)

    bm = BM
    rows = blocks * width
    panel = lower_panel.reshape(rows, 2 * width)
    k_rows = pl.pallas_call(
        kernel_rows,
        grid=(rows // bm,),
        out_shape=jax.ShapeDtypeStruct((rows, queries), F32),
        in_specs=[smem, whole()] + [pl.BlockSpec((bm, piece), lambda i: (i, 0))] * 8,
        out_specs=pl.BlockSpec((bm, queries), lambda i: (i, 0)),
        scratch_shapes=[pltpu.VMEM((bm, feats), BF16)],
        compiler_params=params(16),
        cost_estimate=cost(unit * 2, 14e6),
    )(at, qt, *envs)
    res = pl.pallas_call(
        update,
        grid=(rows // bm,),
        out_shape=jax.ShapeDtypeStruct((rows, queries), F32),
        in_specs=[
            whole(),
            pl.BlockSpec((bm, width), lambda i: (i, 0)),
            pl.BlockSpec((bm, queries), lambda i: (i, 0)),
        ],
        out_specs=pl.BlockSpec((bm, queries), lambda i: (i, 0)),
        compiler_params=params(16),
        cost_estimate=cost(unit * 2, 22e6),
    )(s0, panel, k_rows)

    block1 = pl.BlockSpec((None, width, width), lambda *_: (1, 0, 0), memory_space=pltpu.VMEM)
    out = pl.pallas_call(
        last_step,
        grid=(rows // bm,),
        out_shape=jax.ShapeDtypeStruct((rows, queries), BF16),
        in_specs=[smem]
        + [whole()] * 4
        + [
            block1,
            whole(),
            pl.BlockSpec((bm, width), lambda i: (i, 1)),
            pl.BlockSpec((bm, queries), lambda i: (i, 0)),
        ],
        out_specs=pl.BlockSpec((bm, queries), lambda i: (i, 0)),
        scratch_shapes=[pltpu.VMEM((width, queries), BF16), pltpu.VMEM((width, queries), BF16)],
        compiler_params=params(20),
        cost_estimate=cost(unit * 3, 20e6),
    )(at, *neighbours(t), diag_inv, s0, panel, res)
    return out.reshape(blocks, width, queries)


def solution(mesh):
    return jax.shard_map(
        per_device,
        mesh=mesh,
        in_specs=(P(None, "rows", None), P(None, "rows", "pb"), P("pb", "rows"), P()),
        out_specs=P(None, "rows", "pb"),
        check_vma=False,
    )
```

time: 164 us -> 147 us (0.90)
  starting transfers between devices: 58.9 us -> 36.4 us
  waiting for transfers between devices: 36.7 us -> 57.2 us
  Pallas kernels: 45.6 us -> 29.5 us
  local copies, waits for them, and re-layouts: 16.4 us -> 20 us
    ppermute x13 -> x6, waiting for transfers between devices: 11.3 us -> 30.8 us  [the longest x3 30.8 us: per_device(): lax.ppermute(got[d], 'rows', [(0, d), (1, (1 + d) % N)])]
    ppermute x2, waiting for transfers between devices: 0.01 us -> 11.5 us  [neighbours(): lax.ppermute(v, 'rows', x_perm(-1))]
    unnamed x44 -> x42, local copies, waits for them, and re-layouts: 6.02 us -> 17.5 us
    ppermute x13 -> x6, starting transfers between devices: 19.5 us -> 8.12 us  [the longest x3 3.93 us: per_device(): lax.ppermute(got[d], 'rows', [(0, d), (1, (1 + d) % N)])]
    ppermute x3, waiting for transfers between devices: 9.6 us -> 0.58 us  [per_device(): lax.ppermute(even if d == 2 else odd, 'rows', [(c, d * N + c) for c in ra...]
    ppermute x2, waiting for transfers between devices: 8.26 us -> 0.95 us  [neighbours(): lax.ppermute(v, 'rows', y_perm(-1))]
    pallas_call x1, Pallas kernels: 16 us -> 9.49 us  [per_device(): pl.pallas_call(last_step, grid=(rows // bm,), out_shape=jax.ShapeDtypeStr...]
    slice x4 -> x1, local copies, waits for them, and re-layouts: 6.51 us -> 0.03 us  [per_device(): even = jnp.concatenate([from0[:n], from1[:n], from1[2 * n:3 * n]])]
  transfers between devices with their start and end apart: 34 -> 27, of which waited for: 5 -> 7; matrix products, arithmetic and copies ran while one was open for 8% -> 2% of each run, Pallas kernels for 18% -> 14%
where the time goes in v2:
time: 147 us; the launch traced here: 146 us
  waiting for transfers between devices  57.2 us (39%)
  starting transfers between devices  36.4 us (25%)
  Pallas kernels  29.5 us (20%)
  local copies, waits for them, and re-layouts  20 us (14%)
  other arithmetic  2.78 us (2%)
    ppermute x3, waiting for transfers between devices, per_device(): lax.ppermute(got[d], 'rows', [(0, d), (1, (1 + d) % N)])  30.8 us
    unnamed x42, local copies, waits for them, and re-layouts  17.5 us
    ppermute x3, waiting for transfers between devices, per_device(): slices = [mine] + [lax.ppermute(mine, 'pb', z_perm(d)) for d in (1, -1, 2)]  13.3 us
    ppermute x2, waiting for transfers between devices, neighbours(): lax.ppermute(v, 'rows', x_perm(-1))  11.5 us
    pallas_call x1, Pallas kernels, per_device(): pl.pallas_call(last_step, grid=(rows // bm,), out_shape=jax.ShapeDtypeStr...  9.49 us
    all_to_all x1, starting transfers between devices, per_device(): lax.all_to_all(spread, 'rows', 0, 0, tiled=True).reshape(feats, queries)  7.42 us
    pallas_call x1, Pallas kernels, per_device(): pl.pallas_call(kernel_rows, grid=(rows // bm,), out_shape=jax.ShapeDtypeS...  7.32 us
    ppermute x3, starting transfers between devices, per_device(): slices = [mine] + [lax.ppermute(mine, 'pb', z_perm(d)) for d in (1, -1, 2)]  5.97 us
  transfers between devices with their start and end apart: 27, of which 7 were waited for; matrix products, arithmetic and copies ran while one was open for 2% of the time, Pallas kernels for 14%

profile of v2, /device:TPU:6, one launch (start us, length us, event | category | flops | bytes accessed | tf_op | source)
XLA Modules:
  0.0 146.1 jit_solution(5061749540544915550)
XLA Ops:
  0.0 2.5 %broadcast_in_dim.2 = bf16[16,64,1024]{2,1,0:T(8,128)(2,1)} broadcast(bf16[64,1024]{1,0:T(8,128)(2,1)} %bitcast.20), dimensions={1,2} | broadcast | bytes 2228224 | tf_op jit(solution)/shard_map/broadcast_in_dim | solution.py:145
  2.5 7.4 %all-to-all-start = ((bf16[16,64,1024]{2,1,0:T(8,128)(2,1)}), bf16[16,64,1024]{2,1,0:T(8,128)(2,1)S(1)}, u32[]{:S(2)}, u32[]{:S(2)}) async-start(bf16[16,64,1024]{2,1,0:T(8,128)(2,1)} %broadcast_in_dim.2), calls=%async_computation | async-start | bytes 4194304 | tf_op jit(solution)/shard_map/all_to_all | solution.py:146
  10.0 3.4 %copy-done = bf16[2,1024,2048]{2,1,0:T(8,128)(2,1)S(1)} copy-done((bf16[2,1024,2048]{2,1,0:T(8,128)(2,1)S(1)}, bf16[2,1024,2048]{2,1,0:T(8,128)(2,1)}, u32[]{:S(2)}) %copy-start) | copy-done | bytes 8388632
  13.4 1.4 shard_map.46
  14.8 1.3 collective-permute-start
  16.1 1.3 collective-permute-start.1
  17.4 1.4 collective-permute-start.2
  18.8 20.4 %collective-permute-done = bf16[1024,128]{1,0:T(8,128)(2,1)} collective-permute-done((bf16[1024,128]{1,0:T(8,128)(2,1)}, bf16[1024,128]{1,0:T(8,128)(2,1)}, u32[]{:S(2)}, u32[]{:S(2)}) %collective-permute-start) | collective-permute-done | bytes 262176 | tf_op jit(solution)/shard_map/ppermute | solution.py:163
  39.2 10.4 %collective-permute-done.1 = bf16[1024,128]{1,0:T(8,128)(2,1)} collective-permute-done((bf16[1024,128]{1,0:T(8,128)(2,1)S(1)}, bf16[1024,128]{1,0:T(8,128)(2,1)}, u32[]{:S(2)}, u32[]{:S(2)}) %collective-permute-start.1) | collective-permute-done | bytes 262176 | tf_op jit(solution)/shard_map/ppermute | solution.py:163
  49.6 1.2 select_select_fusion.1
  51.5 2.0 %collective-permute-start.4 = (bf16[768,128]{1,0:T(8,128)(2,1)}, bf16[768,128]{1,0:T(8,128)(2,1)}, u32[]{:S(2)}, u32[]{:S(2)}) collective-permute-start(bf16[768,128]{1,0:T(8,128)(2,1)} %pad_maximum_fusion.1), channel_id=1, source_target_pairs={{0,64},{8,72},{16,80},{24,88},{1,65},{9,73},{17,81},{25,89},{2,66}... | collective-permute-start | bytes 589832 | tf_op jit(solution)/shard_map/ppermute | solution.py:171
  54.2 1.3 collective-permute-start.3
  55.5 2.0 %collective-permute-start.5 = (bf16[768,128]{1,0:T(8,128)(2,1)}, bf16[768,128]{1,0:T(8,128)(2,1)}, u32[]{:S(2)}, u32[]{:S(2)}) collective-permute-start(bf16[768,128]{1,0:T(8,128)(2,1)} %pad_maximum_fusion), channel_id=1, source_target_pairs={{0,32},{8,40},{16,48},{24,56},{1,33},{9,41},{17,49},{25,57},{2,34}... | collective-permute-start | bytes 589832 | tf_op jit(solution)/shard_map/ppermute | solution.py:171
  57.4 1.9 %collective-permute-start.19 = (bf16[2048,128]{1,0:T(8,128)(2,1)S(1)}, bf16[2048,128]{1,0:T(8,128)(2,1)S(1)}, u32[]{:S(2)}, u32[]{:S(2)}) collective-permute-start(bf16[2048,128]{1,0:T(8,128)(2,1)S(1)} %bitcast.15), channel_id=1, source_target_pairs={{0,2},{1,3},{2,4},{3,5},{4,6},{5,7},{6,0},{7,1},{8,10},{9,11},{10,... | collective-permute-start | bytes 1572872 | tf_op jit(solution)/shard_map/ppermute | solution.py:179
  60.7 2.0 %collective-permute-start.6 = (bf16[768,128]{1,0:T(8,128)(2,1)S(1)}, bf16[768,128]{1,0:T(8,128)(2,1)S(1)}, u32[]{:S(2)}, u32[]{:S(2)}) collective-permute-start(bf16[768,128]{1,0:T(8,128)(2,1)S(1)} %select_select_fusion.2.s0), channel_id=1, source_target_pairs={{0,2},{1,3},{2,4},{3,5},{4,6},{5,7},{6,0},{7,1},{8,10},{9,11},{10,... | collective-permute-start | bytes 589832 | tf_op jit(solution)/shard_map/ppermute | solution.py:175
  62.7 2.2 %collective-permute-start.7 = (bf16[768,128]{1,0:T(8,128)(2,1)S(1)}, bf16[768,128]{1,0:T(8,128)(2,1)S(1)}, u32[]{:S(2)}, u32[]{:S(2)}) collective-permute-start(bf16[768,128]{1,0:T(8,128)(2,1)S(1)} %select_select_fusion.2.s0), channel_id=1, source_target_pairs={{0,6},{1,7},{2,0},{3,1},{4,2},{5,3},{6,4},{7,5},{8,14},{9,15},{10,... | collective-permute-start | bytes 589832 | tf_op jit(solution)/shard_map/ppermute | solution.py:175
  64.9 1.8 %collective-permute-start.8 = (bf16[768,128]{1,0:T(8,128)(2,1)S(1)}, bf16[768,128]{1,0:T(8,128)(2,1)S(1)}, u32[]{:S(2)}, u32[]{:S(2)}) collective-permute-start(bf16[768,128]{1,0:T(8,128)(2,1)S(1)} %select_select_fusion.2.s0), channel_id=1, source_target_pairs={{0,4},{1,5},{2,6},{3,7},{4,0},{5,1},{6,2},{7,3},{8,12},{9,13},{10,... | collective-permute-start | bytes 589832 | tf_op jit(solution)/shard_map/ppermute | solution.py:175
  66.7 10.9 %collective-permute-done.6.s1 = bf16[768,128]{1,0:T(8,128)(2,1)S(1)} collective-permute-done((bf16[768,128]{1,0:T(8,128)(2,1)S(1)}, bf16[768,128]{1,0:T(8,128)(2,1)S(1)}, u32[]{:S(2)}, u32[]{:S(2)}) %collective-permute-start.6) | collective-permute-done | bytes 196640 | tf_op jit(solution)/shard_map/ppermute | solution.py:175
  79.5 2.4 %collective-permute-done.8.s3 = bf16[768,128]{1,0:T(8,128)(2,1)S(1)} collective-permute-done((bf16[768,128]{1,0:T(8,128)(2,1)S(1)}, bf16[768,128]{1,0:T(8,128)(2,1)S(1)}, u32[]{:S(2)}, u32[]{:S(2)}) %collective-permute-start.8) | collective-permute-done | bytes 196640 | tf_op jit(solution)/shard_map/ppermute | solution.py:175
  83.5 1.9 %collective-permute-start.21 = (bf16[2048,128]{1,0:T(8,128)(2,1)S(1)}, bf16[2048,128]{1,0:T(8,128)(2,1)}, u32[]{:S(2)}, u32[]{:S(2)}) collective-permute-start(bf16[2048,128]{1,0:T(8,128)(2,1)S(1)} %bitcast.17), channel_id=1, source_target_pairs={{0,4},{1,5},{2,6},{3,7},{4,0},{5,1},{6,2},{7,3},{8,12},{9,13},{10,... | collective-permute-start | bytes 1572872 | tf_op jit(solution)/shard_map/ppermute | solution.py:180
  94.0 2.3 %shard_map.47 = (bf16[256,1024]{1,0:T(8,128)(2,1)S(1)}, f32[256,1024]{1,0:T(8,128)S(1)}, bf16[256,1024]{1,0:T(8,128)(2,1)S(1)}) custom-call(s32[4]{0:T(128)S(1)} %pad_add_fusion.at, bf16[1024,1024]{1,0:T(8,128)(2,1)S(1)} %bitcast.13, bf16[768,128]{1,0:T(8,128)(2,1)S(1)} %select_select_fusion.2.s0, bf16[768,128]{1,0:T(8,128)(2,1)S(1)} %copy-done.5, ...), custom_call_target="tpu_custom_call" | custom-call | flops 1073741824 | bytes 5000000 | tf_op jit(solution)/shard_map/pallas_call | solution.py:184
  96.4 1.4 collective-permute-start.13
  97.8 1.9 %collective-permute-start.14 = (bf16[256,1024]{1,0:T(8,128)(2,1)S(1)}, bf16[256,1024]{1,0:T(8,128)(2,1)S(1)}, u32[]{:S(2)}, u32[]{:S(2)}) collective-permute-start(bf16[256,1024]{1,0:T(8,128)(2,1)S(1)} %get-tuple-element.21.a), channel_id=1, source_target_pairs={{0,8},{8,16},{16,24},{24,0},{32,40},{40,48},{48,56},{56,32},{64,72... | collective-permute-start | bytes 1572872 | tf_op jit(solution)/shard_map/ppermute | solution.py:202
  100.2 11.5 %collective-permute-done.13.b = bf16[256,1024]{1,0:T(8,128)(2,1)S(1)} collective-permute-done((bf16[256,1024]{1,0:T(8,128)(2,1)S(1)}, bf16[256,1024]{1,0:T(8,128)(2,1)S(1)}, u32[]{:S(2)}, u32[]{:S(2)}) %collective-permute-start.13) | collective-permute-done | bytes 524320 | tf_op jit(solution)/shard_map/ppermute | solution.py:201
  112.2 1.0 collective-permute-done.15.d
  113.2 2.2 %copy-done.1 = bf16[2,1024,1024]{2,1,0:T(8,128)(2,1)S(1)} copy-done((bf16[2,1024,1024]{2,1,0:T(8,128)(2,1)S(1)}, bf16[2,1024,1024]{2,1,0:T(8,128)(2,1)}, u32[]{:S(2)}) %copy-start.1) | copy-done | bytes 4194328
  115.4 3.6 %shard_map.48 = (bf16[1024,1024]{1,0:T(8,128)(2,1)S(1)}, bf16[256,1024]{1,0:T(8,128)(2,1)S(1)}) custom-call(s32[4]{0:T(128)S(1)} %pad_add_fusion.at, bf16[256,1024]{1,0:T(8,128)(2,1)S(1)} %get-tuple-element.21.a, bf16[256,1024]{1,0:T(8,128)(2,1)S(1)} %collective-permute-done.13.b, bf16[256,1024]{1,0:T(8,128)(2,1)S(1)} %collective-permute-done.14.c, ...), custom_call_target="tpu_custom_call" | custom-call | flops 2684354560 | bytes 8000000 | tf_op jit(solution)/shard_map/pallas_call | solution.py:207
  119.2 3.1 %collective-permute-start.17 = (bf16[256,1024]{1,0:T(8,128)(2,1)S(1)}, bf16[256,1024]{1,0:T(8,128)(2,1)S(1)}, u32[]{:S(2)}, u32[]{:S(2)}) collective-permute-start(bf16[256,1024]{1,0:T(8,128)(2,1)S(1)} %get-tuple-element.24.a), channel_id=1, source_target_pairs={{0,8},{8,16},{16,24},{24,0},{32,40},{40,48},{48,56},{56,32},{64,72... | collective-permute-start | bytes 1572872 | tf_op jit(solution)/shard_map/ppermute | solution.py:202
  122.3 1.5 %collective-permute-start.18 = (bf16[256,1024]{1,0:T(8,128)(2,1)S(1)}, bf16[256,1024]{1,0:T(8,128)(2,1)S(1)}, u32[]{:S(2)}, u32[]{:S(2)}) collective-permute-start(bf16[256,1024]{1,0:T(8,128)(2,1)S(1)} %get-tuple-element.24.a), channel_id=1, source_target_pairs={{0,96},{8,104},{16,112},{24,120},{32,0},{40,8},{48,16},{56,24},{64... | collective-permute-start | bytes 1572872 | tf_op jit(solution)/shard_map/ppermute | solution.py:203
  123.8 7.3 %shard_map.49.k = f32[2048,1024]{1,0:T(8,128)S(1)} custom-call(s32[4]{0:T(128)S(1)} %pad_add_fusion.at, bf16[1024,1024]{1,0:T(8,128)(2,1)S(1)} %bitcast.14, bf16[2048,128]{1,0:T(8,128)(2,1)S(1)} %bitcast.19, bf16[2048,128]{1,0:T(8,128)(2,1)S(1)} %collective-permute-done.19.p1, bf16[2048,128]{1,0:T(8,128)(2,1)} %collective-permute-done.20.p2, ...), custom_call_target="tpu_custom_call" | custom-call | flops 4294967296 | bytes 14000000 | tf_op jit(solution)/shard_map/pallas_call | solution.py:224
  131.1 5.4 %shard_map.50.res = f32[2048,1024]{1,0:T(8,128)S(1)} custom-call(bf16[1024,1024]{1,0:T(8,128)(2,1)S(1)} %get-tuple-element.25.s0, bf16[2048,2048]{1,0:T(8,128)(2,1)S(1)} %bitcast.11, f32[2048,1024]{1,0:T(8,128)S(1)} %shard_map.49.k), custom_call_target="tpu_custom_call" | custom-call | flops 4294967296 | bytes 22000000 | tf_op jit(solution)/shard_map/pallas_call | solution.py:234
  136.6 9.5 %shard_map.51 = bf16[2048,1024]{1,0:T(8,128)(2,1)} custom-call(s32[4]{0:T(128)S(1)} %pad_add_fusion.at, bf16[256,1024]{1,0:T(8,128)(2,1)S(1)} %get-tuple-element.24.a, bf16[256,1024]{1,0:T(8,128)(2,1)S(1)} %collective-permute-done.16.b, bf16[256,1024]{1,0:T(8,128)(2,1)S(1)} %collective-permute-done.17.c, bf16[256,1024]{1,0:T(8,128)(2,1)S(1)} %collective-permute-done.18.d, ...), custom_call_target="tpu_custom_call" | custom-call | flops 6442450944 | bytes 20000000 | tf_op jit(solution)/shard_map/pallas_call | solution.py:249
  (78 shorter events, 16.2 us)
Async XLA Ops:
  0.0 10.0 %copy-start.3 = (bf16[2,1024,128]{2,1,0:T(8,128)(2,1)S(1)}, bf16[2,1024,128]{2,1,0:T(8,128)(2,1)}, u32[]{:S(2)}) copy-start(bf16[2,1024,128]{2,1,0:T(8,128)(2,1)} %env.1) | copy-start | bytes 1572868
  2.5 85.0 %all-to-all-start = ((bf16[16,64,1024]{2,1,0:T(8,128)(2,1)}), bf16[16,64,1024]{2,1,0:T(8,128)(2,1)S(1)}, u32[]{:S(2)}, u32[]{:S(2)}) async-start(bf16[16,64,1024]{2,1,0:T(8,128)(2,1)} %broadcast_in_dim.2), calls=%async_computation | async-start | bytes 4194304 | tf_op jit(solution)/shard_map/all_to_all | solution.py:146
  10.0 3.4 %copy-start = (bf16[2,1024,2048]{2,1,0:T(8,128)(2,1)S(1)}, bf16[2,1024,2048]{2,1,0:T(8,128)(2,1)}, u32[]{:S(2)}) copy-start(bf16[2,1024,2048]{2,1,0:T(8,128)(2,1)} %low.1) | copy-start | bytes 25165828
  14.8 24.4 %collective-permute-start = (bf16[1024,128]{1,0:T(8,128)(2,1)}, bf16[1024,128]{1,0:T(8,128)(2,1)}, u32[]{:S(2)}, u32[]{:S(2)}) collective-permute-start(bf16[1024,128]{1,0:T(8,128)(2,1)} %get-tuple-element.17), channel_id=1, source_target_pairs={{0,24},{8,0},{1,25},{9,1},{2,26},{10,2},{3,27},{11,3},{4,28},{12,4... | collective-permute-start | bytes 786440 | tf_op jit(solution)/shard_map/ppermute | solution.py:163
  16.1 33.5 %collective-permute-start.1 = (bf16[1024,128]{1,0:T(8,128)(2,1)S(1)}, bf16[1024,128]{1,0:T(8,128)(2,1)}, u32[]{:S(2)}, u32[]{:S(2)}) collective-permute-start(bf16[1024,128]{1,0:T(8,128)(2,1)S(1)} %get-tuple-element.18), channel_id=1, source_target_pairs={{0,16},{8,24},{1,17},{9,25},{2,18},{10,26},{3,19},{11,27},{4,20},{... | collective-permute-start | bytes 786440 | tf_op jit(solution)/shard_map/ppermute | solution.py:163
  17.4 32.2 %collective-permute-start.2 = (bf16[1024,128]{1,0:T(8,128)(2,1)S(1)}, bf16[1024,128]{1,0:T(8,128)(2,1)}, u32[]{:S(2)}, u32[]{:S(2)}) collective-permute-start(bf16[1024,128]{1,0:T(8,128)(2,1)S(1)} %get-tuple-element.19), channel_id=1, source_target_pairs={{0,8},{8,16},{1,9},{9,17},{2,10},{10,18},{3,11},{11,19},{4,12},{12... | collective-permute-start | bytes 786440 | tf_op jit(solution)/shard_map/ppermute | solution.py:163
  51.5 7.9 %collective-permute-start.4 = (bf16[768,128]{1,0:T(8,128)(2,1)}, bf16[768,128]{1,0:T(8,128)(2,1)}, u32[]{:S(2)}, u32[]{:S(2)}) collective-permute-start(bf16[768,128]{1,0:T(8,128)(2,1)} %pad_maximum_fusion.1), channel_id=1, source_target_pairs={{0,64},{8,72},{16,80},{24,88},{1,65},{9,73},{17,81},{25,89},{2,66}... | collective-permute-start | bytes 589832 | tf_op jit(solution)/shard_map/ppermute | solution.py:171
  54.2 5.2 %collective-permute-start.3 = (bf16[768,128]{1,0:T(8,128)(2,1)}, bf16[768,128]{1,0:T(8,128)(2,1)S(1)}, u32[]{:S(2)}, u32[]{:S(2)}) collective-permute-start(bf16[768,128]{1,0:T(8,128)(2,1)} %pad_maximum_fusion), channel_id=1, source_target_pairs={{0,96},{8,104},{16,112},{24,120},{1,97},{9,105},{17,113},{25,121},... | collective-permute-start | bytes 589832 | tf_op jit(solution)/shard_map/ppermute | solution.py:171
  55.5 5.1 %collective-permute-start.5 = (bf16[768,128]{1,0:T(8,128)(2,1)}, bf16[768,128]{1,0:T(8,128)(2,1)}, u32[]{:S(2)}, u32[]{:S(2)}) collective-permute-start(bf16[768,128]{1,0:T(8,128)(2,1)} %pad_maximum_fusion), channel_id=1, source_target_pairs={{0,32},{8,40},{16,48},{24,56},{1,33},{9,41},{17,49},{25,57},{2,34}... | collective-permute-start | bytes 589832 | tf_op jit(solution)/shard_map/ppermute | solution.py:171
  57.4 25.1 %collective-permute-start.19 = (bf16[2048,128]{1,0:T(8,128)(2,1)S(1)}, bf16[2048,128]{1,0:T(8,128)(2,1)S(1)}, u32[]{:S(2)}, u32[]{:S(2)}) collective-permute-start(bf16[2048,128]{1,0:T(8,128)(2,1)S(1)} %bitcast.15), channel_id=1, source_target_pairs={{0,2},{1,3},{2,4},{3,5},{4,6},{5,7},{6,0},{7,1},{8,10},{9,11},{10,... | collective-permute-start | bytes 1572872 | tf_op jit(solution)/shard_map/ppermute | solution.py:179
  60.7 16.9 %collective-permute-start.6 = (bf16[768,128]{1,0:T(8,128)(2,1)S(1)}, bf16[768,128]{1,0:T(8,128)(2,1)S(1)}, u32[]{:S(2)}, u32[]{:S(2)}) collective-permute-start(bf16[768,128]{1,0:T(8,128)(2,1)S(1)} %select_select_fusion.2.s0), channel_id=1, source_target_pairs={{0,2},{1,3},{2,4},{3,5},{4,6},{5,7},{6,0},{7,1},{8,10},{9,11},{10,... | collective-permute-start | bytes 589832 | tf_op jit(solution)/shard_map/ppermute | solution.py:175
  62.7 15.6 %collective-permute-start.7 = (bf16[768,128]{1,0:T(8,128)(2,1)S(1)}, bf16[768,128]{1,0:T(8,128)(2,1)S(1)}, u32[]{:S(2)}, u32[]{:S(2)}) collective-permute-start(bf16[768,128]{1,0:T(8,128)(2,1)S(1)} %select_select_fusion.2.s0), channel_id=1, source_target_pairs={{0,6},{1,7},{2,0},{3,1},{4,2},{5,3},{6,4},{7,5},{8,14},{9,15},{10,... | collective-permute-start | bytes 589832 | tf_op jit(solution)/shard_map/ppermute | solution.py:175
  64.9 16.9 %collective-permute-start.8 = (bf16[768,128]{1,0:T(8,128)(2,1)S(1)}, bf16[768,128]{1,0:T(8,128)(2,1)S(1)}, u32[]{:S(2)}, u32[]{:S(2)}) collective-permute-start(bf16[768,128]{1,0:T(8,128)(2,1)S(1)} %select_select_fusion.2.s0), channel_id=1, source_target_pairs={{0,4},{1,5},{2,6},{3,7},{4,0},{5,1},{6,2},{7,3},{8,12},{9,13},{10,... | collective-permute-start | bytes 589832 | tf_op jit(solution)/shard_map/ppermute | solution.py:175
  66.7 16.1 %collective-permute-start.9 = (bf16[768,128]{1,0:T(8,128)(2,1)S(1)}, bf16[768,128]{1,0:T(8,128)(2,1)S(1)}, u32[]{:S(2)}, u32[]{:S(2)}) collective-permute-start(bf16[768,128]{1,0:T(8,128)(2,1)S(1)} %select_select_fusion.2.s0), channel_id=1, source_target_pairs={{0,1},{1,0},{2,3},{3,2},{4,5},{5,4},{6,7},{7,6},{8,9},{9,8},{10,11... | collective-permute-start | bytes 589832 | tf_op jit(solution)/shard_map/ppermute | solution.py:176
  77.6 7.9 %collective-permute-start.10 = (bf16[768,128]{1,0:T(8,128)(2,1)S(1)}, bf16[768,128]{1,0:T(8,128)(2,1)S(1)}, u32[]{:S(2)}, u32[]{:S(2)}) collective-permute-start(bf16[768,128]{1,0:T(8,128)(2,1)S(1)} %collective-permute-done.6.s1), channel_id=1, source_target_pairs={{0,1},{1,0},{2,3},{3,2},{4,5},{5,4},{6,7},{7,6},{8,9},{9,8},{10,11... | collective-permute-start | bytes 589832 | tf_op jit(solution)/shard_map/ppermute | solution.py:176
  78.3 7.9 %collective-permute-start.11 = (bf16[768,128]{1,0:T(8,128)(2,1)S(1)}, bf16[768,128]{1,0:T(8,128)(2,1)S(1)}, u32[]{:S(2)}, u32[]{:S(2)}) collective-permute-start(bf16[768,128]{1,0:T(8,128)(2,1)S(1)} %collective-permute-done.7.s2), channel_id=1, source_target_pairs={{0,1},{1,0},{2,3},{3,2},{4,5},{5,4},{6,7},{7,6},{8,9},{9,8},{10,11... | collective-permute-start | bytes 589832 | tf_op jit(solution)/shard_map/ppermute | solution.py:176
  81.9 5.0 %collective-permute-start.12 = (bf16[768,128]{1,0:T(8,128)(2,1)S(1)}, bf16[768,128]{1,0:T(8,128)(2,1)S(1)}, u32[]{:S(2)}, u32[]{:S(2)}) collective-permute-start(bf16[768,128]{1,0:T(8,128)(2,1)S(1)} %collective-permute-done.8.s3), channel_id=1, source_target_pairs={{0,1},{1,0},{2,3},{3,2},{4,5},{5,4},{6,7},{7,6},{8,9},{9,8},{10,11... | collective-permute-start | bytes 589832 | tf_op jit(solution)/shard_map/ppermute | solution.py:176
  82.5 17.2 %collective-permute-start.20 = (bf16[2048,128]{1,0:T(8,128)(2,1)S(1)}, bf16[2048,128]{1,0:T(8,128)(2,1)}, u32[]{:S(2)}, u32[]{:S(2)}) collective-permute-start(bf16[2048,128]{1,0:T(8,128)(2,1)S(1)} %bitcast.16), channel_id=1, source_target_pairs={{0,6},{1,7},{2,0},{3,1},{4,2},{5,3},{6,4},{7,5},{8,14},{9,15},{10,... | collective-permute-start | bytes 1572872 | tf_op jit(solution)/shard_map/ppermute | solution.py:179
  83.5 16.2 %collective-permute-start.21 = (bf16[2048,128]{1,0:T(8,128)(2,1)S(1)}, bf16[2048,128]{1,0:T(8,128)(2,1)}, u32[]{:S(2)}, u32[]{:S(2)}) collective-permute-start(bf16[2048,128]{1,0:T(8,128)(2,1)S(1)} %bitcast.17), channel_id=1, source_target_pairs={{0,4},{1,5},{2,6},{3,7},{4,0},{5,1},{6,2},{7,3},{8,12},{9,13},{10,... | collective-permute-start | bytes 1572872 | tf_op jit(solution)/shard_map/ppermute | solution.py:180
  96.4 15.3 %collective-permute-start.13 = (bf16[256,1024]{1,0:T(8,128)(2,1)S(1)}, bf16[256,1024]{1,0:T(8,128)(2,1)S(1)}, u32[]{:S(2)}, u32[]{:S(2)}) collective-permute-start(bf16[256,1024]{1,0:T(8,128)(2,1)S(1)} %get-tuple-element.21.a), channel_id=1, source_target_pairs={{0,24},{8,0},{16,8},{24,16},{32,56},{40,32},{48,40},{56,48},{64,88... | collective-permute-start | bytes 1572872 | tf_op jit(solution)/shard_map/ppermute | solution.py:201
  97.8 13.9 %collective-permute-start.14 = (bf16[256,1024]{1,0:T(8,128)(2,1)S(1)}, bf16[256,1024]{1,0:T(8,128)(2,1)S(1)}, u32[]{:S(2)}, u32[]{:S(2)}) collective-permute-start(bf16[256,1024]{1,0:T(8,128)(2,1)S(1)} %get-tuple-element.21.a), channel_id=1, source_target_pairs={{0,8},{8,16},{16,24},{24,0},{32,40},{40,48},{48,56},{56,32},{64,72... | collective-permute-start | bytes 1572872 | tf_op jit(solution)/shard_map/ppermute | solution.py:202
  99.7 13.5 %collective-permute-start.15 = (bf16[256,1024]{1,0:T(8,128)(2,1)S(1)}, bf16[256,1024]{1,0:T(8,128)(2,1)S(1)}, u32[]{:S(2)}, u32[]{:S(2)}) collective-permute-start(bf16[256,1024]{1,0:T(8,128)(2,1)S(1)} %get-tuple-element.21.a), channel_id=1, source_target_pairs={{0,96},{8,104},{16,112},{24,120},{32,0},{40,8},{48,16},{56,24},{64... | collective-permute-start | bytes 1572872 | tf_op jit(solution)/shard_map/ppermute | solution.py:203
  99.7 19.5 %collective-permute-start.22 = (bf16[2048,128]{1,0:T(8,128)(2,1)S(1)}, bf16[2048,128]{1,0:T(8,128)(2,1)S(1)}, u32[]{:S(2)}, u32[]{:S(2)}) collective-permute-start(bf16[2048,128]{1,0:T(8,128)(2,1)S(1)} %bitcast.18), channel_id=1, source_target_pairs={{0,1},{1,0},{2,3},{3,2},{4,5},{5,4},{6,7},{7,6},{8,9},{9,8},{10,11... | collective-permute-start | bytes 1572872 | tf_op jit(solution)/shard_map/ppermute | solution.py:181
  99.7 22.6 %collective-permute-start.23 = (bf16[2048,128]{1,0:T(8,128)(2,1)S(1)}, bf16[2048,128]{1,0:T(8,128)(2,1)S(1)}, u32[]{:S(2)}, u32[]{:S(2)}) collective-permute-start(bf16[2048,128]{1,0:T(8,128)(2,1)S(1)} %collective-permute-done.19.p1), channel_id=1, source_target_pairs={{0,1},{1,0},{2,3},{3,2},{4,5},{5,4},{6,7},{7,6},{8,9},{9,8},{10,11... | collective-permute-start | bytes 1572872 | tf_op jit(solution)/shard_map/ppermute | solution.py:181
  111.7 12.1 %collective-permute-start.24 = (bf16[2048,128]{1,0:T(8,128)(2,1)}, bf16[2048,128]{1,0:T(8,128)(2,1)S(1)}, u32[]{:S(2)}, u32[]{:S(2)}) collective-permute-start(bf16[2048,128]{1,0:T(8,128)(2,1)} %collective-permute-done.20.p2), channel_id=1, source_target_pairs={{0,1},{1,0},{2,3},{3,2},{4,5},{5,4},{6,7},{7,6},{8,9},{9,8},{10,11... | collective-permute-start | bytes 1572872 | tf_op jit(solution)/shard_map/ppermute | solution.py:181
  111.7 12.1 %collective-permute-start.25 = (bf16[2048,128]{1,0:T(8,128)(2,1)}, bf16[2048,128]{1,0:T(8,128)(2,1)S(1)}, u32[]{:S(2)}, u32[]{:S(2)}) collective-permute-start(bf16[2048,128]{1,0:T(8,128)(2,1)} %collective-permute-done.21.p3), channel_id=1, source_target_pairs={{0,1},{1,0},{2,3},{3,2},{4,5},{5,4},{6,7},{7,6},{8,9},{9,8},{10,11... | collective-permute-start | bytes 1572872 | tf_op jit(solution)/shard_map/ppermute | solution.py:181
  118.9 12.2 %slice-start = ((s8[8388608]{0:T(1024)(128)(4,1)}), s8[4194304]{0:T(1024)(128)(4,1)S(1)}, s32[]{:S(2)}) async-start(s8[8388608]{0:T(1024)(128)(4,1)} %bitcast.9), calls=%async_computation.1 | async-start | bytes 8388608
  118.9 12.2 %slice-start.1 = ((s8[8388608]{0:T(1024)(128)(4,1)}), s8[4194304]{0:T(1024)(128)(4,1)S(1)}, s32[]{:S(2)}) async-start(s8[8388608]{0:T(1024)(128)(4,1)} %bitcast.9), calls=%async_computation.2 | async-start | bytes 8388608
  118.9 17.6 %collective-permute-start.16 = (bf16[256,1024]{1,0:T(8,128)(2,1)S(1)}, bf16[256,1024]{1,0:T(8,128)(2,1)S(1)}, u32[]{:S(2)}, u32[]{:S(2)}) collective-permute-start(bf16[256,1024]{1,0:T(8,128)(2,1)S(1)} %get-tuple-element.24.a), channel_id=1, source_target_pairs={{0,24},{8,0},{16,8},{24,16},{32,56},{40,32},{48,40},{56,48},{64,88... | collective-permute-start | bytes 1572872 | tf_op jit(solution)/shard_map/ppermute | solution.py:201
  119.2 17.4 %collective-permute-start.17 = (bf16[256,1024]{1,0:T(8,128)(2,1)S(1)}, bf16[256,1024]{1,0:T(8,128)(2,1)S(1)}, u32[]{:S(2)}, u32[]{:S(2)}) collective-permute-start(bf16[256,1024]{1,0:T(8,128)(2,1)S(1)} %get-tuple-element.24.a), channel_id=1, source_target_pairs={{0,8},{8,16},{16,24},{24,0},{32,40},{40,48},{48,56},{56,32},{64,72... | collective-permute-start | bytes 1572872 | tf_op jit(solution)/shard_map/ppermute | solution.py:202
  122.3 14.4 %collective-permute-start.18 = (bf16[256,1024]{1,0:T(8,128)(2,1)S(1)}, bf16[256,1024]{1,0:T(8,128)(2,1)S(1)}, u32[]{:S(2)}, u32[]{:S(2)}) collective-permute-start(bf16[256,1024]{1,0:T(8,128)(2,1)S(1)} %get-tuple-element.24.a), channel_id=1, source_target_pairs={{0,96},{8,104},{16,112},{24,120},{32,0},{40,8},{48,16},{56,24},{64... | collective-permute-start | bytes 1572872 | tf_op jit(solution)/shard_map/ppermute | solution.py:203
  131.1 5.5 %copy-start.2 = (bf16[2,1024,1024]{2,1,0:T(8,128)(2,1)S(1)}, bf16[2,1024,1024]{2,1,0:T(8,128)(2,1)}, u32[]{:S(2)}) copy-start(bf16[2,1024,1024]{2,1,0:T(8,128)(2,1)} %inv.3) | copy-start | bytes 12582916
  (16 other events, 14.1 us)

commit v3 on v2

--- a/solution.py
+++ b/solution.py
@@ -48,26 +48,43 @@
     return pl.BlockSpec(memory_space=pltpu.VMEM)
 
 
-def place_features(at, refs, dst, rows=None):
-    z, core = at[2], at[3]
+def feature_offset(z, core, i):
+    zz = lax.rem(z + (0, 3, 1, 2)[i % 4], 4)
+    cc = core if i < 4 else 1 - core
+    return pl.multiple_of((zz * 2 + cc) * 128, 128)
+
+
+def place_features(at, refs, dst):
     for i, ref in enumerate(refs):
-        zz = lax.rem(z + (0, 3, 1, 2)[i % 4], 4)
-        cc = core if i < 4 else 1 - core
-        off = pl.multiple_of((zz * 2 + cc) * 128, 128)
-        dst[:, pl.ds(off, 128)] = ref[...]
-
-
-def pack(at, env, low, p0, p1, p2, p3):
+        dst[:, pl.ds(feature_offset(at[2], at[3], i), 128)] = ref[...]
+
+
+def pack(at, env, low, qt, p0, p1, p2, p3, spread, sems):
+    copies = [
+        pltpu.make_async_copy(qt, spread.at[i], sems.at[i]) for i in range(spread.shape[0])
+    ]
+    for copy in copies:
+        copy.start()
     n = env.shape[0] // 4
     for d, out in enumerate((p0, p1, p2, p3)):
         for i, add in enumerate((d, d + 2)):
             src = pl.ds(pl.multiple_of(lax.rem(at[0] + add, 4) * n, n), n)
             out[i * n : (i + 1) * n, :] = env[src, :]
             out[(i + 2) * n : (i + 3) * n, :] = low[src, :]
-
-
-def kernel_slices(at, qt, s0, s1, s2, s3, s4, s5, s6, s7, k0, k1, low, feats):
-    place_features(at, (s0, s1, s2, s3, s4, s5, s6, s7), feats)
+    for copy in copies:
+        copy.wait()
+
+
+def kernel_slices(at, qt, pieces, k0, k1, low, feats, sems):
+    z, core = at[2], at[3]
+    copies = []
+    for i in range(pieces.shape[0]):
+        off = feature_offset(z, core, i)
+        copies.append(pltpu.make_async_copy(pieces.at[i], feats.at[:, pl.ds(off, 128)], sems.at[i]))
+    for copy in copies:
+        copy.start()
+    for copy in copies:
+        copy.wait()
     n = k0.shape[0]
     low[...] = feats[2 * n :, :]
     scale = 1.0 / (qt.shape[0] ** 0.5)
@@ -141,11 +158,8 @@
     piece = sparse_desc.shape[2]
     feats = piece * 2 * N
 
-    qt = query_desc.T
-    spread = jnp.broadcast_to(qt[None], (N * N,) + qt.shape)
-    qt = lax.all_to_all(spread, "rows", 0, 0, tiled=True).reshape(feats, queries)
-
-    got = pl.pallas_call(
+    own_q = query_desc.T
+    *got, spread = pl.pallas_call(
         pack,
         grid_spec=pltpu.PrefetchScalarGridSpec(
             num_scalar_prefetch=1,
@@ -153,12 +167,23 @@
             in_specs=[
                 pl.BlockSpec((None, width, piece), lambda i, at: (0, 0, 0)),
                 pl.BlockSpec((None, width, piece), lambda i, at: (0, 0, at[2] * 2 + at[3])),
+                pl.BlockSpec(own_q.shape, lambda i, at: (0, 0)),
             ],
-            out_specs=[pl.BlockSpec((width, piece), lambda i, at: (0, 0))] * 4,
+            out_specs=[pl.BlockSpec((width, piece), lambda i, at: (0, 0))] * 4
+            + [pl.BlockSpec(memory_space=pl.ANY)],
+            scratch_shapes=[pltpu.SemaphoreType.DMA((N * N,))],
         ),
-        out_shape=[jax.ShapeDtypeStruct((width, piece), BF16)] * 4,
-        compiler_params=params(16),
-    )(after(at, spread), sparse_desc, lower_panel)
+        out_shape=[jax.ShapeDtypeStruct((width, piece), BF16)] * 4
+        + [jax.ShapeDtypeStruct((N * N,) + own_q.shape, BF16)],
+        compiler_params=params(56),
+    )(at, sparse_desc, lower_panel, own_q)
+    qt = lax.all_to_all(spread, "rows", 0, 0, tiled=True).reshape(feats, queries)
+    own = sparse_desc.reshape(blocks * width, piece)
+    early = after(own, got[0])
+    envs = [own] + [lax.ppermute(early, "pb", z_perm(d)) for d in (1, -1)]
+    envs = envs + [lax.ppermute(after(own, envs[1]), "pb", z_perm(2))]
+    envs = envs + [lax.ppermute(v, "pb", SWAP) for v in envs]
+
     got = [got[0]] + [
         lax.ppermute(got[d], "rows", [(0, d), (1, (1 + d) % N)]) for d in (1, 2, 3)
     ]
@@ -167,18 +192,15 @@
     n = quarter
     even = jnp.concatenate([from0[:n], from1[:n], from1[2 * n : 3 * n]])
     odd = jnp.concatenate([from0[n : 2 * n], from1[n : 2 * n], from1[3 * n :]])
+    even, odd, _, _ = lax.optimization_barrier((even, odd, envs[1], envs[2]))
     got_y = [even] + [
         lax.ppermute(even if d == 2 else odd, "rows", [(c, d * N + c) for c in range(N)])
         for d in (1, 2, 3)
     ]
     mine = pick(y, got_y)
+    mine = after(mine, envs[3])
     slices = [mine] + [lax.ppermute(mine, "pb", z_perm(d)) for d in (1, -1, 2)]
     slices = slices + [lax.ppermute(v, "pb", SWAP) for v in slices]
-
-    own = sparse_desc.reshape(blocks * width, piece)
-    envs = [own] + [lax.ppermute(own, "pb", z_perm(d)) for d in (1, -1)]
-    envs = envs + [lax.ppermute(after(own, envs[1]), "pb", z_perm(2))]
-    envs = envs + [lax.ppermute(v, "pb", SWAP) for v in envs]
 
     unit = 2 * width * feats * queries
     k0, k1, low = pl.pallas_call(
@@ -188,12 +210,12 @@
             jax.ShapeDtypeStruct((quarter, queries), F32),
             jax.ShapeDtypeStruct((quarter, width), BF16),
         ),
-        in_specs=[smem] + [whole()] * 9,
+        in_specs=[smem, whole(), pl.BlockSpec(memory_space=pl.ANY)],
         out_specs=(whole(),) * 3,
-        scratch_shapes=[pltpu.VMEM((3 * quarter, feats), BF16)],
-        compiler_params=params(16),
+        scratch_shapes=[pltpu.VMEM((3 * quarter, feats), BF16), pltpu.SemaphoreType.DMA((8,))],
+        compiler_params=params(56),
         cost_estimate=cost(unit / 2, 5e6),
-    )(at, qt, *slices)
+    )(at, qt, jnp.stack(slices))
 
     def neighbours(v):
         return (

time: 147 us -> 126 us (0.86)
  waiting for transfers between devices: 57.2 us -> 34.7 us
  local copies, waits for them, and re-layouts: 20 us -> 12.4 us
  Pallas kernels: 29.5 us -> 35.5 us
  starting transfers between devices: 36.4 us -> 40.8 us
    ppermute x3, waiting for transfers between devices: 30.8 us -> 9.5 us  [per_device(): lax.ppermute(got[d], 'rows', [(0, d), (1, (1 + d) % N)])]
    all_to_all x1, waiting for transfers between devices: 0.01 us -> 7.88 us  [per_device(): lax.all_to_all(spread, 'rows', 0, 0, tiled=True).reshape(feats, queries)]
    ppermute x3, waiting for transfers between devices: 13.3 us -> 6.32 us  [per_device(): slices = [mine] + [lax.ppermute(mine, 'pb', z_perm(d)) for d in (1, -1, 2)]]
    unnamed x42 -> x33, local copies, waits for them, and re-layouts: 17.5 us -> 11.7 us
    pallas_call x1, Pallas kernels: 2.32 us -> 5.7 us  [per_device(): pl.pallas_call(kernel_slices, out_shape=(jax.ShapeDtypeStruct((quarter, q...]
    ppermute x2, waiting for transfers between devices: 11.5 us -> 8.28 us  [neighbours(): lax.ppermute(v, 'rows', x_perm(-1))]
    pallas_call x1, Pallas kernels: 1.37 us -> 4.3 us  [per_device(): pl.pallas_call(pack, grid_spec=pltpu.PrefetchScalarGridSpec(num_scalar_pr...]
    broadcast_in_dim x1 -> x0, local copies, waits for them, and re-layouts: 2.54 us -> none  [per_device(): spread = jnp.broadcast_to(qt[None], (N * N,) + qt.shape)]
  transfers between devices with their start and end apart: 27 -> 27, of which waited for: 7 -> 7; matrix products, arithmetic and copies ran while one was open for 2% -> 5% of each run, Pallas kernels for 14% -> 13%
where the time goes in v3:
time: 126 us; the launch traced here: 125 us
  starting transfers between devices  40.8 us (32%)
  Pallas kernels  35.5 us (28%)
  waiting for transfers between devices  34.7 us (28%)
  local copies, waits for them, and re-layouts  12.4 us (10%)
  other arithmetic  1.65 us (1%)
    unnamed x33, local copies, waits for them, and re-layouts  11.7 us
    ppermute x3, waiting for transfers between devices, per_device(): lax.ppermute(got[d], 'rows', [(0, d), (1, (1 + d) % N)])  9.5 us
    pallas_call x1, Pallas kernels, per_device(): pl.pallas_call(last_step, grid=(rows // bm,), out_shape=jax.ShapeDtypeStr...  9.42 us
    ppermute x2, waiting for transfers between devices, neighbours(): lax.ppermute(v, 'rows', x_perm(-1))  8.28 us
    all_to_all x1, waiting for transfers between devices, per_device(): lax.all_to_all(spread, 'rows', 0, 0, tiled=True).reshape(feats, queries)  7.88 us
    pallas_call x1, Pallas kernels, per_device(): pl.pallas_call(kernel_rows, grid=(rows // bm,), out_shape=jax.ShapeDtypeS...  7.22 us
    ppermute x3, starting transfers between devices, per_device(): lax.ppermute(even if d == 2 else odd, 'rows', [(c, d * N + c) for c in ra...  7.17 us
    all_to_all x1, starting transfers between devices, per_device(): lax.all_to_all(spread, 'rows', 0, 0, tiled=True).reshape(feats, queries)  6.53 us
  transfers between devices with their start and end apart: 27, of which 7 were waited for; matrix products, arithmetic and copies ran while one was open for 5% of the time, Pallas kernels for 13%

profile of v3, /device:TPU:6, one launch (start us, length us, event | category | flops | bytes accessed | tf_op | source)
XLA Modules:
  0.0 125.4 jit_solution(14664534064377316784)
XLA Ops:
  0.6 4.3 %shard_map.46 = (bf16[1024,128]{1,0:T(8,128)(2,1)}, bf16[1024,128]{1,0:T(8,128)(2,1)}, bf16[1024,128]{1,0:T(8,128)(2,1)}, bf16[1024,128]{1,0:T(8,128)(2,1)}, bf16[16,64,1024]{2,1,0:T(8,128)(2,1)}) custom-call(s32[4]{0:T(128)} %pad_add_fusion.at, bf16[2,1024,128]{2,1,0:T(8,128)(2,1)} %env.1, bf16[2,1024,2048]{2,1,0:T(8,128)(2,1)} %low.1, ...), custom_call_target="tpu_custom_call" | custom-call | tf_op jit(solution)/shard_map/pallas_call | solution.py:162
  4.9 1.3 %collective-permute-start = (bf16[1024,128]{1,0:T(8,128)(2,1)}, bf16[1024,128]{1,0:T(8,128)(2,1)S(1)}, u32[]{:S(2)}, u32[]{:S(2)}) collective-permute-start(bf16[1024,128]{1,0:T(8,128)(2,1)} %get-tuple-element.21), channel_id=1, source_target_pairs={{0,24},{8,0},{1,25},{9,1},{2,26},{10,2},{3,27},{11,3},{4,28},{12,4... | collective-permute-start | bytes 786440 | tf_op jit(solution)/shard_map/ppermute | solution.py:188
  6.2 1.3 %collective-permute-start.1 = (bf16[1024,128]{1,0:T(8,128)(2,1)}, bf16[1024,128]{1,0:T(8,128)(2,1)S(1)}, u32[]{:S(2)}, u32[]{:S(2)}) collective-permute-start(bf16[1024,128]{1,0:T(8,128)(2,1)} %get-tuple-element.22), channel_id=1, source_target_pairs={{0,16},{8,24},{1,17},{9,25},{2,18},{10,26},{3,19},{11,27},{4,20},{... | collective-permute-start | bytes 786440 | tf_op jit(solution)/shard_map/ppermute | solution.py:188
  8.2 2.0 %collective-permute-start.3 = (bf16[2048,128]{1,0:T(8,128)(2,1)S(1)}, bf16[2048,128]{1,0:T(8,128)(2,1)S(1)}, u32[]{:S(2)}, u32[]{:S(2)}) collective-permute-start(bf16[2048,128]{1,0:T(8,128)(2,1)S(1)} %bitcast.31), channel_id=1, source_target_pairs={{0,2},{1,3},{2,4},{3,5},{4,6},{5,7},{6,0},{7,1},{8,10},{9,11},{10,... | collective-permute-start | bytes 1572872 | tf_op jit(solution)/shard_map/ppermute | solution.py:183
  10.2 2.2 %collective-permute-start.4 = (bf16[2048,128]{1,0:T(8,128)(2,1)S(1)}, bf16[2048,128]{1,0:T(8,128)(2,1)S(1)}, u32[]{:S(2)}, u32[]{:S(2)}) collective-permute-start(bf16[2048,128]{1,0:T(8,128)(2,1)S(1)} %bitcast.32), channel_id=1, source_target_pairs={{0,6},{1,7},{2,0},{3,1},{4,2},{5,3},{6,4},{7,5},{8,14},{9,15},{10,... | collective-permute-start | bytes 1572872 | tf_op jit(solution)/shard_map/ppermute | solution.py:183
  12.4 9.5 %collective-permute-done = bf16[1024,128]{1,0:T(8,128)(2,1)S(1)} collective-permute-done((bf16[1024,128]{1,0:T(8,128)(2,1)}, bf16[1024,128]{1,0:T(8,128)(2,1)S(1)}, u32[]{:S(2)}, u32[]{:S(2)}) %collective-permute-start) | collective-permute-done | bytes 262176 | tf_op jit(solution)/shard_map/ppermute | solution.py:188
  22.9 1.3 %collective-permute-done.3.p1 = bf16[2048,128]{1,0:T(8,128)(2,1)S(1)} collective-permute-done((bf16[2048,128]{1,0:T(8,128)(2,1)S(1)}, bf16[2048,128]{1,0:T(8,128)(2,1)S(1)}, u32[]{:S(2)}, u32[]{:S(2)}) %collective-permute-start.3) | collective-permute-done | bytes 524320 | tf_op jit(solution)/shard_map/ppermute | solution.py:183
  24.2 2.7 %collective-permute-start.8 = (bf16[2048,128]{1,0:T(8,128)(2,1)S(1)}, bf16[2048,128]{1,0:T(8,128)(2,1)}, u32[]{:S(2)}, u32[]{:S(2)}) collective-permute-start(bf16[2048,128]{1,0:T(8,128)(2,1)S(1)} %bitcast.33), channel_id=1, source_target_pairs={{0,4},{1,5},{2,6},{3,7},{4,0},{5,1},{6,2},{7,3},{8,12},{9,13},{10,... | collective-permute-start | bytes 1572872 | tf_op jit(solution)/shard_map/ppermute | solution.py:184
  26.9 3.3 %collective-permute-start.5 = (bf16[768,128]{1,0:T(8,128)(2,1)S(1)}, bf16[768,128]{1,0:T(8,128)(2,1)}, u32[]{:S(2)}, u32[]{:S(2)}) collective-permute-start(bf16[768,128]{1,0:T(8,128)(2,1)S(1)} %pad_maximum_fusion.1), channel_id=1, source_target_pairs={{0,96},{8,104},{16,112},{24,120},{1,97},{9,105},{17,113},{25,121},... | collective-permute-start | bytes 589832 | tf_op jit(solution)/shard_map/ppermute | solution.py:197
  30.2 2.0 %collective-permute-start.6 = (bf16[768,128]{1,0:T(8,128)(2,1)S(1)}, bf16[768,128]{1,0:T(8,128)(2,1)}, u32[]{:S(2)}, u32[]{:S(2)}) collective-permute-start(bf16[768,128]{1,0:T(8,128)(2,1)S(1)} %pad_maximum_fusion), channel_id=1, source_target_pairs={{0,64},{8,72},{16,80},{24,88},{1,65},{9,73},{17,81},{25,89},{2,66}... | collective-permute-start | bytes 589832 | tf_op jit(solution)/shard_map/ppermute | solution.py:197
  32.1 2.0 %collective-permute-start.7 = (bf16[768,128]{1,0:T(8,128)(2,1)S(1)}, bf16[768,128]{1,0:T(8,128)(2,1)}, u32[]{:S(2)}, u32[]{:S(2)}) collective-permute-start(bf16[768,128]{1,0:T(8,128)(2,1)S(1)} %pad_maximum_fusion.1), channel_id=1, source_target_pairs={{0,32},{8,40},{16,48},{24,56},{1,33},{9,41},{17,49},{25,57},{2,34}... | collective-permute-start | bytes 589832 | tf_op jit(solution)/shard_map/ppermute | solution.py:197
  34.1 6.5 %all-to-all-start = ((bf16[16,64,1024]{2,1,0:T(8,128)(2,1)}), bf16[16,64,1024]{2,1,0:T(8,128)(2,1)S(1)}, u32[]{:S(2)}, u32[]{:S(2)}) async-start(bf16[16,64,1024]{2,1,0:T(8,128)(2,1)} %get-tuple-element.20), calls=%async_computation | async-start | bytes 4194304 | tf_op jit(solution)/shard_map/all_to_all | solution.py:180
  40.7 1.1 collective-permute-start.9
  41.8 2.2 %collective-permute-start.10 = (bf16[768,128]{1,0:T(8,128)(2,1)S(1)}, bf16[768,128]{1,0:T(8,128)(2,1)S(1)}, u32[]{:S(2)}, u32[]{:S(2)}) collective-permute-start(bf16[768,128]{1,0:T(8,128)(2,1)S(1)} %select_select_fusion.2), channel_id=1, source_target_pairs={{0,6},{1,7},{2,0},{3,1},{4,2},{5,3},{6,4},{7,5},{8,14},{9,15},{10,... | collective-permute-start | bytes 589832 | tf_op jit(solution)/shard_map/ppermute | solution.py:202
  45.5 6.3 %collective-permute-done.9 = bf16[768,128]{1,0:T(8,128)(2,1)S(1)} collective-permute-done((bf16[768,128]{1,0:T(8,128)(2,1)S(1)}, bf16[768,128]{1,0:T(8,128)(2,1)S(1)}, u32[]{:S(2)}, u32[]{:S(2)}) %collective-permute-start.9) | collective-permute-done | bytes 196640 | tf_op jit(solution)/shard_map/ppermute | solution.py:202
  57.2 7.9 %all-to-all-done = bf16[16,64,1024]{2,1,0:T(8,128)(2,1)S(1)} async-done(((bf16[16,64,1024]{2,1,0:T(8,128)(2,1)}), bf16[16,64,1024]{2,1,0:T(8,128)(2,1)S(1)}, u32[]{:S(2)}, u32[]{:S(2)}) %all-to-all-start) | async-done | bytes 2097184 | tf_op jit(solution)/shard_map/all_to_all | solution.py:180
  65.1 1.3 %copy-done.2 = bf16[16,64,1024]{2,1,0:T(8,128)(2,1)} copy-done((bf16[16,64,1024]{2,1,0:T(8,128)(2,1)}, bf16[16,64,1024]{2,1,0:T(8,128)(2,1)S(1)}, u32[]{:S(2)}) %copy-start.2) | copy-done | bytes 2097176
  66.4 5.7 %shard_map.47 = (bf16[256,1024]{1,0:T(8,128)(2,1)}, f32[256,1024]{1,0:T(8,128)}, bf16[256,1024]{1,0:T(8,128)(2,1)}) custom-call(s32[4]{0:T(128)} %pad_add_fusion.at, bf16[1024,1024]{1,0:T(8,128)(2,1)} %bitcast.29, bf16[8,768,128]{2,1,0:T(8,128)(2,1)} %bitcast_dynamic-update-slice_fusion.pieces), custom_call_target="tpu_custom_call" | custom-call | flops 1073741824 | bytes 5000000 | tf_op jit(solution)/shard_map/pallas_call | solution.py:206
  72.1 1.4 %collective-permute-start.16 = (bf16[256,1024]{1,0:T(8,128)(2,1)}, bf16[256,1024]{1,0:T(8,128)(2,1)S(1)}, u32[]{:S(2)}, u32[]{:S(2)}) collective-permute-start(bf16[256,1024]{1,0:T(8,128)(2,1)} %get-tuple-element.30.a), channel_id=1, source_target_pairs={{0,24},{8,0},{16,8},{24,16},{32,56},{40,32},{48,40},{56,48},{64,88... | collective-permute-start | bytes 1572872 | tf_op jit(solution)/shard_map/ppermute | solution.py:223
  73.5 3.4 %collective-permute-start.17 = (bf16[256,1024]{1,0:T(8,128)(2,1)}, bf16[256,1024]{1,0:T(8,128)(2,1)S(1)}, u32[]{:S(2)}, u32[]{:S(2)}) collective-permute-start(bf16[256,1024]{1,0:T(8,128)(2,1)} %get-tuple-element.30.a), channel_id=1, source_target_pairs={{0,8},{8,16},{16,24},{24,0},{32,40},{40,48},{48,56},{56,32},{64,72... | collective-permute-start | bytes 1572872 | tf_op jit(solution)/shard_map/ppermute | solution.py:224
  78.0 8.3 %collective-permute-done.16.b = bf16[256,1024]{1,0:T(8,128)(2,1)S(1)} collective-permute-done((bf16[256,1024]{1,0:T(8,128)(2,1)}, bf16[256,1024]{1,0:T(8,128)(2,1)S(1)}, u32[]{:S(2)}, u32[]{:S(2)}) %collective-permute-start.16) | collective-permute-done | bytes 524320 | tf_op jit(solution)/shard_map/ppermute | solution.py:223
  87.8 2.2 %copy-done = bf16[2,1024,1024]{2,1,0:T(8,128)(2,1)S(1)} copy-done((bf16[2,1024,1024]{2,1,0:T(8,128)(2,1)S(1)}, bf16[2,1024,1024]{2,1,0:T(8,128)(2,1)}, u32[]{:S(2)}) %copy-start) | copy-done | bytes 4194328
  90.0 1.0 copy-done.8
  91.0 1.2 copy-done.9
  92.3 1.0 copy-done.10
  93.3 3.5 %shard_map.48 = (bf16[1024,1024]{1,0:T(8,128)(2,1)S(1)}, bf16[256,1024]{1,0:T(8,128)(2,1)S(1)}) custom-call(s32[4]{0:T(128)S(1)} %copy-done.5, bf16[256,1024]{1,0:T(8,128)(2,1)S(1)} %copy-done.8, bf16[256,1024]{1,0:T(8,128)(2,1)S(1)} %collective-permute-done.16.b, bf16[256,1024]{1,0:T(8,128)(2,1)S(1)} %collective-permute-done.17.c, ...), custom_call_target="tpu_custom_call" | custom-call | flops 2684354560 | bytes 8000000 | tf_op jit(solution)/shard_map/pallas_call | solution.py:229
  96.9 1.7 %collective-permute-start.19 = (bf16[256,1024]{1,0:T(8,128)(2,1)S(1)}, bf16[256,1024]{1,0:T(8,128)(2,1)S(1)}, u32[]{:S(2)}, u32[]{:S(2)}) collective-permute-start(bf16[256,1024]{1,0:T(8,128)(2,1)S(1)} %get-tuple-element.33.a), channel_id=1, source_target_pairs={{0,24},{8,0},{16,8},{24,16},{32,56},{40,32},{48,40},{56,48},{64,88... | collective-permute-start | bytes 1572872 | tf_op jit(solution)/shard_map/ppermute | solution.py:223
  98.6 1.6 %collective-permute-start.20 = (bf16[256,1024]{1,0:T(8,128)(2,1)S(1)}, bf16[256,1024]{1,0:T(8,128)(2,1)S(1)}, u32[]{:S(2)}, u32[]{:S(2)}) collective-permute-start(bf16[256,1024]{1,0:T(8,128)(2,1)S(1)} %get-tuple-element.33.a), channel_id=1, source_target_pairs={{0,8},{8,16},{16,24},{24,0},{32,40},{40,48},{48,56},{56,32},{64,72... | collective-permute-start | bytes 1572872 | tf_op jit(solution)/shard_map/ppermute | solution.py:224
  100.2 3.1 %collective-permute-start.21 = (bf16[256,1024]{1,0:T(8,128)(2,1)S(1)}, bf16[256,1024]{1,0:T(8,128)(2,1)S(1)}, u32[]{:S(2)}, u32[]{:S(2)}) collective-permute-start(bf16[256,1024]{1,0:T(8,128)(2,1)S(1)} %get-tuple-element.33.a), channel_id=1, source_target_pairs={{0,96},{8,104},{16,112},{24,120},{32,0},{40,8},{48,16},{56,24},{64... | collective-permute-start | bytes 1572872 | tf_op jit(solution)/shard_map/ppermute | solution.py:225
  103.3 7.2 %shard_map.49.k = f32[2048,1024]{1,0:T(8,128)S(1)} custom-call(s32[4]{0:T(128)S(1)} %copy-done.5, bf16[1024,1024]{1,0:T(8,128)(2,1)S(1)} %bitcast.30, bf16[2048,128]{1,0:T(8,128)(2,1)S(1)} %bitcast.35, bf16[2048,128]{1,0:T(8,128)(2,1)S(1)} %collective-permute-done.3.p1, bf16[2048,128]{1,0:T(8,128)(2,1)S(1)} %copy-done.7, ...), custom_call_target="tpu_custom_call" | custom-call | flops 4294967296 | bytes 14000000 | tf_op jit(solution)/shard_map/pallas_call | solution.py:246
  110.6 5.3 %shard_map.50.res = f32[2048,1024]{1,0:T(8,128)S(1)} custom-call(bf16[1024,1024]{1,0:T(8,128)(2,1)S(1)} %get-tuple-element.34.s0, bf16[2048,2048]{1,0:T(8,128)(2,1)S(1)} %bitcast.27, f32[2048,1024]{1,0:T(8,128)S(1)} %shard_map.49.k), custom_call_target="tpu_custom_call" | custom-call | flops 4294967296 | bytes 22000000 | tf_op jit(solution)/shard_map/pallas_call | solution.py:256
  116.0 9.4 %shard_map.51 = bf16[2048,1024]{1,0:T(8,128)(2,1)} custom-call(s32[4]{0:T(128)S(1)} %copy-done.5, bf16[256,1024]{1,0:T(8,128)(2,1)S(1)} %get-tuple-element.33.a, bf16[256,1024]{1,0:T(8,128)(2,1)S(1)} %collective-permute-done.19.b, bf16[256,1024]{1,0:T(8,128)(2,1)S(1)} %collective-permute-done.20.c, bf16[256,1024]{1,0:T(8,128)(2,1)S(1)} %collective-permute-done.21.d, ...), custom_call_target="tpu_custom_call" | custom-call | flops 6442450944 | bytes 20000000 | tf_op jit(solution)/shard_map/pallas_call | solution.py:271
  (69 shorter events, 11.9 us)
Async XLA Ops:
  4.9 17.0 %collective-permute-start = (bf16[1024,128]{1,0:T(8,128)(2,1)}, bf16[1024,128]{1,0:T(8,128)(2,1)S(1)}, u32[]{:S(2)}, u32[]{:S(2)}) collective-permute-start(bf16[1024,128]{1,0:T(8,128)(2,1)} %get-tuple-element.21), channel_id=1, source_target_pairs={{0,24},{8,0},{1,25},{9,1},{2,26},{10,2},{3,27},{11,3},{4,28},{12,4... | collective-permute-start | bytes 786440 | tf_op jit(solution)/shard_map/ppermute | solution.py:188
  6.2 15.7 %collective-permute-start.1 = (bf16[1024,128]{1,0:T(8,128)(2,1)}, bf16[1024,128]{1,0:T(8,128)(2,1)S(1)}, u32[]{:S(2)}, u32[]{:S(2)}) collective-permute-start(bf16[1024,128]{1,0:T(8,128)(2,1)} %get-tuple-element.22), channel_id=1, source_target_pairs={{0,16},{8,24},{1,17},{9,25},{2,18},{10,26},{3,19},{11,27},{4,20},{... | collective-permute-start | bytes 786440 | tf_op jit(solution)/shard_map/ppermute | solution.py:188
  7.5 14.4 %collective-permute-start.2 = (bf16[1024,128]{1,0:T(8,128)(2,1)}, bf16[1024,128]{1,0:T(8,128)(2,1)S(1)}, u32[]{:S(2)}, u32[]{:S(2)}) collective-permute-start(bf16[1024,128]{1,0:T(8,128)(2,1)} %get-tuple-element.23), channel_id=1, source_target_pairs={{0,8},{8,16},{1,9},{9,17},{2,10},{10,18},{3,11},{11,19},{4,12},{12... | collective-permute-start | bytes 786440 | tf_op jit(solution)/shard_map/ppermute | solution.py:188
  8.2 16.0 %collective-permute-start.3 = (bf16[2048,128]{1,0:T(8,128)(2,1)S(1)}, bf16[2048,128]{1,0:T(8,128)(2,1)S(1)}, u32[]{:S(2)}, u32[]{:S(2)}) collective-permute-start(bf16[2048,128]{1,0:T(8,128)(2,1)S(1)} %bitcast.31), channel_id=1, source_target_pairs={{0,2},{1,3},{2,4},{3,5},{4,6},{5,7},{6,0},{7,1},{8,10},{9,11},{10,... | collective-permute-start | bytes 1572872 | tf_op jit(solution)/shard_map/ppermute | solution.py:183
  10.2 16.8 %collective-permute-start.4 = (bf16[2048,128]{1,0:T(8,128)(2,1)S(1)}, bf16[2048,128]{1,0:T(8,128)(2,1)S(1)}, u32[]{:S(2)}, u32[]{:S(2)}) collective-permute-start(bf16[2048,128]{1,0:T(8,128)(2,1)S(1)} %bitcast.32), channel_id=1, source_target_pairs={{0,6},{1,7},{2,0},{3,1},{4,2},{5,3},{6,4},{7,5},{8,14},{9,15},{10,... | collective-permute-start | bytes 1572872 | tf_op jit(solution)/shard_map/ppermute | solution.py:183
  24.2 16.5 %collective-permute-start.8 = (bf16[2048,128]{1,0:T(8,128)(2,1)S(1)}, bf16[2048,128]{1,0:T(8,128)(2,1)}, u32[]{:S(2)}, u32[]{:S(2)}) collective-permute-start(bf16[2048,128]{1,0:T(8,128)(2,1)S(1)} %bitcast.33), channel_id=1, source_target_pairs={{0,4},{1,5},{2,6},{3,7},{4,0},{5,1},{6,2},{7,3},{8,12},{9,13},{10,... | collective-permute-start | bytes 1572872 | tf_op jit(solution)/shard_map/ppermute | solution.py:184
  26.9 13.7 %collective-permute-start.5 = (bf16[768,128]{1,0:T(8,128)(2,1)S(1)}, bf16[768,128]{1,0:T(8,128)(2,1)}, u32[]{:S(2)}, u32[]{:S(2)}) collective-permute-start(bf16[768,128]{1,0:T(8,128)(2,1)S(1)} %pad_maximum_fusion.1), channel_id=1, source_target_pairs={{0,96},{8,104},{16,112},{24,120},{1,97},{9,105},{17,113},{25,121},... | collective-permute-start | bytes 589832 | tf_op jit(solution)/shard_map/ppermute | solution.py:197
  30.2 10.5 %collective-permute-start.6 = (bf16[768,128]{1,0:T(8,128)(2,1)S(1)}, bf16[768,128]{1,0:T(8,128)(2,1)}, u32[]{:S(2)}, u32[]{:S(2)}) collective-permute-start(bf16[768,128]{1,0:T(8,128)(2,1)S(1)} %pad_maximum_fusion), channel_id=1, source_target_pairs={{0,64},{8,72},{16,80},{24,88},{1,65},{9,73},{17,81},{25,89},{2,66}... | collective-permute-start | bytes 589832 | tf_op jit(solution)/shard_map/ppermute | solution.py:197
  32.1 8.5 %collective-permute-start.7 = (bf16[768,128]{1,0:T(8,128)(2,1)S(1)}, bf16[768,128]{1,0:T(8,128)(2,1)}, u32[]{:S(2)}, u32[]{:S(2)}) collective-permute-start(bf16[768,128]{1,0:T(8,128)(2,1)S(1)} %pad_maximum_fusion.1), channel_id=1, source_target_pairs={{0,32},{8,40},{16,48},{24,56},{1,33},{9,41},{17,49},{25,57},{2,34}... | collective-permute-start | bytes 589832 | tf_op jit(solution)/shard_map/ppermute | solution.py:197
  34.1 31.0 %all-to-all-start = ((bf16[16,64,1024]{2,1,0:T(8,128)(2,1)}), bf16[16,64,1024]{2,1,0:T(8,128)(2,1)S(1)}, u32[]{:S(2)}, u32[]{:S(2)}) async-start(bf16[16,64,1024]{2,1,0:T(8,128)(2,1)} %get-tuple-element.20), calls=%async_computation | async-start | bytes 4194304 | tf_op jit(solution)/shard_map/all_to_all | solution.py:180
  40.7 11.1 %collective-permute-start.9 = (bf16[768,128]{1,0:T(8,128)(2,1)S(1)}, bf16[768,128]{1,0:T(8,128)(2,1)S(1)}, u32[]{:S(2)}, u32[]{:S(2)}) collective-permute-start(bf16[768,128]{1,0:T(8,128)(2,1)S(1)} %select_select_fusion.2), channel_id=1, source_target_pairs={{0,2},{1,3},{2,4},{3,5},{4,6},{5,7},{6,0},{7,1},{8,10},{9,11},{10,... | collective-permute-start | bytes 589832 | tf_op jit(solution)/shard_map/ppermute | solution.py:202
  41.8 10.0 %collective-permute-start.10 = (bf16[768,128]{1,0:T(8,128)(2,1)S(1)}, bf16[768,128]{1,0:T(8,128)(2,1)S(1)}, u32[]{:S(2)}, u32[]{:S(2)}) collective-permute-start(bf16[768,128]{1,0:T(8,128)(2,1)S(1)} %select_select_fusion.2), channel_id=1, source_target_pairs={{0,6},{1,7},{2,0},{3,1},{4,2},{5,3},{6,4},{7,5},{8,14},{9,15},{10,... | collective-permute-start | bytes 589832 | tf_op jit(solution)/shard_map/ppermute | solution.py:202
  44.0 8.3 %collective-permute-start.11 = (bf16[768,128]{1,0:T(8,128)(2,1)S(1)}, bf16[768,128]{1,0:T(8,128)(2,1)S(1)}, u32[]{:S(2)}, u32[]{:S(2)}) collective-permute-start(bf16[768,128]{1,0:T(8,128)(2,1)S(1)} %select_select_fusion.2), channel_id=1, source_target_pairs={{0,4},{1,5},{2,6},{3,7},{4,0},{5,1},{6,2},{7,3},{8,12},{9,13},{10,... | collective-permute-start | bytes 589832 | tf_op jit(solution)/shard_map/ppermute | solution.py:202
  44.8 9.7 %collective-permute-start.12 = (bf16[768,128]{1,0:T(8,128)(2,1)S(1)}, bf16[768,128]{1,0:T(8,128)(2,1)S(1)}, u32[]{:S(2)}, u32[]{:S(2)}) collective-permute-start(bf16[768,128]{1,0:T(8,128)(2,1)S(1)} %select_select_fusion.2), channel_id=1, source_target_pairs={{0,1},{1,0},{2,3},{3,2},{4,5},{5,4},{6,7},{7,6},{8,9},{9,8},{10,11... | collective-permute-start | bytes 589832 | tf_op jit(solution)/shard_map/ppermute | solution.py:203
  51.8 3.4 %collective-permute-start.13 = (bf16[768,128]{1,0:T(8,128)(2,1)S(1)}, bf16[768,128]{1,0:T(8,128)(2,1)S(1)}, u32[]{:S(2)}, u32[]{:S(2)}) collective-permute-start(bf16[768,128]{1,0:T(8,128)(2,1)S(1)} %collective-permute-done.9), channel_id=1, source_target_pairs={{0,1},{1,0},{2,3},{3,2},{4,5},{5,4},{6,7},{7,6},{8,9},{9,8},{10,11... | collective-permute-start | bytes 589832 | tf_op jit(solution)/shard_map/ppermute | solution.py:203
  51.8 4.0 %collective-permute-start.14 = (bf16[768,128]{1,0:T(8,128)(2,1)S(1)}, bf16[768,128]{1,0:T(8,128)(2,1)S(1)}, u32[]{:S(2)}, u32[]{:S(2)}) collective-permute-start(bf16[768,128]{1,0:T(8,128)(2,1)S(1)} %collective-permute-done.10), channel_id=1, source_target_pairs={{0,1},{1,0},{2,3},{3,2},{4,5},{5,4},{6,7},{7,6},{8,9},{9,8},{10,11... | collective-permute-start | bytes 589832 | tf_op jit(solution)/shard_map/ppermute | solution.py:203
  52.3 4.2 %collective-permute-start.15 = (bf16[768,128]{1,0:T(8,128)(2,1)S(1)}, bf16[768,128]{1,0:T(8,128)(2,1)S(1)}, u32[]{:S(2)}, u32[]{:S(2)}) collective-permute-start(bf16[768,128]{1,0:T(8,128)(2,1)S(1)} %collective-permute-done.11), channel_id=1, source_target_pairs={{0,1},{1,0},{2,3},{3,2},{4,5},{5,4},{6,7},{7,6},{8,9},{9,8},{10,11... | collective-permute-start | bytes 589832 | tf_op jit(solution)/shard_map/ppermute | solution.py:203
  66.4 19.9 %copy-start.7 = (bf16[2048,128]{1,0:T(8,128)(2,1)S(1)}, bf16[2048,128]{1,0:T(8,128)(2,1)}, u32[]{:S(2)}) copy-start(bf16[2048,128]{1,0:T(8,128)(2,1)} %copy-done.6) | copy-start | bytes 1572868
  66.4 21.4 %copy-start.5 = (s32[4]{0:T(128)S(1)}, s32[4]{0:T(128)}, u32[]{:S(2)}) copy-start(s32[4]{0:T(128)} %pad_add_fusion.at) | copy-start | bytes 52
  72.1 14.2 %collective-permute-start.16 = (bf16[256,1024]{1,0:T(8,128)(2,1)}, bf16[256,1024]{1,0:T(8,128)(2,1)S(1)}, u32[]{:S(2)}, u32[]{:S(2)}) collective-permute-start(bf16[256,1024]{1,0:T(8,128)(2,1)} %get-tuple-element.30.a), channel_id=1, source_target_pairs={{0,24},{8,0},{16,8},{24,16},{32,56},{40,32},{48,40},{56,48},{64,88... | collective-permute-start | bytes 1572872 | tf_op jit(solution)/shard_map/ppermute | solution.py:223
  73.5 13.7 %collective-permute-start.17 = (bf16[256,1024]{1,0:T(8,128)(2,1)}, bf16[256,1024]{1,0:T(8,128)(2,1)S(1)}, u32[]{:S(2)}, u32[]{:S(2)}) collective-permute-start(bf16[256,1024]{1,0:T(8,128)(2,1)} %get-tuple-element.30.a), channel_id=1, source_target_pairs={{0,8},{8,16},{16,24},{24,0},{32,40},{40,48},{48,56},{56,32},{64,72... | collective-permute-start | bytes 1572872 | tf_op jit(solution)/shard_map/ppermute | solution.py:224
  76.9 10.9 %collective-permute-start.18 = (bf16[256,1024]{1,0:T(8,128)(2,1)}, bf16[256,1024]{1,0:T(8,128)(2,1)S(1)}, u32[]{:S(2)}, u32[]{:S(2)}) collective-permute-start(bf16[256,1024]{1,0:T(8,128)(2,1)} %get-tuple-element.30.a), channel_id=1, source_target_pairs={{0,96},{8,104},{16,112},{24,120},{32,0},{40,8},{48,16},{56,24},{64... | collective-permute-start | bytes 1572872 | tf_op jit(solution)/shard_map/ppermute | solution.py:225
  77.5 21.0 %collective-permute-start.22 = (bf16[2048,128]{1,0:T(8,128)(2,1)S(1)}, bf16[2048,128]{1,0:T(8,128)(2,1)S(1)}, u32[]{:S(2)}, u32[]{:S(2)}) collective-permute-start(bf16[2048,128]{1,0:T(8,128)(2,1)S(1)} %bitcast.34), channel_id=1, source_target_pairs={{0,1},{1,0},{2,3},{3,2},{4,5},{5,4},{6,7},{7,6},{8,9},{9,8},{10,11... | collective-permute-start | bytes 1572872 | tf_op jit(solution)/shard_map/ppermute | solution.py:185
  77.5 22.6 %collective-permute-start.23 = (bf16[2048,128]{1,0:T(8,128)(2,1)S(1)}, bf16[2048,128]{1,0:T(8,128)(2,1)S(1)}, u32[]{:S(2)}, u32[]{:S(2)}) collective-permute-start(bf16[2048,128]{1,0:T(8,128)(2,1)S(1)} %collective-permute-done.3.p1), channel_id=1, source_target_pairs={{0,1},{1,0},{2,3},{3,2},{4,5},{5,4},{6,7},{7,6},{8,9},{9,8},{10,11... | collective-permute-start | bytes 1572872 | tf_op jit(solution)/shard_map/ppermute | solution.py:185
  86.3 17.0 %collective-permute-start.24 = (bf16[2048,128]{1,0:T(8,128)(2,1)S(1)}, bf16[2048,128]{1,0:T(8,128)(2,1)S(1)}, u32[]{:S(2)}, u32[]{:S(2)}) collective-permute-start(bf16[2048,128]{1,0:T(8,128)(2,1)S(1)} %copy-done.7), channel_id=1, source_target_pairs={{0,1},{1,0},{2,3},{3,2},{4,5},{5,4},{6,7},{7,6},{8,9},{9,8},{10,11... | collective-permute-start | bytes 1572872 | tf_op jit(solution)/shard_map/ppermute | solution.py:185
  87.3 16.1 %collective-permute-start.25 = (bf16[2048,128]{1,0:T(8,128)(2,1)}, bf16[2048,128]{1,0:T(8,128)(2,1)S(1)}, u32[]{:S(2)}, u32[]{:S(2)}) collective-permute-start(bf16[2048,128]{1,0:T(8,128)(2,1)} %collective-permute-done.8.p3), channel_id=1, source_target_pairs={{0,1},{1,0},{2,3},{3,2},{4,5},{5,4},{6,7},{7,6},{8,9},{9,8},{10,11... | collective-permute-start | bytes 1572872 | tf_op jit(solution)/shard_map/ppermute | solution.py:185
  93.3 10.0 %copy-start.3 = (bf16[16,64,1024]{2,1,0:T(8,128)(2,1)S(1)}, bf16[16,64,1024]{2,1,0:T(8,128)(2,1)}, u32[]{:S(2)}) copy-start(bf16[16,64,1024]{2,1,0:T(8,128)(2,1)} %copy-done.2) | copy-start | bytes 6291460
  93.3 17.2 %slice-start = ((s8[8388608]{0:T(1024)(128)(4,1)}), s8[4194304]{0:T(1024)(128)(4,1)S(1)}, s32[]{:S(2)}) async-start(s8[8388608]{0:T(1024)(128)(4,1)} %bitcast.25), calls=%async_computation.1 | async-start | bytes 8388608
  96.9 13.7 %slice-start.1 = ((s8[8388608]{0:T(1024)(128)(4,1)}), s8[4194304]{0:T(1024)(128)(4,1)S(1)}, s32[]{:S(2)}) async-start(s8[8388608]{0:T(1024)(128)(4,1)} %bitcast.25), calls=%async_computation.2 | async-start | bytes 8388608
  96.9 19.1 %collective-permute-start.19 = (bf16[256,1024]{1,0:T(8,128)(2,1)S(1)}, bf16[256,1024]{1,0:T(8,128)(2,1)S(1)}, u32[]{:S(2)}, u32[]{:S(2)}) collective-permute-start(bf16[256,1024]{1,0:T(8,128)(2,1)S(1)} %get-tuple-element.33.a), channel_id=1, source_target_pairs={{0,24},{8,0},{16,8},{24,16},{32,56},{40,32},{48,40},{56,48},{64,88... | collective-permute-start | bytes 1572872 | tf_op jit(solution)/shard_map/ppermute | solution.py:223
  98.6 17.4 %collective-permute-start.20 = (bf16[256,1024]{1,0:T(8,128)(2,1)S(1)}, bf16[256,1024]{1,0:T(8,128)(2,1)S(1)}, u32[]{:S(2)}, u32[]{:S(2)}) collective-permute-start(bf16[256,1024]{1,0:T(8,128)(2,1)S(1)} %get-tuple-element.33.a), channel_id=1, source_target_pairs={{0,8},{8,16},{16,24},{24,0},{32,40},{40,48},{48,56},{56,32},{64,72... | collective-permute-start | bytes 1572872 | tf_op jit(solution)/shard_map/ppermute | solution.py:224
  100.2 15.8 %collective-permute-start.21 = (bf16[256,1024]{1,0:T(8,128)(2,1)S(1)}, bf16[256,1024]{1,0:T(8,128)(2,1)S(1)}, u32[]{:S(2)}, u32[]{:S(2)}) collective-permute-start(bf16[256,1024]{1,0:T(8,128)(2,1)S(1)} %get-tuple-element.33.a), channel_id=1, source_target_pairs={{0,96},{8,104},{16,112},{24,120},{32,0},{40,8},{48,16},{56,24},{64... | collective-permute-start | bytes 1572872 | tf_op jit(solution)/shard_map/ppermute | solution.py:225
  (8 other events, 27.0 us)

commit v4 on v2

--- a/solution.py
+++ b/solution.py
@@ -48,13 +48,23 @@
     return pl.BlockSpec(memory_space=pltpu.VMEM)
 
 
-def place_features(at, refs, dst, rows=None):
-    z, core = at[2], at[3]
+def feature_offset(z, core, i):
+    zz = lax.rem(z + (0, 3, 1, 2)[i % 4], 4)
+    cc = core if i < 4 else 1 - core
+    return pl.multiple_of((zz * 2 + cc) * 128, 128)
+
+
+def place_features(at, refs, dst):
     for i, ref in enumerate(refs):
-        zz = lax.rem(z + (0, 3, 1, 2)[i % 4], 4)
-        cc = core if i < 4 else 1 - core
-        off = pl.multiple_of((zz * 2 + cc) * 128, 128)
-        dst[:, pl.ds(off, 128)] = ref[...]
+        dst[:, pl.ds(feature_offset(at[2], at[3], i), 128)] = ref[...]
+
+
+def spread(src, dst, sems):
+    copies = [pltpu.make_async_copy(src, dst.at[i], sems.at[i]) for i in range(dst.shape[0])]
+    for copy in copies:
+        copy.start()
+    for copy in copies:
+        copy.wait()
 
 
 def pack(at, env, low, p0, p1, p2, p3):
@@ -66,15 +76,32 @@
             out[(i + 2) * n : (i + 3) * n, :] = low[src, :]
 
 
-def kernel_slices(at, qt, s0, s1, s2, s3, s4, s5, s6, s7, k0, k1, low, feats):
-    place_features(at, (s0, s1, s2, s3, s4, s5, s6, s7), feats)
-    n = k0.shape[0]
-    low[...] = feats[2 * n :, :]
-    scale = 1.0 / (qt.shape[0] ** 0.5)
-    dots = jnp.dot(feats[: 2 * n, :], qt[...], preferred_element_type=F32) * scale
-    k = dots * dots
-    k0[...] = k[:n].astype(BF16)
-    k1[...] = k[n:]
+def assemble(at, p0, p1, p2, p3, p4, p5, p6, p7, feats, low):
+    n = low.shape[0]
+    for i, ref in enumerate((p0, p1, p2, p3, p4, p5, p6, p7)):
+        cols = pl.ds(feature_offset(at[2], at[3], i), 128)
+        feats[:, cols] = ref[: 2 * n, :]
+        low[:, cols] = ref[2 * n :, :]
+
+
+def through_first(low, inv, high, rest):
+    both = jnp.dot(low[...], inv[...], preferred_element_type=F32)
+    high[...] = both.astype(BF16)
+    rest[...] = (both - high[...].astype(F32)).astype(BF16)
+
+
+def square(feats, qt, total):
+    dots = jnp.dot(feats, qt, preferred_element_type=F32) * (1.0 / (total**0.5))
+    return dots * dots
+
+
+def kernel_slices(feats, qa, qb, k0, k1):
+    n, half = k0.shape[0], qa.shape[1]
+    for i, q in enumerate((qa, qb)):
+        cols = slice(i * half, (i + 1) * half)
+        k = square(feats[...], q[...], qa.shape[0])
+        k0[:, cols] = k[:n].astype(BF16)
+        k1[:, cols] = k[n:]
 
 
 def place_rows(at, refs, dst):
@@ -84,17 +111,22 @@
         dst[pl.ds(off, ref.shape[0]), :] = ref[...]
 
 
-def first_solve(at, a, b, c, d, inv, low, k1, s0, t, rhs):
+def right_side(at, a, b, c, d, high, rest, k1, t, rhs):
     place_rows(at, (a, b, c, d), rhs)
+    low = jnp.dot(high[...], rhs[...], preferred_element_type=F32)
+    low = low + jnp.dot(rest[...], rhs[...], preferred_element_type=F32)
+    t[...] = (k1[...] - low).astype(BF16)
+
+
+def first_solve(rhs, inv, s0):
     s0[...] = jnp.dot(inv[...], rhs[...], preferred_element_type=F32).astype(BF16)
-    t[...] = (k1[...] - jnp.dot(low[...], s0[...], preferred_element_type=F32)).astype(BF16)
-
-
-def kernel_rows(at, qt, p0, p1, p2, p3, p4, p5, p6, p7, out, feats):
+
+
+def kernel_rows(at, qa, qb, p0, p1, p2, p3, p4, p5, p6, p7, out, feats):
     place_features(at, (p0, p1, p2, p3, p4, p5, p6, p7), feats)
-    scale = 1.0 / (qt.shape[0] ** 0.5)
-    dots = jnp.dot(feats[...], qt[...], preferred_element_type=F32) * scale
-    out[...] = dots * dots
+    half = qa.shape[1]
+    for i, q in enumerate((qa, qb)):
+        out[:, i * half : (i + 1) * half] = square(feats[...], q[...], qa.shape[0])
 
 
 def update(s0, low, k, out):
@@ -140,10 +172,6 @@
     quarter = width // 4
     piece = sparse_desc.shape[2]
     feats = piece * 2 * N
-
-    qt = query_desc.T
-    spread = jnp.broadcast_to(qt[None], (N * N,) + qt.shape)
-    qt = lax.all_to_all(spread, "rows", 0, 0, tiled=True).reshape(feats, queries)
 
     got = pl.pallas_call(
         pack,
@@ -157,8 +185,31 @@
             out_specs=[pl.BlockSpec((width, piece), lambda i, at: (0, 0))] * 4,
         ),
         out_shape=[jax.ShapeDtypeStruct((width, piece), BF16)] * 4,
-        compiler_params=params(16),
-    )(after(at, spread), sparse_desc, lower_panel)
+        compiler_params=params(56),
+    )(at, sparse_desc, lower_panel)
+
+    own_q = query_desc.T
+    half = queries // 2
+
+    def gather_queries(part, source):
+        block = pl.BlockSpec((own_q.shape[0], half), lambda i: (0, part))
+        copies = pl.pallas_call(
+            spread,
+            grid=(1,),
+            in_specs=[block],
+            out_specs=pl.BlockSpec(memory_space=pl.ANY),
+            out_shape=jax.ShapeDtypeStruct((N * N, own_q.shape[0], half), BF16),
+            scratch_shapes=[pltpu.SemaphoreType.DMA((N * N,))],
+            compiler_params=params(56),
+        )(source)
+        return lax.all_to_all(copies, "rows", 0, 0, tiled=True).reshape(feats, half)
+
+    qa = gather_queries(0, after(own_q, got[0]))
+
+    own = sparse_desc.reshape(blocks * width, piece)
+    envs = [own] + [lax.ppermute(own, "pb", z_perm(d)) for d in (1, -1, 2)]
+    envs = envs + [lax.ppermute(v, "pb", SWAP) for v in envs]
+
     got = [got[0]] + [
         lax.ppermute(got[d], "rows", [(0, d), (1, (1 + d) % N)]) for d in (1, 2, 3)
     ]
@@ -167,33 +218,49 @@
     n = quarter
     even = jnp.concatenate([from0[:n], from1[:n], from1[2 * n : 3 * n]])
     odd = jnp.concatenate([from0[n : 2 * n], from1[n : 2 * n], from1[3 * n :]])
+    qb = gather_queries(1, after(own_q, even))
     got_y = [even] + [
         lax.ppermute(even if d == 2 else odd, "rows", [(c, d * N + c) for c in range(N)])
         for d in (1, 2, 3)
     ]
     mine = pick(y, got_y)
+    mine, _, _, _ = lax.optimization_barrier((mine, envs[1], envs[2], envs[3]))
     slices = [mine] + [lax.ppermute(mine, "pb", z_perm(d)) for d in (1, -1, 2)]
     slices = slices + [lax.ppermute(v, "pb", SWAP) for v in slices]
 
-    own = sparse_desc.reshape(blocks * width, piece)
-    envs = [own] + [lax.ppermute(own, "pb", z_perm(d)) for d in (1, -1)]
-    envs = envs + [lax.ppermute(after(own, envs[1]), "pb", z_perm(2))]
-    envs = envs + [lax.ppermute(v, "pb", SWAP) for v in envs]
-
     unit = 2 * width * feats * queries
-    k0, k1, low = pl.pallas_call(
+    def block(i):
+        return pl.BlockSpec((None, width, width), lambda *_: (i, 0, 0))
+
+    narrow = jax.ShapeDtypeStruct((quarter, width), BF16)
+    slice_feats, low = pl.pallas_call(
+        assemble,
+        out_shape=(jax.ShapeDtypeStruct((2 * quarter, feats), BF16), narrow),
+        in_specs=[smem] + [whole()] * 8,
+        out_specs=(whole(),) * 2,
+        compiler_params=params(16),
+    )(at, *slices)
+    k0, k1 = pl.pallas_call(
         kernel_slices,
         out_shape=(
             jax.ShapeDtypeStruct((quarter, queries), BF16),
             jax.ShapeDtypeStruct((quarter, queries), F32),
-            jax.ShapeDtypeStruct((quarter, width), BF16),
         ),
-        in_specs=[smem] + [whole()] * 9,
-        out_specs=(whole(),) * 3,
-        scratch_shapes=[pltpu.VMEM((3 * quarter, feats), BF16)],
+        in_specs=[whole()] * 3,
+        out_specs=(whole(), whole()),
         compiler_params=params(16),
         cost_estimate=cost(unit / 2, 5e6),
-    )(at, qt, *slices)
+    )(slice_feats, qa, qb)
+
+    high, rest = pl.pallas_call(
+        through_first,
+        grid=(1,),
+        out_shape=(narrow, narrow),
+        in_specs=[whole(), block(0)],
+        out_specs=(whole(),) * 2,
+        compiler_params=params(16),
+        cost_estimate=cost(unit / 4, 5e6),
+    )(after(low, k0), diag_inv)
 
     def neighbours(v):
         return (
@@ -203,20 +270,26 @@
             lax.ppermute(v, "rows", y_perm(-1)),
         )
 
-    block = pl.BlockSpec((None, width, width), lambda *_: (0, 0, 0), memory_space=pltpu.VMEM)
-    s0, t = pl.pallas_call(
+    t, rhs = pl.pallas_call(
+        right_side,
+        out_shape=(
+            jax.ShapeDtypeStruct((quarter, queries), BF16),
+            jax.ShapeDtypeStruct((width, queries), BF16),
+        ),
+        in_specs=[smem] + [whole()] * 7,
+        out_specs=(whole(),) * 2,
+        compiler_params=params(20),
+        cost_estimate=cost(unit * 0.5, 8e6),
+    )(at, *neighbours(k0), high, rest, k1)
+    s0 = pl.pallas_call(
         first_solve,
         grid=(1,),
-        out_shape=(
-            jax.ShapeDtypeStruct((width, queries), BF16),
-            jax.ShapeDtypeStruct((quarter, queries), BF16),
-        ),
-        in_specs=[smem] + [whole()] * 4 + [block] + [whole()] * 2,
-        out_specs=(whole(), whole()),
-        scratch_shapes=[pltpu.VMEM((width, queries), BF16)],
+        out_shape=jax.ShapeDtypeStruct((width, queries), BF16),
+        in_specs=[whole(), block(0)],
+        out_specs=whole(),
         compiler_params=params(20),
-        cost_estimate=cost(unit * 1.25, 8e6),
-    )(at, *neighbours(k0), diag_inv, low, k1)
+        cost_estimate=cost(unit, 6e6),
+    )(rhs, diag_inv)
 
     bm = BM
     rows = blocks * width
@@ -225,12 +298,12 @@
         kernel_rows,
         grid=(rows // bm,),
         out_shape=jax.ShapeDtypeStruct((rows, queries), F32),
-        in_specs=[smem, whole()] + [pl.BlockSpec((bm, piece), lambda i: (i, 0))] * 8,
+        in_specs=[smem, whole(), whole()] + [pl.BlockSpec((bm, piece), lambda i: (i, 0))] * 8,
         out_specs=pl.BlockSpec((bm, queries), lambda i: (i, 0)),
         scratch_shapes=[pltpu.VMEM((bm, feats), BF16)],
         compiler_params=params(16),
         cost_estimate=cost(unit * 2, 14e6),
-    )(at, qt, *envs)
+    )(at, qa, qb, *envs)
     res = pl.pallas_call(
         update,
         grid=(rows // bm,),
@@ -245,7 +318,6 @@
         cost_estimate=cost(unit * 2, 22e6),
     )(s0, panel, k_rows)
 
-    block1 = pl.BlockSpec((None, width, width), lambda *_: (1, 0, 0), memory_space=pltpu.VMEM)
     out = pl.pallas_call(
         last_step,
         grid=(rows // bm,),
@@ -253,7 +325,7 @@
         in_specs=[smem]
         + [whole()] * 4
         + [
-            block1,
+            block(1),
             whole(),
             pl.BlockSpec((bm, width), lambda i: (i, 1)),
             pl.BlockSpec((bm, queries), lambda i: (i, 0)),

time: 147 us -> 115 us (0.78)
  waiting for transfers between devices: 57.2 us -> 29.1 us
  local copies, waits for them, and re-layouts: 20 us -> 4.43 us
  Pallas kernels: 29.5 us -> 37.1 us
  starting transfers between devices: 36.4 us -> 42.1 us
    ppermute x3, waiting for transfers between devices: 30.8 us -> 7.66 us  [per_device(): lax.ppermute(got[d], 'rows', [(0, d), (1, (1 + d) % N)])]
    unnamed x42 -> x16, local copies, waits for them, and re-layouts: 17.5 us -> 4.4 us
    ppermute x2, waiting for transfers between devices: 11.5 us -> 2.17 us  [neighbours(): lax.ppermute(v, 'rows', x_perm(-1))]
    all_to_all x1 -> x2, starting transfers between devices: 7.42 us -> 15.2 us  [gather_queries(): return lax.all_to_all(copies, 'rows', 0, 0, tiled=True).reshape(feats, half)]
    ppermute x3, waiting for transfers between devices: 13.3 us -> 6.59 us  [per_device(): slices = [mine] + [lax.ppermute(mine, 'pb', z_perm(d)) for d in (1, -1, 2)]]
    ppermute x3, waiting for transfers between devices: 0.01 us -> 6.6 us  [per_device(): envs = [own] + [lax.ppermute(own, 'pb', z_perm(d)) for d in (1, -1, 2)]]
    pallas_call x1 -> x6, Pallas kernels: 3.55 us -> 10 us  [the longest x2 3.92 us: gather_queries(): pl.pallas_call(spread, grid=(1,), in_specs=[block], out_specs=pl.BlockSpe...]
    ppermute x2, starting transfers between devices: 1.68 us -> 5.3 us  [neighbours(): lax.ppermute(v, 'rows', x_perm(-1))]
  transfers between devices with their start and end apart: 27 -> 28, of which waited for: 7 -> 13; matrix products, arithmetic and copies ran while one was open for 2% -> 1% of each run, Pallas kernels for 14% -> 20%
where the time goes in v4:
time: 115 us
  starting transfers between devices  42.1 us (37%)
  Pallas kernels  37.1 us (32%)
  waiting for transfers between devices  29.1 us (25%)
  local copies, waits for them, and re-layouts  4.43 us (4%)
  other arithmetic  1.82 us (2%)
    all_to_all x2, starting transfers between devices, gather_queries(): return lax.all_to_all(copies, 'rows', 0, 0, tiled=True).reshape(feats, half)  15.2 us
    pallas_call x1, Pallas kernels, per_device(): pl.pallas_call(last_step, grid=(rows // bm,), out_shape=jax.ShapeDtypeStr...  9.46 us
    pallas_call x1, Pallas kernels, per_device(): pl.pallas_call(kernel_rows, grid=(rows // bm,), out_shape=jax.ShapeDtypeS...  8.11 us
    ppermute x3, waiting for transfers between devices, per_device(): lax.ppermute(got[d], 'rows', [(0, d), (1, (1 + d) % N)])  7.66 us
    ppermute x3, waiting for transfers between devices, per_device(): envs = [own] + [lax.ppermute(own, 'pb', z_perm(d)) for d in (1, -1, 2)]  6.6 us
    ppermute x3, waiting for transfers between devices, per_device(): slices = [mine] + [lax.ppermute(mine, 'pb', z_perm(d)) for d in (1, -1, 2)]  6.59 us
    ppermute x3, starting transfers between devices, per_device(): envs = [own] + [lax.ppermute(own, 'pb', z_perm(d)) for d in (1, -1, 2)]  5.97 us
    pallas_call x1, Pallas kernels, per_device(): pl.pallas_call(update, grid=(rows // bm,), out_shape=jax.ShapeDtypeStruct...  5.44 us
  transfers between devices with their start and end apart: 28, of which 13 were waited for; matrix products, arithmetic and copies ran while one was open for 1% of the time, Pallas kernels for 20%

profile of v4, /device:TPU:6, one launch (start us, length us, event | category | flops | bytes accessed | tf_op | source)
XLA Modules:
  0.0 114.8 jit_solution(9960570433772084370)
XLA Ops:
  0.6 2.8 %shard_map.46 = (bf16[1024,128]{1,0:T(8,128)(2,1)}, bf16[1024,128]{1,0:T(8,128)(2,1)}, bf16[1024,128]{1,0:T(8,128)(2,1)}, bf16[1024,128]{1,0:T(8,128)(2,1)}) custom-call(s32[4]{0:T(128)} %pad_add_fusion.at, bf16[2,1024,128]{2,1,0:T(8,128)(2,1)} %env.1, bf16[2,1024,2048]{2,1,0:T(8,128)(2,1)} %low.1), custom_call_target="tpu_custom_call" | custom-call | tf_op jit(solution)/shard_map/pallas_call | solution.py:176
  3.4 1.4 %collective-permute-start = (bf16[1024,128]{1,0:T(8,128)(2,1)}, bf16[1024,128]{1,0:T(8,128)(2,1)S(1)}, u32[]{:S(2)}, u32[]{:S(2)}) collective-permute-start(bf16[1024,128]{1,0:T(8,128)(2,1)} %get-tuple-element.21), channel_id=1, source_target_pairs={{0,24},{8,0},{1,25},{9,1},{2,26},{10,2},{3,27},{11,3},{4,28},{12,4... | collective-permute-start | bytes 786440 | tf_op jit(solution)/shard_map/ppermute | solution.py:214
  6.8 1.9 %shard_map.48 = bf16[16,64,512]{2,1,0:T(8,128)(2,1)} custom-call(bf16[64,1024]{1,0:T(8,128)(2,1)} %bitcast.23), custom_call_target="tpu_custom_call" | custom-call | tf_op jit(solution)/shard_map/pallas_call | solution.py:196
  8.7 9.4 %all-to-all-start = ((bf16[16,64,512]{2,1,0:T(8,128)(2,1)}), bf16[16,64,512]{2,1,0:T(8,128)(2,1)S(1)}, u32[]{:S(2)}, u32[]{:S(2)}) async-start(bf16[16,64,512]{2,1,0:T(8,128)(2,1)} %shard_map.48), calls=%async_computation | async-start | bytes 2097152 | tf_op jit(solution)/shard_map/all_to_all | solution.py:205
  18.2 7.7 %collective-permute-done = bf16[1024,128]{1,0:T(8,128)(2,1)S(1)} collective-permute-done((bf16[1024,128]{1,0:T(8,128)(2,1)}, bf16[1024,128]{1,0:T(8,128)(2,1)S(1)}, u32[]{:S(2)}, u32[]{:S(2)}) %collective-permute-start) | collective-permute-done | bytes 262176 | tf_op jit(solution)/shard_map/ppermute | solution.py:214
  27.0 1.3 %collective-permute-start.4 = (bf16[768,128]{1,0:T(8,128)(2,1)S(1)}, bf16[768,128]{1,0:T(8,128)(2,1)S(1)}, u32[]{:S(2)}, u32[]{:S(2)}) collective-permute-start(bf16[768,128]{1,0:T(8,128)(2,1)S(1)} %pad_maximum_fusion.1), channel_id=1, source_target_pairs={{0,64},{8,72},{16,80},{24,88},{1,65},{9,73},{17,81},{25,89},{2,66}... | collective-permute-start | bytes 589832 | tf_op jit(solution)/shard_map/ppermute | solution.py:223
  28.3 2.0 %collective-permute-start.6 = (bf16[2048,128]{1,0:T(8,128)(2,1)S(1)}, bf16[2048,128]{1,0:T(8,128)(2,1)}, u32[]{:S(2)}, u32[]{:S(2)}) collective-permute-start(bf16[2048,128]{1,0:T(8,128)(2,1)S(1)} %bitcast.18), channel_id=1, source_target_pairs={{0,2},{1,3},{2,4},{3,5},{4,6},{5,7},{6,0},{7,1},{8,10},{9,11},{10,... | collective-permute-start | bytes 1572872 | tf_op jit(solution)/shard_map/ppermute | solution.py:210
  30.3 2.2 %collective-permute-start.7 = (bf16[2048,128]{1,0:T(8,128)(2,1)S(1)}, bf16[2048,128]{1,0:T(8,128)(2,1)}, u32[]{:S(2)}, u32[]{:S(2)}) collective-permute-start(bf16[2048,128]{1,0:T(8,128)(2,1)S(1)} %bitcast.19), channel_id=1, source_target_pairs={{0,6},{1,7},{2,0},{3,1},{4,2},{5,3},{6,4},{7,5},{8,14},{9,15},{10,... | collective-permute-start | bytes 1572872 | tf_op jit(solution)/shard_map/ppermute | solution.py:210
  32.5 1.8 %collective-permute-start.8 = (bf16[2048,128]{1,0:T(8,128)(2,1)S(1)}, bf16[2048,128]{1,0:T(8,128)(2,1)}, u32[]{:S(2)}, u32[]{:S(2)}) collective-permute-start(bf16[2048,128]{1,0:T(8,128)(2,1)S(1)} %bitcast.20), channel_id=1, source_target_pairs={{0,4},{1,5},{2,6},{3,7},{4,0},{5,1},{6,2},{7,3},{8,12},{9,13},{10,... | collective-permute-start | bytes 1572872 | tf_op jit(solution)/shard_map/ppermute | solution.py:210
  34.3 1.3 %collective-permute-start.3 = (bf16[768,128]{1,0:T(8,128)(2,1)S(1)}, bf16[768,128]{1,0:T(8,128)(2,1)S(1)}, u32[]{:S(2)}, u32[]{:S(2)}) collective-permute-start(bf16[768,128]{1,0:T(8,128)(2,1)S(1)} %pad_maximum_fusion), channel_id=1, source_target_pairs={{0,96},{8,104},{16,112},{24,120},{1,97},{9,105},{17,113},{25,121},... | collective-permute-start | bytes 589832 | tf_op jit(solution)/shard_map/ppermute | solution.py:223
  35.6 2.0 %collective-permute-start.5 = (bf16[768,128]{1,0:T(8,128)(2,1)S(1)}, bf16[768,128]{1,0:T(8,128)(2,1)}, u32[]{:S(2)}, u32[]{:S(2)}) collective-permute-start(bf16[768,128]{1,0:T(8,128)(2,1)S(1)} %pad_maximum_fusion), channel_id=1, source_target_pairs={{0,32},{8,40},{16,48},{24,56},{1,33},{9,41},{17,49},{25,57},{2,34}... | collective-permute-start | bytes 589832 | tf_op jit(solution)/shard_map/ppermute | solution.py:223
  37.6 2.0 %shard_map.49 = bf16[16,64,512]{2,1,0:T(8,128)(2,1)} custom-call(bf16[64,1024]{1,0:T(8,128)(2,1)} %bitcast.24), custom_call_target="tpu_custom_call" | custom-call | tf_op jit(solution)/shard_map/pallas_call | solution.py:196
  39.6 5.7 %all-to-all-start.1 = ((bf16[16,64,512]{2,1,0:T(8,128)(2,1)}), bf16[16,64,512]{2,1,0:T(8,128)(2,1)S(1)}, u32[]{:S(2)}, u32[]{:S(2)}) async-start(bf16[16,64,512]{2,1,0:T(8,128)(2,1)} %shard_map.49), calls=%async_computation.1 | async-start | bytes 2097152 | tf_op jit(solution)/shard_map/all_to_all | solution.py:205
  45.5 4.5 %collective-permute-done.7.p2 = bf16[2048,128]{1,0:T(8,128)(2,1)} collective-permute-done((bf16[2048,128]{1,0:T(8,128)(2,1)S(1)}, bf16[2048,128]{1,0:T(8,128)(2,1)}, u32[]{:S(2)}, u32[]{:S(2)}) %collective-permute-start.7) | collective-permute-done | bytes 524320 | tf_op jit(solution)/shard_map/ppermute | solution.py:210
  50.0 2.1 %collective-permute-done.8.p3 = bf16[2048,128]{1,0:T(8,128)(2,1)} collective-permute-done((bf16[2048,128]{1,0:T(8,128)(2,1)S(1)}, bf16[2048,128]{1,0:T(8,128)(2,1)}, u32[]{:S(2)}, u32[]{:S(2)}) %collective-permute-start.8) | collective-permute-done | bytes 524320 | tf_op jit(solution)/shard_map/ppermute | solution.py:210
  53.3 2.0 %collective-permute-start.10 = (bf16[768,128]{1,0:T(8,128)(2,1)S(1)}, bf16[768,128]{1,0:T(8,128)(2,1)S(1)}, u32[]{:S(2)}, u32[]{:S(2)}) collective-permute-start(bf16[768,128]{1,0:T(8,128)(2,1)S(1)} %select_select_fusion.2.p0), channel_id=1, source_target_pairs={{0,6},{1,7},{2,0},{3,1},{4,2},{5,3},{6,4},{7,5},{8,14},{9,15},{10,... | collective-permute-start | bytes 589832 | tf_op jit(solution)/shard_map/ppermute | solution.py:228
  55.4 3.6 %collective-permute-done.9.p1 = bf16[768,128]{1,0:T(8,128)(2,1)S(1)} collective-permute-done((bf16[768,128]{1,0:T(8,128)(2,1)S(1)}, bf16[768,128]{1,0:T(8,128)(2,1)S(1)}, u32[]{:S(2)}, u32[]{:S(2)}) %collective-permute-start.9) | collective-permute-done | bytes 196640 | tf_op jit(solution)/shard_map/ppermute | solution.py:228
  60.7 1.8 %collective-permute-done.11.p3 = bf16[768,128]{1,0:T(8,128)(2,1)S(1)} collective-permute-done((bf16[768,128]{1,0:T(8,128)(2,1)S(1)}, bf16[768,128]{1,0:T(8,128)(2,1)S(1)}, u32[]{:S(2)}, u32[]{:S(2)}) %collective-permute-start.11) | collective-permute-done | bytes 196640 | tf_op jit(solution)/shard_map/ppermute | solution.py:228
  64.3 1.4 %collective-permute-done.15.p7 = bf16[768,128]{1,0:T(8,128)(2,1)S(1)} collective-permute-done((bf16[768,128]{1,0:T(8,128)(2,1)S(1)}, bf16[768,128]{1,0:T(8,128)(2,1)S(1)}, u32[]{:S(2)}, u32[]{:S(2)}) %collective-permute-start.15) | collective-permute-done | bytes 196640 | tf_op jit(solution)/shard_map/ppermute | solution.py:229
  70.2 3.6 %collective-permute-start.16 = (bf16[256,1024]{1,0:T(8,128)(2,1)S(1)}, bf16[256,1024]{1,0:T(8,128)(2,1)S(1)}, u32[]{:S(2)}, u32[]{:S(2)}) collective-permute-start(bf16[256,1024]{1,0:T(8,128)(2,1)S(1)} %get-tuple-element.29.a), channel_id=1, source_target_pairs={{0,24},{8,0},{16,8},{24,16},{32,56},{40,32},{48,40},{56,48},{64,88... | collective-permute-start | bytes 1572872 | tf_op jit(solution)/shard_map/ppermute | solution.py:268
  73.9 2.2 %copy-done = bf16[2,1024,1024]{2,1,0:T(8,128)(2,1)S(1)} copy-done((bf16[2,1024,1024]{2,1,0:T(8,128)(2,1)S(1)}, bf16[2,1024,1024]{2,1,0:T(8,128)(2,1)}, u32[]{:S(2)}) %copy-start) | copy-done | bytes 4194328
  76.8 8.1 %shard_map.54.k = f32[2048,1024]{1,0:T(8,128)S(1)} custom-call(s32[4]{0:T(128)S(1)} %copy-done.3, bf16[1024,512]{1,0:T(8,128)(2,1)S(1)} %bitcast.15, bf16[1024,512]{1,0:T(8,128)(2,1)S(1)} %bitcast.17, bf16[2048,128]{1,0:T(8,128)(2,1)S(1)} %bitcast.22, bf16[2048,128]{1,0:T(8,128)(2,1)} %collective-permute-done.6.p1, ...), custom_call_target="tpu_custom_call" | custom-call | flops 4294967296 | bytes 14000000 | tf_op jit(solution)/shard_map/pallas_call | solution.py:297
  85.5 2.0 %collective-permute-done.17.c = bf16[256,1024]{1,0:T(8,128)(2,1)S(1)} collective-permute-done((bf16[256,1024]{1,0:T(8,128)(2,1)S(1)}, bf16[256,1024]{1,0:T(8,128)(2,1)S(1)}, u32[]{:S(2)}, u32[]{:S(2)}) %collective-permute-start.17) | collective-permute-done | bytes 524320 | tf_op jit(solution)/shard_map/ppermute | solution.py:269
  87.6 2.0 %shard_map.52 = (bf16[256,1024]{1,0:T(8,128)(2,1)S(1)}, bf16[1024,1024]{1,0:T(8,128)(2,1)S(1)}) custom-call(s32[4]{0:T(128)S(1)} %copy-done.3, bf16[256,1024]{1,0:T(8,128)(2,1)S(1)} %get-tuple-element.29.a, bf16[256,1024]{1,0:T(8,128)(2,1)S(1)} %collective-permute-done.16.b, bf16[256,1024]{1,0:T(8,128)(2,1)S(1)} %collective-permute-done.17.c, ...), custom_call_target="tpu_custom_call" | custom-call | flops 1073741824 | bytes 8000000 | tf_op jit(solution)/shard_map/pallas_call | solution.py:273
  89.7 1.7 %collective-permute-start.19 = (bf16[256,1024]{1,0:T(8,128)(2,1)S(1)}, bf16[256,1024]{1,0:T(8,128)(2,1)S(1)}, u32[]{:S(2)}, u32[]{:S(2)}) collective-permute-start(bf16[256,1024]{1,0:T(8,128)(2,1)S(1)} %get-tuple-element.35.a), channel_id=1, source_target_pairs={{0,24},{8,0},{16,8},{24,16},{32,56},{40,32},{48,40},{56,48},{64,88... | collective-permute-start | bytes 1572872 | tf_op jit(solution)/shard_map/ppermute | solution.py:268
  91.4 1.6 %collective-permute-start.20 = (bf16[256,1024]{1,0:T(8,128)(2,1)S(1)}, bf16[256,1024]{1,0:T(8,128)(2,1)S(1)}, u32[]{:S(2)}, u32[]{:S(2)}) collective-permute-start(bf16[256,1024]{1,0:T(8,128)(2,1)S(1)} %get-tuple-element.35.a), channel_id=1, source_target_pairs={{0,8},{8,16},{16,24},{24,0},{32,40},{40,48},{48,56},{56,32},{64,72... | collective-permute-start | bytes 1572872 | tf_op jit(solution)/shard_map/ppermute | solution.py:269
  93.0 1.5 %collective-permute-start.21 = (bf16[256,1024]{1,0:T(8,128)(2,1)S(1)}, bf16[256,1024]{1,0:T(8,128)(2,1)S(1)}, u32[]{:S(2)}, u32[]{:S(2)}) collective-permute-start(bf16[256,1024]{1,0:T(8,128)(2,1)S(1)} %get-tuple-element.35.a), channel_id=1, source_target_pairs={{0,96},{8,104},{16,112},{24,120},{32,0},{40,8},{48,16},{56,24},{64... | collective-permute-start | bytes 1572872 | tf_op jit(solution)/shard_map/ppermute | solution.py:270
  94.5 2.3 %shard_map.53.s0 = bf16[1024,1024]{1,0:T(8,128)(2,1)S(1)} custom-call(bf16[1024,1024]{1,0:T(8,128)(2,1)S(1)} %get-tuple-element.36.rhs, bf16[2,1024,1024]{2,1,0:T(8,128)(2,1)S(1)} %copy-done.1), custom_call_target="tpu_custom_call" | custom-call | flops 2147483648 | bytes 6000000 | tf_op jit(solution)/shard_map/pallas_call | solution.py:284
  96.8 5.4 %shard_map.55.res = f32[2048,1024]{1,0:T(8,128)S(1)} custom-call(bf16[1024,1024]{1,0:T(8,128)(2,1)S(1)} %shard_map.53.s0, bf16[2048,2048]{1,0:T(8,128)(2,1)S(1)} %bitcast.12, f32[2048,1024]{1,0:T(8,128)S(1)} %shard_map.54.k), custom_call_target="tpu_custom_call" | custom-call | flops 4294967296 | bytes 22000000 | tf_op jit(solution)/shard_map/pallas_call | solution.py:307
  102.3 1.6 %collective-permute-done.19.b = bf16[256,1024]{1,0:T(8,128)(2,1)S(1)} collective-permute-done((bf16[256,1024]{1,0:T(8,128)(2,1)S(1)}, bf16[256,1024]{1,0:T(8,128)(2,1)S(1)}, u32[]{:S(2)}, u32[]{:S(2)}) %collective-permute-start.19) | collective-permute-done | bytes 524320 | tf_op jit(solution)/shard_map/ppermute | solution.py:268
  103.9 1.5 %collective-permute-done.21.d = bf16[256,1024]{1,0:T(8,128)(2,1)S(1)} collective-permute-done((bf16[256,1024]{1,0:T(8,128)(2,1)S(1)}, bf16[256,1024]{1,0:T(8,128)(2,1)S(1)}, u32[]{:S(2)}, u32[]{:S(2)}) %collective-permute-start.21) | collective-permute-done | bytes 524320 | tf_op jit(solution)/shard_map/ppermute | solution.py:270
  105.3 9.5 %shard_map.56 = bf16[2048,1024]{1,0:T(8,128)(2,1)} custom-call(s32[4]{0:T(128)S(1)} %copy-done.3, bf16[256,1024]{1,0:T(8,128)(2,1)S(1)} %get-tuple-element.35.a, bf16[256,1024]{1,0:T(8,128)(2,1)S(1)} %collective-permute-done.19.b, bf16[256,1024]{1,0:T(8,128)(2,1)S(1)} %collective-permute-done.20.c, bf16[256,1024]{1,0:T(8,128)(2,1)S(1)} %collective-permute-done.21.d, ...), custom_call_target="tpu_custom_call" | custom-call | flops 6442450944 | bytes 20000000 | tf_op jit(solution)/shard_map/pallas_call | solution.py:321
  (58 shorter events, 14.6 us)
Async XLA Ops:
  3.4 24.9 %copy-start.2 = (bf16[2,1024,128]{2,1,0:T(8,128)(2,1)S(1)}, bf16[2,1024,128]{2,1,0:T(8,128)(2,1)}, u32[]{:S(2)}) copy-start(bf16[2,1024,128]{2,1,0:T(8,128)(2,1)} %env.1) | copy-start | bytes 1572868
  3.4 22.5 %collective-permute-start = (bf16[1024,128]{1,0:T(8,128)(2,1)}, bf16[1024,128]{1,0:T(8,128)(2,1)S(1)}, u32[]{:S(2)}, u32[]{:S(2)}) collective-permute-start(bf16[1024,128]{1,0:T(8,128)(2,1)} %get-tuple-element.21), channel_id=1, source_target_pairs={{0,24},{8,0},{1,25},{9,1},{2,26},{10,2},{3,27},{11,3},{4,28},{12,4... | collective-permute-start | bytes 786440 | tf_op jit(solution)/shard_map/ppermute | solution.py:214
  4.8 21.0 %collective-permute-start.1 = (bf16[1024,128]{1,0:T(8,128)(2,1)}, bf16[1024,128]{1,0:T(8,128)(2,1)S(1)}, u32[]{:S(2)}, u32[]{:S(2)}) collective-permute-start(bf16[1024,128]{1,0:T(8,128)(2,1)} %get-tuple-element.22), channel_id=1, source_target_pairs={{0,16},{8,24},{1,17},{9,25},{2,18},{10,26},{3,19},{11,27},{4,20},{... | collective-permute-start | bytes 786440 | tf_op jit(solution)/shard_map/ppermute | solution.py:214
  6.1 19.7 %collective-permute-start.2 = (bf16[1024,128]{1,0:T(8,128)(2,1)}, bf16[1024,128]{1,0:T(8,128)(2,1)S(1)}, u32[]{:S(2)}, u32[]{:S(2)}) collective-permute-start(bf16[1024,128]{1,0:T(8,128)(2,1)} %get-tuple-element.23), channel_id=1, source_target_pairs={{0,8},{8,16},{1,9},{9,17},{2,10},{10,18},{3,11},{11,19},{4,12},{12... | collective-permute-start | bytes 786440 | tf_op jit(solution)/shard_map/ppermute | solution.py:214
  8.7 30.8 %all-to-all-start = ((bf16[16,64,512]{2,1,0:T(8,128)(2,1)}), bf16[16,64,512]{2,1,0:T(8,128)(2,1)S(1)}, u32[]{:S(2)}, u32[]{:S(2)}) async-start(bf16[16,64,512]{2,1,0:T(8,128)(2,1)} %shard_map.48), calls=%async_computation | async-start | bytes 2097152 | tf_op jit(solution)/shard_map/all_to_all | solution.py:205
  18.2 47.6 %copy-start.3 = (s32[4]{0:T(128)S(1)}, s32[4]{0:T(128)}, u32[]{:S(2)}) copy-start(s32[4]{0:T(128)} %pad_add_fusion.at) | copy-start | bytes 52
  27.0 8.6 %collective-permute-start.4 = (bf16[768,128]{1,0:T(8,128)(2,1)S(1)}, bf16[768,128]{1,0:T(8,128)(2,1)S(1)}, u32[]{:S(2)}, u32[]{:S(2)}) collective-permute-start(bf16[768,128]{1,0:T(8,128)(2,1)S(1)} %pad_maximum_fusion.1), channel_id=1, source_target_pairs={{0,64},{8,72},{16,80},{24,88},{1,65},{9,73},{17,81},{25,89},{2,66}... | collective-permute-start | bytes 589832 | tf_op jit(solution)/shard_map/ppermute | solution.py:223
  28.3 17.2 %collective-permute-start.6 = (bf16[2048,128]{1,0:T(8,128)(2,1)S(1)}, bf16[2048,128]{1,0:T(8,128)(2,1)}, u32[]{:S(2)}, u32[]{:S(2)}) collective-permute-start(bf16[2048,128]{1,0:T(8,128)(2,1)S(1)} %bitcast.18), channel_id=1, source_target_pairs={{0,2},{1,3},{2,4},{3,5},{4,6},{5,7},{6,0},{7,1},{8,10},{9,11},{10,... | collective-permute-start | bytes 1572872 | tf_op jit(solution)/shard_map/ppermute | solution.py:210
  30.3 19.7 %collective-permute-start.7 = (bf16[2048,128]{1,0:T(8,128)(2,1)S(1)}, bf16[2048,128]{1,0:T(8,128)(2,1)}, u32[]{:S(2)}, u32[]{:S(2)}) collective-permute-start(bf16[2048,128]{1,0:T(8,128)(2,1)S(1)} %bitcast.19), channel_id=1, source_target_pairs={{0,6},{1,7},{2,0},{3,1},{4,2},{5,3},{6,4},{7,5},{8,14},{9,15},{10,... | collective-permute-start | bytes 1572872 | tf_op jit(solution)/shard_map/ppermute | solution.py:210
  32.5 19.6 %collective-permute-start.8 = (bf16[2048,128]{1,0:T(8,128)(2,1)S(1)}, bf16[2048,128]{1,0:T(8,128)(2,1)}, u32[]{:S(2)}, u32[]{:S(2)}) collective-permute-start(bf16[2048,128]{1,0:T(8,128)(2,1)S(1)} %bitcast.20), channel_id=1, source_target_pairs={{0,4},{1,5},{2,6},{3,7},{4,0},{5,1},{6,2},{7,3},{8,12},{9,13},{10,... | collective-permute-start | bytes 1572872 | tf_op jit(solution)/shard_map/ppermute | solution.py:210
  34.3 11.0 %collective-permute-start.3 = (bf16[768,128]{1,0:T(8,128)(2,1)S(1)}, bf16[768,128]{1,0:T(8,128)(2,1)S(1)}, u32[]{:S(2)}, u32[]{:S(2)}) collective-permute-start(bf16[768,128]{1,0:T(8,128)(2,1)S(1)} %pad_maximum_fusion), channel_id=1, source_target_pairs={{0,96},{8,104},{16,112},{24,120},{1,97},{9,105},{17,113},{25,121},... | collective-permute-start | bytes 589832 | tf_op jit(solution)/shard_map/ppermute | solution.py:223
  35.6 9.7 %collective-permute-start.5 = (bf16[768,128]{1,0:T(8,128)(2,1)S(1)}, bf16[768,128]{1,0:T(8,128)(2,1)}, u32[]{:S(2)}, u32[]{:S(2)}) collective-permute-start(bf16[768,128]{1,0:T(8,128)(2,1)S(1)} %pad_maximum_fusion), channel_id=1, source_target_pairs={{0,32},{8,40},{16,48},{24,56},{1,33},{9,41},{17,49},{25,57},{2,34}... | collective-permute-start | bytes 589832 | tf_op jit(solution)/shard_map/ppermute | solution.py:223
  39.6 28.1 %all-to-all-start.1 = ((bf16[16,64,512]{2,1,0:T(8,128)(2,1)}), bf16[16,64,512]{2,1,0:T(8,128)(2,1)S(1)}, u32[]{:S(2)}, u32[]{:S(2)}) async-start(bf16[16,64,512]{2,1,0:T(8,128)(2,1)} %shard_map.49), calls=%async_computation.1 | async-start | bytes 2097152 | tf_op jit(solution)/shard_map/all_to_all | solution.py:205
  52.1 6.9 %collective-permute-start.9 = (bf16[768,128]{1,0:T(8,128)(2,1)S(1)}, bf16[768,128]{1,0:T(8,128)(2,1)S(1)}, u32[]{:S(2)}, u32[]{:S(2)}) collective-permute-start(bf16[768,128]{1,0:T(8,128)(2,1)S(1)} %select_select_fusion.2.p0), channel_id=1, source_target_pairs={{0,2},{1,3},{2,4},{3,5},{4,6},{5,7},{6,0},{7,1},{8,10},{9,11},{10,... | collective-permute-start | bytes 589832 | tf_op jit(solution)/shard_map/ppermute | solution.py:228
  53.3 7.3 %collective-permute-start.10 = (bf16[768,128]{1,0:T(8,128)(2,1)S(1)}, bf16[768,128]{1,0:T(8,128)(2,1)S(1)}, u32[]{:S(2)}, u32[]{:S(2)}) collective-permute-start(bf16[768,128]{1,0:T(8,128)(2,1)S(1)} %select_select_fusion.2.p0), channel_id=1, source_target_pairs={{0,6},{1,7},{2,0},{3,1},{4,2},{5,3},{6,4},{7,5},{8,14},{9,15},{10,... | collective-permute-start | bytes 589832 | tf_op jit(solution)/shard_map/ppermute | solution.py:228
  55.3 7.2 %collective-permute-start.11 = (bf16[768,128]{1,0:T(8,128)(2,1)S(1)}, bf16[768,128]{1,0:T(8,128)(2,1)S(1)}, u32[]{:S(2)}, u32[]{:S(2)}) collective-permute-start(bf16[768,128]{1,0:T(8,128)(2,1)S(1)} %select_select_fusion.2.p0), channel_id=1, source_target_pairs={{0,4},{1,5},{2,6},{3,7},{4,0},{5,1},{6,2},{7,3},{8,12},{9,13},{10,... | collective-permute-start | bytes 589832 | tf_op jit(solution)/shard_map/ppermute | solution.py:228
  55.4 7.1 %collective-permute-start.12 = (bf16[768,128]{1,0:T(8,128)(2,1)S(1)}, bf16[768,128]{1,0:T(8,128)(2,1)S(1)}, u32[]{:S(2)}, u32[]{:S(2)}) collective-permute-start(bf16[768,128]{1,0:T(8,128)(2,1)S(1)} %select_select_fusion.2.p0), channel_id=1, source_target_pairs={{0,1},{1,0},{2,3},{3,2},{4,5},{5,4},{6,7},{7,6},{8,9},{9,8},{10,11... | collective-permute-start | bytes 589832 | tf_op jit(solution)/shard_map/ppermute | solution.py:229
  59.0 4.0 %collective-permute-start.13 = (bf16[768,128]{1,0:T(8,128)(2,1)S(1)}, bf16[768,128]{1,0:T(8,128)(2,1)S(1)}, u32[]{:S(2)}, u32[]{:S(2)}) collective-permute-start(bf16[768,128]{1,0:T(8,128)(2,1)S(1)} %collective-permute-done.9.p1), channel_id=1, source_target_pairs={{0,1},{1,0},{2,3},{3,2},{4,5},{5,4},{6,7},{7,6},{8,9},{9,8},{10,11... | collective-permute-start | bytes 589832 | tf_op jit(solution)/shard_map/ppermute | solution.py:229
  59.0 14.8 %collective-permute-start.22 = (bf16[2048,128]{1,0:T(8,128)(2,1)S(1)}, bf16[2048,128]{1,0:T(8,128)(2,1)}, u32[]{:S(2)}, u32[]{:S(2)}) collective-permute-start(bf16[2048,128]{1,0:T(8,128)(2,1)S(1)} %bitcast.21), channel_id=1, source_target_pairs={{0,1},{1,0},{2,3},{3,2},{4,5},{5,4},{6,7},{7,6},{8,9},{9,8},{10,11... | collective-permute-start | bytes 1572872 | tf_op jit(solution)/shard_map/ppermute | solution.py:211
  60.6 13.1 %collective-permute-start.23 = (bf16[2048,128]{1,0:T(8,128)(2,1)}, bf16[2048,128]{1,0:T(8,128)(2,1)}, u32[]{:S(2)}, u32[]{:S(2)}) collective-permute-start(bf16[2048,128]{1,0:T(8,128)(2,1)} %collective-permute-done.6.p1), channel_id=1, source_target_pairs={{0,1},{1,0},{2,3},{3,2},{4,5},{5,4},{6,7},{7,6},{8,9},{9,8},{10,11... | collective-permute-start | bytes 1572872 | tf_op jit(solution)/shard_map/ppermute | solution.py:211
  62.5 1.6 %collective-permute-start.14 = (bf16[768,128]{1,0:T(8,128)(2,1)S(1)}, bf16[768,128]{1,0:T(8,128)(2,1)S(1)}, u32[]{:S(2)}, u32[]{:S(2)}) collective-permute-start(bf16[768,128]{1,0:T(8,128)(2,1)S(1)} %collective-permute-done.10.p2), channel_id=1, source_target_pairs={{0,1},{1,0},{2,3},{3,2},{4,5},{5,4},{6,7},{7,6},{8,9},{9,8},{10,11... | collective-permute-start | bytes 589832 | tf_op jit(solution)/shard_map/ppermute | solution.py:229
  62.5 14.3 %collective-permute-start.24 = (bf16[2048,128]{1,0:T(8,128)(2,1)}, bf16[2048,128]{1,0:T(8,128)(2,1)}, u32[]{:S(2)}, u32[]{:S(2)}) collective-permute-start(bf16[2048,128]{1,0:T(8,128)(2,1)} %collective-permute-done.7.p2), channel_id=1, source_target_pairs={{0,1},{1,0},{2,3},{3,2},{4,5},{5,4},{6,7},{7,6},{8,9},{9,8},{10,11... | collective-permute-start | bytes 1572872 | tf_op jit(solution)/shard_map/ppermute | solution.py:211
  63.0 13.8 %collective-permute-start.25 = (bf16[2048,128]{1,0:T(8,128)(2,1)}, bf16[2048,128]{1,0:T(8,128)(2,1)}, u32[]{:S(2)}, u32[]{:S(2)}) collective-permute-start(bf16[2048,128]{1,0:T(8,128)(2,1)} %collective-permute-done.8.p3), channel_id=1, source_target_pairs={{0,1},{1,0},{2,3},{3,2},{4,5},{5,4},{6,7},{7,6},{8,9},{9,8},{10,11... | collective-permute-start | bytes 1572872 | tf_op jit(solution)/shard_map/ppermute | solution.py:211
  64.1 1.6 %collective-permute-start.15 = (bf16[768,128]{1,0:T(8,128)(2,1)S(1)}, bf16[768,128]{1,0:T(8,128)(2,1)S(1)}, u32[]{:S(2)}, u32[]{:S(2)}) collective-permute-start(bf16[768,128]{1,0:T(8,128)(2,1)S(1)} %collective-permute-done.11.p3), channel_id=1, source_target_pairs={{0,1},{1,0},{2,3},{3,2},{4,5},{5,4},{6,7},{7,6},{8,9},{9,8},{10,11... | collective-permute-start | bytes 589832 | tf_op jit(solution)/shard_map/ppermute | solution.py:229
  70.2 15.3 %collective-permute-start.16 = (bf16[256,1024]{1,0:T(8,128)(2,1)S(1)}, bf16[256,1024]{1,0:T(8,128)(2,1)S(1)}, u32[]{:S(2)}, u32[]{:S(2)}) collective-permute-start(bf16[256,1024]{1,0:T(8,128)(2,1)S(1)} %get-tuple-element.29.a), channel_id=1, source_target_pairs={{0,24},{8,0},{16,8},{24,16},{32,56},{40,32},{48,40},{56,48},{64,88... | collective-permute-start | bytes 1572872 | tf_op jit(solution)/shard_map/ppermute | solution.py:268
  73.8 13.8 %collective-permute-start.17 = (bf16[256,1024]{1,0:T(8,128)(2,1)S(1)}, bf16[256,1024]{1,0:T(8,128)(2,1)S(1)}, u32[]{:S(2)}, u32[]{:S(2)}) collective-permute-start(bf16[256,1024]{1,0:T(8,128)(2,1)S(1)} %get-tuple-element.29.a), channel_id=1, source_target_pairs={{0,8},{8,16},{16,24},{24,0},{32,40},{40,48},{48,56},{56,32},{64,72... | collective-permute-start | bytes 1572872 | tf_op jit(solution)/shard_map/ppermute | solution.py:269
  73.8 13.9 %collective-permute-start.18 = (bf16[256,1024]{1,0:T(8,128)(2,1)S(1)}, bf16[256,1024]{1,0:T(8,128)(2,1)S(1)}, u32[]{:S(2)}, u32[]{:S(2)}) collective-permute-start(bf16[256,1024]{1,0:T(8,128)(2,1)S(1)} %get-tuple-element.29.a), channel_id=1, source_target_pairs={{0,96},{8,104},{16,112},{24,120},{32,0},{40,8},{48,16},{56,24},{64... | collective-permute-start | bytes 1572872 | tf_op jit(solution)/shard_map/ppermute | solution.py:270
  76.0 20.8 %slice-start = ((s8[8388608]{0:T(1024)(128)(4,1)}), s8[4194304]{0:T(1024)(128)(4,1)S(1)}, s32[]{:S(2)}) async-start(s8[8388608]{0:T(1024)(128)(4,1)} %bitcast.10), calls=%async_computation.2 | async-start | bytes 8388608
  76.8 20.0 %slice-start.1 = ((s8[8388608]{0:T(1024)(128)(4,1)}), s8[4194304]{0:T(1024)(128)(4,1)S(1)}, s32[]{:S(2)}) async-start(s8[8388608]{0:T(1024)(128)(4,1)} %bitcast.10), calls=%async_computation.3 | async-start | bytes 8388608
  89.7 14.2 %collective-permute-start.19 = (bf16[256,1024]{1,0:T(8,128)(2,1)S(1)}, bf16[256,1024]{1,0:T(8,128)(2,1)S(1)}, u32[]{:S(2)}, u32[]{:S(2)}) collective-permute-start(bf16[256,1024]{1,0:T(8,128)(2,1)S(1)} %get-tuple-element.35.a), channel_id=1, source_target_pairs={{0,24},{8,0},{16,8},{24,16},{32,56},{40,32},{48,40},{56,48},{64,88... | collective-permute-start | bytes 1572872 | tf_op jit(solution)/shard_map/ppermute | solution.py:268
  91.4 12.5 %collective-permute-start.20 = (bf16[256,1024]{1,0:T(8,128)(2,1)S(1)}, bf16[256,1024]{1,0:T(8,128)(2,1)S(1)}, u32[]{:S(2)}, u32[]{:S(2)}) collective-permute-start(bf16[256,1024]{1,0:T(8,128)(2,1)S(1)} %get-tuple-element.35.a), channel_id=1, source_target_pairs={{0,8},{8,16},{16,24},{24,0},{32,40},{40,48},{48,56},{56,32},{64,72... | collective-permute-start | bytes 1572872 | tf_op jit(solution)/shard_map/ppermute | solution.py:269
  93.0 12.4 %collective-permute-start.21 = (bf16[256,1024]{1,0:T(8,128)(2,1)S(1)}, bf16[256,1024]{1,0:T(8,128)(2,1)S(1)}, u32[]{:S(2)}, u32[]{:S(2)}) collective-permute-start(bf16[256,1024]{1,0:T(8,128)(2,1)S(1)} %get-tuple-element.35.a), channel_id=1, source_target_pairs={{0,96},{8,104},{16,112},{24,120},{32,0},{40,8},{48,16},{56,24},{64... | collective-permute-start | bytes 1572872 | tf_op jit(solution)/shard_map/ppermute | solution.py:270
  (4 other events, 13.9 us)

commit v5 on v4

--- a/solution.py
+++ b/solution.py
@@ -1,3 +1,5 @@
+import functools
+
 import jax
 import jax.numpy as jnp
 from jax import lax
@@ -59,8 +61,9 @@
         dst[:, pl.ds(feature_offset(at[2], at[3], i), 128)] = ref[...]
 
 
-def spread(src, dst, sems):
-    copies = [pltpu.make_async_copy(src, dst.at[i], sems.at[i]) for i in range(dst.shape[0])]
+def spread(start, src, dst, sems):
+    part = src.at[:, start : start + dst.shape[2]]
+    copies = [pltpu.make_async_copy(part, dst.at[i], sems.at[i]) for i in range(dst.shape[0])]
     for copy in copies:
         copy.start()
     for copy in copies:
@@ -96,12 +99,13 @@
 
 
 def kernel_slices(feats, qa, qb, k0, k1):
-    n, half = k0.shape[0], qa.shape[1]
-    for i, q in enumerate((qa, qb)):
-        cols = slice(i * half, (i + 1) * half)
-        k = square(feats[...], q[...], qa.shape[0])
+    n, start = k0.shape[0], 0
+    for q in (qa, qb):
+        cols = slice(start, start + q.shape[1])
+        k = square(feats[...], q[...], q.shape[0])
         k0[:, cols] = k[:n].astype(BF16)
         k1[:, cols] = k[n:]
+        start += q.shape[1]
 
 
 def place_rows(at, refs, dst):
@@ -124,9 +128,10 @@
 
 def kernel_rows(at, qa, qb, p0, p1, p2, p3, p4, p5, p6, p7, out, feats):
     place_features(at, (p0, p1, p2, p3, p4, p5, p6, p7), feats)
-    half = qa.shape[1]
-    for i, q in enumerate((qa, qb)):
-        out[:, i * half : (i + 1) * half] = square(feats[...], q[...], qa.shape[0])
+    start = 0
+    for q in (qa, qb):
+        out[:, start : start + q.shape[1]] = square(feats[...], q[...], q.shape[0])
+        start += q.shape[1]
 
 
 def update(s0, low, k, out):
@@ -189,26 +194,24 @@
     )(at, sparse_desc, lower_panel)
 
     own_q = query_desc.T
-    half = queries // 2
-
-    def gather_queries(part, source):
-        block = pl.BlockSpec((own_q.shape[0], half), lambda i: (0, part))
+    first_part = queries // 4
+
+    def gather_queries(start, count, source):
         copies = pl.pallas_call(
-            spread,
-            grid=(1,),
-            in_specs=[block],
+            functools.partial(spread, start),
+            in_specs=[whole()],
             out_specs=pl.BlockSpec(memory_space=pl.ANY),
-            out_shape=jax.ShapeDtypeStruct((N * N, own_q.shape[0], half), BF16),
+            out_shape=jax.ShapeDtypeStruct((N * N, own_q.shape[0], count), BF16),
             scratch_shapes=[pltpu.SemaphoreType.DMA((N * N,))],
             compiler_params=params(56),
         )(source)
-        return lax.all_to_all(copies, "rows", 0, 0, tiled=True).reshape(feats, half)
-
-    qa = gather_queries(0, after(own_q, got[0]))
+        return lax.all_to_all(copies, "rows", 0, 0, tiled=True).reshape(feats, count)
+
+    qa = gather_queries(0, first_part, after(own_q, got[0]))
 
     own = sparse_desc.reshape(blocks * width, piece)
-    envs = [own] + [lax.ppermute(own, "pb", z_perm(d)) for d in (1, -1, 2)]
-    envs = envs + [lax.ppermute(v, "pb", SWAP) for v in envs]
+    early = after(own, got[0])
+    envs = [own] + [lax.ppermute(early, "pb", z_perm(d)) for d in (1, -1)]
 
     got = [got[0]] + [
         lax.ppermute(got[d], "rows", [(0, d), (1, (1 + d) % N)]) for d in (1, 2, 3)
@@ -218,14 +221,15 @@
     n = quarter
     even = jnp.concatenate([from0[:n], from1[:n], from1[2 * n : 3 * n]])
     odd = jnp.concatenate([from0[n : 2 * n], from1[n : 2 * n], from1[3 * n :]])
-    qb = gather_queries(1, after(own_q, even))
+    qb = gather_queries(first_part, queries - first_part, after(own_q, even))
     got_y = [even] + [
         lax.ppermute(even if d == 2 else odd, "rows", [(c, d * N + c) for c in range(N)])
         for d in (1, 2, 3)
     ]
     mine = pick(y, got_y)
-    mine, _, _, _ = lax.optimization_barrier((mine, envs[1], envs[2], envs[3]))
+    mine, _, _ = lax.optimization_barrier((mine, envs[1], envs[2]))
     slices = [mine] + [lax.ppermute(mine, "pb", z_perm(d)) for d in (1, -1, 2)]
+    envs = envs + [lax.ppermute(after(own, slices[1]), "pb", z_perm(2))]
     slices = slices + [lax.ppermute(v, "pb", SWAP) for v in slices]
 
     unit = 2 * width * feats * queries
@@ -239,6 +243,7 @@
         in_specs=[smem] + [whole()] * 8,
         out_specs=(whole(),) * 2,
         compiler_params=params(16),
+        cost_estimate=cost(6900000000, 22200000),
     )(at, *slices)
     k0, k1 = pl.pallas_call(
         kernel_slices,
@@ -260,7 +265,7 @@
         out_specs=(whole(),) * 2,
         compiler_params=params(16),
         cost_estimate=cost(unit / 4, 5e6),
-    )(after(low, k0), diag_inv)
+    )(low, diag_inv)
 
     def neighbours(v):
         return (
@@ -291,6 +296,8 @@
         cost_estimate=cost(unit, 6e6),
     )(rhs, diag_inv)
 
+    envs = envs + [lax.ppermute(v, "pb", SWAP) for v in (after(e, k0) for e in envs)]
+
     bm = BM
     rows = blocks * width
     panel = lower_panel.reshape(rows, 2 * width)

time: 115 us -> 111 us (0.965)
  waiting for transfers between devices: 29.1 us -> 19.8 us
  starting transfers between devices: 42.1 us -> 46.6 us
    ppermute x3, waiting for transfers between devices: 7.66 us -> 0.01 us  [per_device(): lax.ppermute(got[d], 'rows', [(0, d), (1, (1 + d) % N)])]
    ppermute x7, waiting for transfers between devices: 6.61 us -> 0.66 us  [the longest x1 0.64 us: per_device(): envs = envs + [lax.ppermute(after(own, slices[1]), 'pb', z_perm(2))]]
    ppermute x2, waiting for transfers between devices: 2.17 us -> 7.76 us  [neighbours(): lax.ppermute(v, 'rows', x_perm(-1))]
    ppermute x3, starting transfers between devices: 4.58 us -> 9.53 us  [per_device(): lax.ppermute(even if d == 2 else odd, 'rows', [(c, d * N + c) for c in ra...]
    ppermute x2, starting transfers between devices: 1.57 us -> 5.87 us  [neighbours(): lax.ppermute(v, 'rows', x_perm(1))]
    ppermute x2, starting transfers between devices: 5.3 us -> 1 us  [neighbours(): lax.ppermute(v, 'rows', x_perm(-1))]
    all_to_all x2, waiting for transfers between devices: 0.01 us -> 4.07 us  [gather_queries(): lax.all_to_all(copies, 'rows', 0, 0, tiled=True).reshape(feats, count)]
    ppermute x4, waiting for transfers between devices: 2.49 us -> 0.13 us  [per_device(): slices = slices + [lax.ppermute(v, 'pb', SWAP) for v in slices]]
  transfers between devices with their start and end apart: 28 -> 28, of which waited for: 13 -> 7; matrix products, arithmetic and copies ran while one was open for 1% -> 2% of each run, Pallas kernels for 20% -> 22%
where the time goes in v5:
time: 111 us; the launch traced here: 110 us
  starting transfers between devices  46.6 us (42%)
  Pallas kernels  36.3 us (33%)
  waiting for transfers between devices  19.8 us (18%)
  local copies, waits for them, and re-layouts  4.48 us (4%)
  other arithmetic  2.52 us (2%)
    all_to_all x2, starting transfers between devices, gather_queries(): lax.all_to_all(copies, 'rows', 0, 0, tiled=True).reshape(feats, count)  14.2 us
    ppermute x3, starting transfers between devices, per_device(): lax.ppermute(even if d == 2 else odd, 'rows', [(c, d * N + c) for c in ra...  9.53 us
    pallas_call x1, Pallas kernels, per_device(): pl.pallas_call(last_step, grid=(rows // bm,), out_shape=jax.ShapeDtypeStr...  9.43 us
    ppermute x2, waiting for transfers between devices, neighbours(): lax.ppermute(v, 'rows', x_perm(-1))  7.76 us
    pallas_call x1, Pallas kernels, per_device(): pl.pallas_call(kernel_rows, grid=(rows // bm,), out_shape=jax.ShapeDtypeS...  7.35 us
    ppermute x3, waiting for transfers between devices, per_device(): slices = [mine] + [lax.ppermute(mine, 'pb', z_perm(d)) for d in (1, -1, 2)]  7.15 us
    ppermute x2, starting transfers between devices, neighbours(): lax.ppermute(v, 'rows', x_perm(1))  5.87 us
    pallas_call x1, Pallas kernels, per_device(): pl.pallas_call(update, grid=(rows // bm,), out_shape=jax.ShapeDtypeStruct...  5.35 us
  transfers between devices with their start and end apart: 28, of which 7 were waited for; matrix products, arithmetic and copies ran while one was open for 2% of the time, Pallas kernels for 22%

profile of v5, /device:TPU:6, one launch (start us, length us, event | category | flops | bytes accessed | tf_op | source)
XLA Modules:
  0.0 110.1 jit_solution(596836856040452310)
XLA Ops:
  0.7 2.9 %shard_map.46 = (bf16[1024,128]{1,0:T(8,128)(2,1)}, bf16[1024,128]{1,0:T(8,128)(2,1)}, bf16[1024,128]{1,0:T(8,128)(2,1)}, bf16[1024,128]{1,0:T(8,128)(2,1)}) custom-call(s32[4]{0:T(128)} %pad_add_fusion.at, bf16[2,1024,128]{2,1,0:T(8,128)(2,1)} %env.1, bf16[2,1024,2048]{2,1,0:T(8,128)(2,1)} %low.1), custom_call_target="tpu_custom_call" | custom-call | tf_op jit(solution)/shard_map/pallas_call | solution.py:181
  3.5 1.3 %collective-permute-start = (bf16[1024,128]{1,0:T(8,128)(2,1)}, bf16[1024,128]{1,0:T(8,128)(2,1)S(1)}, u32[]{:S(2)}, u32[]{:S(2)}) collective-permute-start(bf16[1024,128]{1,0:T(8,128)(2,1)} %get-tuple-element.26), channel_id=1, source_target_pairs={{0,24},{8,0},{1,25},{9,1},{2,26},{10,2},{3,27},{11,3},{4,28},{12,4... | collective-permute-start | bytes 786440 | tf_op jit(solution)/shard_map/ppermute | solution.py:217
  4.8 1.3 %collective-permute-start.1 = (bf16[1024,128]{1,0:T(8,128)(2,1)}, bf16[1024,128]{1,0:T(8,128)(2,1)S(1)}, u32[]{:S(2)}, u32[]{:S(2)}) collective-permute-start(bf16[1024,128]{1,0:T(8,128)(2,1)} %get-tuple-element.27), channel_id=1, source_target_pairs={{0,16},{8,24},{1,17},{9,25},{2,18},{10,26},{3,19},{11,27},{4,20},{... | collective-permute-start | bytes 786440 | tf_op jit(solution)/shard_map/ppermute | solution.py:217
  6.8 2.0 %collective-permute-start.6 = (bf16[2048,128]{1,0:T(8,128)(2,1)S(1)}, bf16[2048,128]{1,0:T(8,128)(2,1)S(1)}, u32[]{:S(2)}, u32[]{:S(2)}) collective-permute-start(bf16[2048,128]{1,0:T(8,128)(2,1)S(1)} %bitcast.16), channel_id=1, source_target_pairs={{0,2},{1,3},{2,4},{3,5},{4,6},{5,7},{6,0},{7,1},{8,10},{9,11},{10,... | collective-permute-start | bytes 1572872 | tf_op jit(solution)/shard_map/ppermute | solution.py:214
  8.8 2.2 %collective-permute-start.7 = (bf16[2048,128]{1,0:T(8,128)(2,1)S(1)}, bf16[2048,128]{1,0:T(8,128)(2,1)}, u32[]{:S(2)}, u32[]{:S(2)}) collective-permute-start(bf16[2048,128]{1,0:T(8,128)(2,1)S(1)} %bitcast.17), channel_id=1, source_target_pairs={{0,6},{1,7},{2,0},{3,1},{4,2},{5,3},{6,4},{7,5},{8,14},{9,15},{10,... | collective-permute-start | bytes 1572872 | tf_op jit(solution)/shard_map/ppermute | solution.py:214
  11.0 1.8 %shard_map.48 = bf16[16,64,256]{2,1,0:T(8,128)(2,1)} custom-call(bf16[64,1024]{1,0:T(8,128)(2,1)} %bitcast.23), custom_call_target="tpu_custom_call" | custom-call | tf_op jit(solution)/shard_map/pallas_call | solution.py:200
  12.9 9.3 %all-to-all-start = ((bf16[16,64,256]{2,1,0:T(8,128)(2,1)}), bf16[16,64,256]{2,1,0:T(8,128)(2,1)S(1)}, u32[]{:S(2)}, u32[]{:S(2)}) async-start(bf16[16,64,256]{2,1,0:T(8,128)(2,1)} %shard_map.48), calls=%async_computation | async-start | bytes 1048576 | tf_op jit(solution)/shard_map/all_to_all | solution.py:208
  22.2 1.0 select_select_fusion.1
  24.0 5.6 %collective-permute-start.4 = (bf16[768,128]{1,0:T(8,128)(2,1)}, bf16[768,128]{1,0:T(8,128)(2,1)}, u32[]{:S(2)}, u32[]{:S(2)}) collective-permute-start(bf16[768,128]{1,0:T(8,128)(2,1)} %pad_maximum_fusion.1), channel_id=1, source_target_pairs={{0,64},{8,72},{16,80},{24,88},{1,65},{9,73},{17,81},{25,89},{2,66}... | collective-permute-start | bytes 589832 | tf_op jit(solution)/shard_map/ppermute | solution.py:226
  29.6 2.0 %collective-permute-start.3 = (bf16[768,128]{1,0:T(8,128)(2,1)S(1)}, bf16[768,128]{1,0:T(8,128)(2,1)}, u32[]{:S(2)}, u32[]{:S(2)}) collective-permute-start(bf16[768,128]{1,0:T(8,128)(2,1)S(1)} %pad_maximum_fusion), channel_id=1, source_target_pairs={{0,96},{8,104},{16,112},{24,120},{1,97},{9,105},{17,113},{25,121},... | collective-permute-start | bytes 589832 | tf_op jit(solution)/shard_map/ppermute | solution.py:226
  31.6 2.0 %collective-permute-start.5 = (bf16[768,128]{1,0:T(8,128)(2,1)S(1)}, bf16[768,128]{1,0:T(8,128)(2,1)}, u32[]{:S(2)}, u32[]{:S(2)}) collective-permute-start(bf16[768,128]{1,0:T(8,128)(2,1)S(1)} %pad_maximum_fusion), channel_id=1, source_target_pairs={{0,32},{8,40},{16,48},{24,56},{1,33},{9,41},{17,49},{25,57},{2,34}... | collective-permute-start | bytes 589832 | tf_op jit(solution)/shard_map/ppermute | solution.py:226
  33.5 2.2 %shard_map.49 = bf16[16,64,768]{2,1,0:T(8,128)(2,1)} custom-call(bf16[64,1024]{1,0:T(8,128)(2,1)} %bitcast.24), custom_call_target="tpu_custom_call" | custom-call | tf_op jit(solution)/shard_map/pallas_call | solution.py:200
  35.7 4.8 %all-to-all-start.1 = ((bf16[16,64,768]{2,1,0:T(8,128)(2,1)}), bf16[16,64,768]{2,1,0:T(8,128)(2,1)S(1)}, u32[]{:S(2)}, u32[]{:S(2)}) async-start(bf16[16,64,768]{2,1,0:T(8,128)(2,1)} %shard_map.49), calls=%async_computation.1 | async-start | bytes 3145728 | tf_op jit(solution)/shard_map/all_to_all | solution.py:208
  40.8 3.2 %collective-permute-start.9 = (bf16[768,128]{1,0:T(8,128)(2,1)S(1)}, bf16[768,128]{1,0:T(8,128)(2,1)S(1)}, u32[]{:S(2)}, u32[]{:S(2)}) collective-permute-start(bf16[768,128]{1,0:T(8,128)(2,1)S(1)} %select_select_fusion.2.p0), channel_id=1, source_target_pairs={{0,6},{1,7},{2,0},{3,1},{4,2},{5,3},{6,4},{7,5},{8,14},{9,15},{10,... | collective-permute-start | bytes 589832 | tf_op jit(solution)/shard_map/ppermute | solution.py:231
  44.6 5.0 %collective-permute-done.8.p1 = bf16[768,128]{1,0:T(8,128)(2,1)S(1)} collective-permute-done((bf16[768,128]{1,0:T(8,128)(2,1)S(1)}, bf16[768,128]{1,0:T(8,128)(2,1)S(1)}, u32[]{:S(2)}, u32[]{:S(2)}) %collective-permute-start.8) | collective-permute-done | bytes 196640 | tf_op jit(solution)/shard_map/ppermute | solution.py:231
  50.3 1.5 %collective-permute-done.10.p3 = bf16[768,128]{1,0:T(8,128)(2,1)S(1)} collective-permute-done((bf16[768,128]{1,0:T(8,128)(2,1)S(1)}, bf16[768,128]{1,0:T(8,128)(2,1)S(1)}, u32[]{:S(2)}, u32[]{:S(2)}) %collective-permute-start.10) | collective-permute-done | bytes 196640 | tf_op jit(solution)/shard_map/ppermute | solution.py:231
  51.8 1.3 %collective-permute-start.21 = (bf16[2048,128]{1,0:T(8,128)(2,1)S(1)}, bf16[2048,128]{1,0:T(8,128)(2,1)}, u32[]{:S(2)}, u32[]{:S(2)}) collective-permute-start(bf16[2048,128]{1,0:T(8,128)(2,1)S(1)} %bitcast.18), channel_id=1, source_target_pairs={{0,4},{1,5},{2,6},{3,7},{4,0},{5,1},{6,2},{7,3},{8,12},{9,13},{10,... | collective-permute-start | bytes 1572872 | tf_op jit(solution)/shard_map/ppermute | solution.py:232
  53.2 1.0 shard_map.47
  54.2 1.0 copy-done.6
  55.2 4.1 %all-to-all-done.1 = bf16[16,64,768]{2,1,0:T(8,128)(2,1)S(1)} async-done(((bf16[16,64,768]{2,1,0:T(8,128)(2,1)}), bf16[16,64,768]{2,1,0:T(8,128)(2,1)S(1)}, u32[]{:S(2)}, u32[]{:S(2)}) %all-to-all-start.1) | async-done | bytes 1572896 | tf_op jit(solution)/shard_map/all_to_all | solution.py:208
  59.3 1.2 %copy-done.7 = bf16[512,1024]{1,0:T(8,128)(2,1)S(1)} copy-done((bf16[512,1024]{1,0:T(8,128)(2,1)S(1)}, bf16[512,1024]{1,0:T(8,128)(2,1)}, u32[]{:S(2)}) %copy-start.7) | copy-done | bytes 1048600
  60.5 1.3 %shard_map.50 = (bf16[256,1024]{1,0:T(8,128)(2,1)S(1)}, f32[256,1024]{1,0:T(8,128)S(1)}) custom-call(bf16[512,1024]{1,0:T(8,128)(2,1)S(1)} %copy-done.7, bf16[1024,256]{1,0:T(8,128)(2,1)S(1)} %bitcast.21, bf16[1024,768]{1,0:T(8,128)(2,1)S(1)} %bitcast.14), custom_call_target="tpu_custom_call" | custom-call | flops 1073741824 | bytes 5000000 | tf_op jit(solution)/shard_map/pallas_call | solution.py:248
  62.7 2.7 %collective-permute-start.16 = (bf16[256,1024]{1,0:T(8,128)(2,1)S(1)}, bf16[256,1024]{1,0:T(8,128)(2,1)S(1)}, u32[]{:S(2)}, u32[]{:S(2)}) collective-permute-start(bf16[256,1024]{1,0:T(8,128)(2,1)S(1)} %get-tuple-element.35.a), channel_id=1, source_target_pairs={{0,8},{8,16},{16,24},{24,0},{32,40},{40,48},{48,56},{56,32},{64,72... | collective-permute-start | bytes 1572872 | tf_op jit(solution)/shard_map/ppermute | solution.py:274
  65.4 1.7 %collective-permute-start.17 = (bf16[256,1024]{1,0:T(8,128)(2,1)S(1)}, bf16[256,1024]{1,0:T(8,128)(2,1)S(1)}, u32[]{:S(2)}, u32[]{:S(2)}) collective-permute-start(bf16[256,1024]{1,0:T(8,128)(2,1)S(1)} %get-tuple-element.35.a), channel_id=1, source_target_pairs={{0,96},{8,104},{16,112},{24,120},{32,0},{40,8},{48,16},{56,24},{64... | collective-permute-start | bytes 1572872 | tf_op jit(solution)/shard_map/ppermute | solution.py:275
  68.2 7.8 %collective-permute-done.15.b = bf16[256,1024]{1,0:T(8,128)(2,1)S(1)} collective-permute-done((bf16[256,1024]{1,0:T(8,128)(2,1)S(1)}, bf16[256,1024]{1,0:T(8,128)(2,1)S(1)}, u32[]{:S(2)}, u32[]{:S(2)}) %collective-permute-start.15) | collective-permute-done | bytes 524320 | tf_op jit(solution)/shard_map/ppermute | solution.py:273
  76.5 2.2 %copy-done = bf16[2,1024,1024]{2,1,0:T(8,128)(2,1)S(1)} copy-done((bf16[2,1024,1024]{2,1,0:T(8,128)(2,1)S(1)}, bf16[2,1024,1024]{2,1,0:T(8,128)(2,1)}, u32[]{:S(2)}) %copy-start) | copy-done | bytes 4194328
  79.5 2.0 %shard_map.52 = (bf16[256,1024]{1,0:T(8,128)(2,1)S(1)}, bf16[1024,1024]{1,0:T(8,128)(2,1)S(1)}) custom-call(s32[4]{0:T(128)S(1)} %copy-done.3, bf16[256,1024]{1,0:T(8,128)(2,1)S(1)} %get-tuple-element.35.a, bf16[256,1024]{1,0:T(8,128)(2,1)S(1)} %collective-permute-done.15.b, bf16[256,1024]{1,0:T(8,128)(2,1)S(1)} %collective-permute-done.16.c, ...), custom_call_target="tpu_custom_call" | custom-call | flops 1073741824 | bytes 8000000 | tf_op jit(solution)/shard_map/pallas_call | solution.py:278
  81.6 3.2 %collective-permute-start.19 = (bf16[256,1024]{1,0:T(8,128)(2,1)S(1)}, bf16[256,1024]{1,0:T(8,128)(2,1)S(1)}, u32[]{:S(2)}, u32[]{:S(2)}) collective-permute-start(bf16[256,1024]{1,0:T(8,128)(2,1)S(1)} %get-tuple-element.40.a), channel_id=1, source_target_pairs={{0,8},{8,16},{16,24},{24,0},{32,40},{40,48},{48,56},{56,32},{64,72... | collective-permute-start | bytes 1572872 | tf_op jit(solution)/shard_map/ppermute | solution.py:274
  85.5 7.3 %shard_map.54.k = f32[2048,1024]{1,0:T(8,128)S(1)} custom-call(s32[4]{0:T(128)S(1)} %copy-done.3, bf16[1024,256]{1,0:T(8,128)(2,1)S(1)} %bitcast.22, bf16[1024,768]{1,0:T(8,128)(2,1)S(1)} %bitcast.15, bf16[2048,128]{1,0:T(8,128)(2,1)S(1)} %bitcast.20, bf16[2048,128]{1,0:T(8,128)(2,1)S(1)} %copy-done.5, bf16[2048,128]{1,0:T(8,128)(2,1)} %collective-permute-done.7.p2, ...), custom_call_target="tpu_custom_call" | custom-call | flops 4294967296 | bytes 14000000 | tf_op jit(solution)/shard_map/pallas_call | solution.py:304
  92.9 2.3 %shard_map.53.s0 = bf16[1024,1024]{1,0:T(8,128)(2,1)S(1)} custom-call(bf16[1024,1024]{1,0:T(8,128)(2,1)S(1)} %get-tuple-element.41.rhs, bf16[2,1024,1024]{2,1,0:T(8,128)(2,1)S(1)} %copy-done.1), custom_call_target="tpu_custom_call" | custom-call | flops 2147483648 | bytes 6000000 | tf_op jit(solution)/shard_map/pallas_call | solution.py:289
  95.3 5.3 %shard_map.55.res = f32[2048,1024]{1,0:T(8,128)S(1)} custom-call(bf16[1024,1024]{1,0:T(8,128)(2,1)S(1)} %shard_map.53.s0, bf16[2048,2048]{1,0:T(8,128)(2,1)S(1)} %bitcast.12, f32[2048,1024]{1,0:T(8,128)S(1)} %shard_map.54.k), custom_call_target="tpu_custom_call" | custom-call | flops 4294967296 | bytes 22000000 | tf_op jit(solution)/shard_map/pallas_call | solution.py:314
  100.6 9.4 %shard_map.56 = bf16[2048,1024]{1,0:T(8,128)(2,1)} custom-call(s32[4]{0:T(128)S(1)} %copy-done.3, bf16[256,1024]{1,0:T(8,128)(2,1)S(1)} %get-tuple-element.40.a, bf16[256,1024]{1,0:T(8,128)(2,1)S(1)} %collective-permute-done.18.b, bf16[256,1024]{1,0:T(8,128)(2,1)S(1)} %collective-permute-done.19.c, bf16[256,1024]{1,0:T(8,128)(2,1)S(1)} %collective-permute-done.20.d, ...), custom_call_target="tpu_custom_call" | custom-call | flops 6442450944 | bytes 20000000 | tf_op jit(solution)/shard_map/pallas_call | solution.py:328
  (62 shorter events, 7.8 us)
Async XLA Ops:
  3.5 18.7 %collective-permute-start = (bf16[1024,128]{1,0:T(8,128)(2,1)}, bf16[1024,128]{1,0:T(8,128)(2,1)S(1)}, u32[]{:S(2)}, u32[]{:S(2)}) collective-permute-start(bf16[1024,128]{1,0:T(8,128)(2,1)} %get-tuple-element.26), channel_id=1, source_target_pairs={{0,24},{8,0},{1,25},{9,1},{2,26},{10,2},{3,27},{11,3},{4,28},{12,4... | collective-permute-start | bytes 786440 | tf_op jit(solution)/shard_map/ppermute | solution.py:217
  4.8 17.4 %collective-permute-start.1 = (bf16[1024,128]{1,0:T(8,128)(2,1)}, bf16[1024,128]{1,0:T(8,128)(2,1)S(1)}, u32[]{:S(2)}, u32[]{:S(2)}) collective-permute-start(bf16[1024,128]{1,0:T(8,128)(2,1)} %get-tuple-element.27), channel_id=1, source_target_pairs={{0,16},{8,24},{1,17},{9,25},{2,18},{10,26},{3,19},{11,27},{4,20},{... | collective-permute-start | bytes 786440 | tf_op jit(solution)/shard_map/ppermute | solution.py:217
  6.1 16.1 %collective-permute-start.2 = (bf16[1024,128]{1,0:T(8,128)(2,1)}, bf16[1024,128]{1,0:T(8,128)(2,1)S(1)}, u32[]{:S(2)}, u32[]{:S(2)}) collective-permute-start(bf16[1024,128]{1,0:T(8,128)(2,1)} %get-tuple-element.28), channel_id=1, source_target_pairs={{0,8},{8,16},{1,9},{9,17},{2,10},{10,18},{3,11},{11,19},{4,12},{12... | collective-permute-start | bytes 786440 | tf_op jit(solution)/shard_map/ppermute | solution.py:217
  6.8 33.9 %collective-permute-start.6 = (bf16[2048,128]{1,0:T(8,128)(2,1)S(1)}, bf16[2048,128]{1,0:T(8,128)(2,1)S(1)}, u32[]{:S(2)}, u32[]{:S(2)}) collective-permute-start(bf16[2048,128]{1,0:T(8,128)(2,1)S(1)} %bitcast.16), channel_id=1, source_target_pairs={{0,2},{1,3},{2,4},{3,5},{4,6},{5,7},{6,0},{7,1},{8,10},{9,11},{10,... | collective-permute-start | bytes 1572872 | tf_op jit(solution)/shard_map/ppermute | solution.py:214
  8.8 31.9 %collective-permute-start.7 = (bf16[2048,128]{1,0:T(8,128)(2,1)S(1)}, bf16[2048,128]{1,0:T(8,128)(2,1)}, u32[]{:S(2)}, u32[]{:S(2)}) collective-permute-start(bf16[2048,128]{1,0:T(8,128)(2,1)S(1)} %bitcast.17), channel_id=1, source_target_pairs={{0,6},{1,7},{2,0},{3,1},{4,2},{5,3},{6,4},{7,5},{8,14},{9,15},{10,... | collective-permute-start | bytes 1572872 | tf_op jit(solution)/shard_map/ppermute | solution.py:214
  12.9 22.9 %all-to-all-start = ((bf16[16,64,256]{2,1,0:T(8,128)(2,1)}), bf16[16,64,256]{2,1,0:T(8,128)(2,1)S(1)}, u32[]{:S(2)}, u32[]{:S(2)}) async-start(bf16[16,64,256]{2,1,0:T(8,128)(2,1)} %shard_map.48), calls=%async_computation | async-start | bytes 1048576 | tf_op jit(solution)/shard_map/all_to_all | solution.py:208
  22.2 31.0 %copy-start.3 = (s32[4]{0:T(128)S(1)}, s32[4]{0:T(128)}, u32[]{:S(2)}) copy-start(s32[4]{0:T(128)} %pad_add_fusion.at) | copy-start | bytes 52
  24.0 16.6 %collective-permute-start.4 = (bf16[768,128]{1,0:T(8,128)(2,1)}, bf16[768,128]{1,0:T(8,128)(2,1)}, u32[]{:S(2)}, u32[]{:S(2)}) collective-permute-start(bf16[768,128]{1,0:T(8,128)(2,1)} %pad_maximum_fusion.1), channel_id=1, source_target_pairs={{0,64},{8,72},{16,80},{24,88},{1,65},{9,73},{17,81},{25,89},{2,66}... | collective-permute-start | bytes 589832 | tf_op jit(solution)/shard_map/ppermute | solution.py:226
  29.6 11.0 %collective-permute-start.3 = (bf16[768,128]{1,0:T(8,128)(2,1)S(1)}, bf16[768,128]{1,0:T(8,128)(2,1)}, u32[]{:S(2)}, u32[]{:S(2)}) collective-permute-start(bf16[768,128]{1,0:T(8,128)(2,1)S(1)} %pad_maximum_fusion), channel_id=1, source_target_pairs={{0,96},{8,104},{16,112},{24,120},{1,97},{9,105},{17,113},{25,121},... | collective-permute-start | bytes 589832 | tf_op jit(solution)/shard_map/ppermute | solution.py:226
  31.6 9.0 %collective-permute-start.5 = (bf16[768,128]{1,0:T(8,128)(2,1)S(1)}, bf16[768,128]{1,0:T(8,128)(2,1)}, u32[]{:S(2)}, u32[]{:S(2)}) collective-permute-start(bf16[768,128]{1,0:T(8,128)(2,1)S(1)} %pad_maximum_fusion), channel_id=1, source_target_pairs={{0,32},{8,40},{16,48},{24,56},{1,33},{9,41},{17,49},{25,57},{2,34}... | collective-permute-start | bytes 589832 | tf_op jit(solution)/shard_map/ppermute | solution.py:226
  35.7 23.6 %all-to-all-start.1 = ((bf16[16,64,768]{2,1,0:T(8,128)(2,1)}), bf16[16,64,768]{2,1,0:T(8,128)(2,1)S(1)}, u32[]{:S(2)}, u32[]{:S(2)}) async-start(bf16[16,64,768]{2,1,0:T(8,128)(2,1)} %shard_map.49), calls=%async_computation.1 | async-start | bytes 3145728 | tf_op jit(solution)/shard_map/all_to_all | solution.py:208
  40.7 12.4 %copy-start.4 = (bf16[2048,128]{1,0:T(8,128)(2,1)}, bf16[2048,128]{1,0:T(8,128)(2,1)S(1)}, u32[]{:S(2)}) copy-start(bf16[2048,128]{1,0:T(8,128)(2,1)S(1)} %collective-permute-done.6.p1) | copy-start | bytes 1572868
  40.7 8.9 %collective-permute-start.8 = (bf16[768,128]{1,0:T(8,128)(2,1)S(1)}, bf16[768,128]{1,0:T(8,128)(2,1)S(1)}, u32[]{:S(2)}, u32[]{:S(2)}) collective-permute-start(bf16[768,128]{1,0:T(8,128)(2,1)S(1)} %select_select_fusion.2.p0), channel_id=1, source_target_pairs={{0,2},{1,3},{2,4},{3,5},{4,6},{5,7},{6,0},{7,1},{8,10},{9,11},{10,... | collective-permute-start | bytes 589832 | tf_op jit(solution)/shard_map/ppermute | solution.py:231
  40.8 9.5 %collective-permute-start.9 = (bf16[768,128]{1,0:T(8,128)(2,1)S(1)}, bf16[768,128]{1,0:T(8,128)(2,1)S(1)}, u32[]{:S(2)}, u32[]{:S(2)}) collective-permute-start(bf16[768,128]{1,0:T(8,128)(2,1)S(1)} %select_select_fusion.2.p0), channel_id=1, source_target_pairs={{0,6},{1,7},{2,0},{3,1},{4,2},{5,3},{6,4},{7,5},{8,14},{9,15},{10,... | collective-permute-start | bytes 589832 | tf_op jit(solution)/shard_map/ppermute | solution.py:231
  44.1 7.7 %collective-permute-start.10 = (bf16[768,128]{1,0:T(8,128)(2,1)S(1)}, bf16[768,128]{1,0:T(8,128)(2,1)S(1)}, u32[]{:S(2)}, u32[]{:S(2)}) collective-permute-start(bf16[768,128]{1,0:T(8,128)(2,1)S(1)} %select_select_fusion.2.p0), channel_id=1, source_target_pairs={{0,4},{1,5},{2,6},{3,7},{4,0},{5,1},{6,2},{7,3},{8,12},{9,13},{10,... | collective-permute-start | bytes 589832 | tf_op jit(solution)/shard_map/ppermute | solution.py:231
  44.6 8.5 %collective-permute-start.11 = (bf16[768,128]{1,0:T(8,128)(2,1)S(1)}, bf16[768,128]{1,0:T(8,128)(2,1)S(1)}, u32[]{:S(2)}, u32[]{:S(2)}) collective-permute-start(bf16[768,128]{1,0:T(8,128)(2,1)S(1)} %select_select_fusion.2.p0), channel_id=1, source_target_pairs={{0,1},{1,0},{2,3},{3,2},{4,5},{5,4},{6,7},{7,6},{8,9},{9,8},{10,11... | collective-permute-start | bytes 589832 | tf_op jit(solution)/shard_map/ppermute | solution.py:233
  49.7 3.4 %collective-permute-start.12 = (bf16[768,128]{1,0:T(8,128)(2,1)S(1)}, bf16[768,128]{1,0:T(8,128)(2,1)S(1)}, u32[]{:S(2)}, u32[]{:S(2)}) collective-permute-start(bf16[768,128]{1,0:T(8,128)(2,1)S(1)} %collective-permute-done.8.p1), channel_id=1, source_target_pairs={{0,1},{1,0},{2,3},{3,2},{4,5},{5,4},{6,7},{7,6},{8,9},{9,8},{10,11... | collective-permute-start | bytes 589832 | tf_op jit(solution)/shard_map/ppermute | solution.py:233
  50.3 2.8 %collective-permute-start.13 = (bf16[768,128]{1,0:T(8,128)(2,1)S(1)}, bf16[768,128]{1,0:T(8,128)(2,1)S(1)}, u32[]{:S(2)}, u32[]{:S(2)}) collective-permute-start(bf16[768,128]{1,0:T(8,128)(2,1)S(1)} %collective-permute-done.9.p2), channel_id=1, source_target_pairs={{0,1},{1,0},{2,3},{3,2},{4,5},{5,4},{6,7},{7,6},{8,9},{9,8},{10,11... | collective-permute-start | bytes 589832 | tf_op jit(solution)/shard_map/ppermute | solution.py:233
  51.8 1.4 %collective-permute-start.14 = (bf16[768,128]{1,0:T(8,128)(2,1)S(1)}, bf16[768,128]{1,0:T(8,128)(2,1)S(1)}, u32[]{:S(2)}, u32[]{:S(2)}) collective-permute-start(bf16[768,128]{1,0:T(8,128)(2,1)S(1)} %collective-permute-done.10.p3), channel_id=1, source_target_pairs={{0,1},{1,0},{2,3},{3,2},{4,5},{5,4},{6,7},{7,6},{8,9},{9,8},{10,11... | collective-permute-start | bytes 589832 | tf_op jit(solution)/shard_map/ppermute | solution.py:233
  51.8 15.9 %collective-permute-start.21 = (bf16[2048,128]{1,0:T(8,128)(2,1)S(1)}, bf16[2048,128]{1,0:T(8,128)(2,1)}, u32[]{:S(2)}, u32[]{:S(2)}) collective-permute-start(bf16[2048,128]{1,0:T(8,128)(2,1)S(1)} %bitcast.18), channel_id=1, source_target_pairs={{0,4},{1,5},{2,6},{3,7},{4,0},{5,1},{6,2},{7,3},{8,12},{9,13},{10,... | collective-permute-start | bytes 1572872 | tf_op jit(solution)/shard_map/ppermute | solution.py:232
  61.8 14.2 %collective-permute-start.15 = (bf16[256,1024]{1,0:T(8,128)(2,1)S(1)}, bf16[256,1024]{1,0:T(8,128)(2,1)S(1)}, u32[]{:S(2)}, u32[]{:S(2)}) collective-permute-start(bf16[256,1024]{1,0:T(8,128)(2,1)S(1)} %get-tuple-element.35.a), channel_id=1, source_target_pairs={{0,24},{8,0},{16,8},{24,16},{32,56},{40,32},{48,40},{56,48},{64,88... | collective-permute-start | bytes 1572872 | tf_op jit(solution)/shard_map/ppermute | solution.py:273
  62.7 13.3 %collective-permute-start.16 = (bf16[256,1024]{1,0:T(8,128)(2,1)S(1)}, bf16[256,1024]{1,0:T(8,128)(2,1)S(1)}, u32[]{:S(2)}, u32[]{:S(2)}) collective-permute-start(bf16[256,1024]{1,0:T(8,128)(2,1)S(1)} %get-tuple-element.35.a), channel_id=1, source_target_pairs={{0,8},{8,16},{16,24},{24,0},{32,40},{40,48},{48,56},{56,32},{64,72... | collective-permute-start | bytes 1572872 | tf_op jit(solution)/shard_map/ppermute | solution.py:274
  65.4 14.1 %collective-permute-start.17 = (bf16[256,1024]{1,0:T(8,128)(2,1)S(1)}, bf16[256,1024]{1,0:T(8,128)(2,1)S(1)}, u32[]{:S(2)}, u32[]{:S(2)}) collective-permute-start(bf16[256,1024]{1,0:T(8,128)(2,1)S(1)} %get-tuple-element.35.a), channel_id=1, source_target_pairs={{0,96},{8,104},{16,112},{24,120},{32,0},{40,8},{48,16},{56,24},{64... | collective-permute-start | bytes 1572872 | tf_op jit(solution)/shard_map/ppermute | solution.py:275
  67.7 13.9 %collective-permute-start.25 = (bf16[2048,128]{1,0:T(8,128)(2,1)}, bf16[2048,128]{1,0:T(8,128)(2,1)S(1)}, u32[]{:S(2)}, u32[]{:S(2)}) collective-permute-start(bf16[2048,128]{1,0:T(8,128)(2,1)} %collective-permute-done.21.p3), channel_id=1, source_target_pairs={{0,1},{1,0},{2,3},{3,2},{4,5},{5,4},{6,7},{7,6},{8,9},{9,8},{10,11... | collective-permute-start | bytes 1572872 | tf_op jit(solution)/shard_map/ppermute | solution.py:299
  67.7 17.1 %collective-permute-start.23 = (bf16[2048,128]{1,0:T(8,128)(2,1)}, bf16[2048,128]{1,0:T(8,128)(2,1)S(1)}, u32[]{:S(2)}, u32[]{:S(2)}) collective-permute-start(bf16[2048,128]{1,0:T(8,128)(2,1)} %copy-done.4), channel_id=1, source_target_pairs={{0,1},{1,0},{2,3},{3,2},{4,5},{5,4},{6,7},{7,6},{8,9},{9,8},{10,11... | collective-permute-start | bytes 1572872 | tf_op jit(solution)/shard_map/ppermute | solution.py:299
  76.0 9.5 %collective-permute-start.24 = (bf16[2048,128]{1,0:T(8,128)(2,1)}, bf16[2048,128]{1,0:T(8,128)(2,1)S(1)}, u32[]{:S(2)}, u32[]{:S(2)}) collective-permute-start(bf16[2048,128]{1,0:T(8,128)(2,1)} %collective-permute-done.7.p2), channel_id=1, source_target_pairs={{0,1},{1,0},{2,3},{3,2},{4,5},{5,4},{6,7},{7,6},{8,9},{9,8},{10,11... | collective-permute-start | bytes 1572872 | tf_op jit(solution)/shard_map/ppermute | solution.py:299
  76.0 9.5 %collective-permute-start.22 = (bf16[2048,128]{1,0:T(8,128)(2,1)S(1)}, bf16[2048,128]{1,0:T(8,128)(2,1)S(1)}, u32[]{:S(2)}, u32[]{:S(2)}) collective-permute-start(bf16[2048,128]{1,0:T(8,128)(2,1)S(1)} %bitcast.19), channel_id=1, source_target_pairs={{0,1},{1,0},{2,3},{3,2},{4,5},{5,4},{6,7},{7,6},{8,9},{9,8},{10,11... | collective-permute-start | bytes 1572872 | tf_op jit(solution)/shard_map/ppermute | solution.py:299
  79.4 15.8 %slice-start = ((s8[8388608]{0:T(1024)(128)(4,1)}), s8[4194304]{0:T(1024)(128)(4,1)S(1)}, s32[]{:S(2)}) async-start(s8[8388608]{0:T(1024)(128)(4,1)} %bitcast.10), calls=%async_computation.2 | async-start | bytes 8388608
  81.5 13.7 %slice-start.1 = ((s8[8388608]{0:T(1024)(128)(4,1)}), s8[4194304]{0:T(1024)(128)(4,1)S(1)}, s32[]{:S(2)}) async-start(s8[8388608]{0:T(1024)(128)(4,1)} %bitcast.10), calls=%async_computation.3 | async-start | bytes 8388608
  81.5 19.1 %collective-permute-start.18 = (bf16[256,1024]{1,0:T(8,128)(2,1)S(1)}, bf16[256,1024]{1,0:T(8,128)(2,1)S(1)}, u32[]{:S(2)}, u32[]{:S(2)}) collective-permute-start(bf16[256,1024]{1,0:T(8,128)(2,1)S(1)} %get-tuple-element.40.a), channel_id=1, source_target_pairs={{0,24},{8,0},{16,8},{24,16},{32,56},{40,32},{48,40},{56,48},{64,88... | collective-permute-start | bytes 1572872 | tf_op jit(solution)/shard_map/ppermute | solution.py:273
  81.6 19.0 %collective-permute-start.19 = (bf16[256,1024]{1,0:T(8,128)(2,1)S(1)}, bf16[256,1024]{1,0:T(8,128)(2,1)S(1)}, u32[]{:S(2)}, u32[]{:S(2)}) collective-permute-start(bf16[256,1024]{1,0:T(8,128)(2,1)S(1)} %get-tuple-element.40.a), channel_id=1, source_target_pairs={{0,8},{8,16},{16,24},{24,0},{32,40},{40,48},{48,56},{56,32},{64,72... | collective-permute-start | bytes 1572872 | tf_op jit(solution)/shard_map/ppermute | solution.py:274
  84.8 15.8 %collective-permute-start.20 = (bf16[256,1024]{1,0:T(8,128)(2,1)S(1)}, bf16[256,1024]{1,0:T(8,128)(2,1)S(1)}, u32[]{:S(2)}, u32[]{:S(2)}) collective-permute-start(bf16[256,1024]{1,0:T(8,128)(2,1)S(1)} %get-tuple-element.40.a), channel_id=1, source_target_pairs={{0,96},{8,104},{16,112},{24,120},{32,0},{40,8},{48,16},{56,24},{64... | collective-permute-start | bytes 1572872 | tf_op jit(solution)/shard_map/ppermute | solution.py:275
  (6 other events, 28.8 us)

commit v6 on v5

--- a/solution.py
+++ b/solution.py
@@ -138,32 +138,43 @@
     out[...] = k[...] - jnp.dot(low[...], s0[...], preferred_element_type=F32)
 
 
-def last_step(at, a, b, c, d, inv, s0, low, res, out, rhs, s1):
+def through_second(at, low, inv, out):
+    here = at[0] + 4 * at[1]
+    i, bm = pl.program_id(0), out.shape[0]
+    solving = jnp.logical_and(here == 1, i < inv.shape[0] // bm)
+
+    @pl.when(solving)
+    def _():
+        out[...] = inv[pl.ds(pl.multiple_of(lax.rem(i * bm, inv.shape[0]), bm), bm), :]
+
+    @pl.when(jnp.logical_not(solving))
+    def _():
+        out[...] = jnp.dot(low[...], inv[...], preferred_element_type=F32).astype(BF16)
+
+
+def last_step(at, a, b, c, d, s0, low, res, out, rhs):
     i = pl.program_id(0)
     here = at[0] + 4 * at[1]
     bm = out.shape[0]
-    per_block = s1.shape[0] // bm
+    per_block = s0.shape[0] // bm
 
     @pl.when(i == 0)
     def _():
         place_rows(at, (a, b, c, d), rhs)
 
-        s1[...] = jnp.dot(inv[...], rhs[...], preferred_element_type=F32).astype(BF16)
-
-    rows = pl.ds(pl.multiple_of(lax.rem(i, per_block) * bm, bm), bm)
     first = i < per_block
 
     @pl.when(jnp.logical_and(first, here == 0))
     def _():
-        out[...] = s0[rows, :]
+        out[...] = s0[pl.ds(pl.multiple_of(lax.rem(i, per_block) * bm, bm), bm), :]
 
     @pl.when(jnp.logical_and(first, here == 1))
     def _():
-        out[...] = s1[rows, :]
+        out[...] = jnp.dot(low[...], rhs[...], preferred_element_type=F32).astype(BF16)
 
     @pl.when(jnp.logical_not(jnp.logical_and(first, here < 2)))
     def _():
-        out[...] = (res[...] - jnp.dot(low[...], s1[...], preferred_element_type=F32)).astype(BF16)
+        out[...] = (res[...] - jnp.dot(low[...], rhs[...], preferred_element_type=F32)).astype(BF16)
 
 
 def per_device(lower_panel, sparse_desc, query_desc, diag_inv):
@@ -245,6 +256,24 @@
         compiler_params=params(16),
         cost_estimate=cost(6900000000, 22200000),
     )(at, *slices)
+    high, rest = pl.pallas_call(
+        through_first,
+        grid=(1,),
+        out_shape=(narrow, narrow),
+        in_specs=[whole(), block(0)],
+        out_specs=(whole(),) * 2,
+        compiler_params=params(16),
+        cost_estimate=cost(unit / 4, 5e6),
+    )(low, diag_inv)
+    second = pl.pallas_call(
+        through_second,
+        grid=(blocks * width // BM,),
+        out_shape=jax.ShapeDtypeStruct((blocks * width, width), BF16),
+        in_specs=[smem, pl.BlockSpec((BM, width), lambda i: (i, 1)), block(1)],
+        out_specs=pl.BlockSpec((BM, width), lambda i: (i, 0)),
+        compiler_params=params(20),
+        cost_estimate=cost(unit / 50, 2e5),
+    )(after(at, high), lower_panel.reshape(blocks * width, 2 * width), diag_inv)
     k0, k1 = pl.pallas_call(
         kernel_slices,
         out_shape=(
@@ -255,17 +284,7 @@
         out_specs=(whole(), whole()),
         compiler_params=params(16),
         cost_estimate=cost(unit / 2, 5e6),
-    )(slice_feats, qa, qb)
-
-    high, rest = pl.pallas_call(
-        through_first,
-        grid=(1,),
-        out_shape=(narrow, narrow),
-        in_specs=[whole(), block(0)],
-        out_specs=(whole(),) * 2,
-        compiler_params=params(16),
-        cost_estimate=cost(unit / 4, 5e6),
-    )(low, diag_inv)
+    )(after(slice_feats, high, second), qa, qb)
 
     def neighbours(v):
         return (
@@ -275,6 +294,22 @@
             lax.ppermute(v, "rows", y_perm(-1)),
         )
 
+    ready = [after(e, slice_feats) for e in envs[:3]] + [after(envs[3], k0)]
+    envs = envs + [lax.ppermute(v, "pb", SWAP) for v in ready]
+
+    bm = BM
+    rows = blocks * width
+    panel = lower_panel.reshape(rows, 2 * width)
+    k_rows = pl.pallas_call(
+        kernel_rows,
+        grid=(rows // bm,),
+        out_shape=jax.ShapeDtypeStruct((rows, queries), F32),
+        in_specs=[smem, whole(), whole()] + [pl.BlockSpec((bm, piece), lambda i: (i, 0))] * 8,
+        out_specs=pl.BlockSpec((bm, queries), lambda i: (i, 0)),
+        scratch_shapes=[pltpu.VMEM((bm, feats), BF16)],
+        compiler_params=params(16),
+        cost_estimate=cost(unit * 2, 14e6),
+    )(at, qa, qb, *envs)
     t, rhs = pl.pallas_call(
         right_side,
         out_shape=(
@@ -285,7 +320,7 @@
         out_specs=(whole(),) * 2,
         compiler_params=params(20),
         cost_estimate=cost(unit * 0.5, 8e6),
-    )(at, *neighbours(k0), high, rest, k1)
+    )(at, *neighbours(k0), high, rest, after(k1, k_rows))
     s0 = pl.pallas_call(
         first_solve,
         grid=(1,),
@@ -296,21 +331,6 @@
         cost_estimate=cost(unit, 6e6),
     )(rhs, diag_inv)
 
-    envs = envs + [lax.ppermute(v, "pb", SWAP) for v in (after(e, k0) for e in envs)]
-
-    bm = BM
-    rows = blocks * width
-    panel = lower_panel.reshape(rows, 2 * width)
-    k_rows = pl.pallas_call(
-        kernel_rows,
-        grid=(rows // bm,),
-        out_shape=jax.ShapeDtypeStruct((rows, queries), F32),
-        in_specs=[smem, whole(), whole()] + [pl.BlockSpec((bm, piece), lambda i: (i, 0))] * 8,
-        out_specs=pl.BlockSpec((bm, queries), lambda i: (i, 0)),
-        scratch_shapes=[pltpu.VMEM((bm, feats), BF16)],
-        compiler_params=params(16),
-        cost_estimate=cost(unit * 2, 14e6),
-    )(at, qa, qb, *envs)
     res = pl.pallas_call(
         update,
         grid=(rows // bm,),
@@ -321,6 +341,7 @@
             pl.BlockSpec((bm, queries), lambda i: (i, 0)),
         ],
         out_specs=pl.BlockSpec((bm, queries), lambda i: (i, 0)),
+        input_output_aliases={2: 0},
         compiler_params=params(16),
         cost_estimate=cost(unit * 2, 22e6),
     )(s0, panel, k_rows)
@@ -332,16 +353,15 @@
         in_specs=[smem]
         + [whole()] * 4
         + [
-            block(1),
             whole(),
-            pl.BlockSpec((bm, width), lambda i: (i, 1)),
+            pl.BlockSpec((bm, width), lambda i: (i, 0)),
             pl.BlockSpec((bm, queries), lambda i: (i, 0)),
         ],
         out_specs=pl.BlockSpec((bm, queries), lambda i: (i, 0)),
-        scratch_shapes=[pltpu.VMEM((width, queries), BF16), pltpu.VMEM((width, queries), BF16)],
+        scratch_shapes=[pltpu.VMEM((width, queries), BF16)],
         compiler_params=params(20),
-        cost_estimate=cost(unit * 3, 20e6),
-    )(at, *neighbours(t), diag_inv, s0, panel, res)
+        cost_estimate=cost(unit * 2, 18e6),
+    )(at, *neighbours(t), s0, second, res)
     return out.reshape(blocks, width, queries)
 
 

time: 111 us -> 109 us (0.982)
  Pallas kernels: 36.3 us -> 40.6 us
  waiting for transfers between devices: 19.8 us -> 15.7 us
  starting transfers between devices: 46.6 us -> 44.3 us
    pallas_call x0 -> x1, Pallas kernels: none -> 5.89 us  [per_device(): pl.pallas_call(through_second, grid=(blocks * width // BM,), out_shape=ja...]
    ppermute x2, starting transfers between devices: 5.87 us -> 0.84 us  [neighbours(): lax.ppermute(v, 'rows', x_perm(1))]
    ppermute x2, waiting for transfers between devices: 7.76 us -> 3.04 us  [neighbours(): lax.ppermute(v, 'rows', x_perm(-1))]
    all_to_all x2, waiting for transfers between devices: 4.07 us -> 0.01 us  [gather_queries(): lax.all_to_all(copies, 'rows', 0, 0, tiled=True).reshape(feats, count)]
    ppermute x2, waiting for transfers between devices: 0.01 us -> 3.2 us  [neighbours(): lax.ppermute(v, 'rows', y_perm(-1))]
    ppermute x2, waiting for transfers between devices: 0.01 us -> 2.78 us  [neighbours(): lax.ppermute(v, 'rows', x_perm(1))]
    pallas_call x1, Pallas kernels: 9.43 us -> 6.84 us  [per_device(): pl.pallas_call(last_step, grid=(rows // bm,), out_shape=jax.ShapeDtypeStr...]
    ppermute x2, starting transfers between devices: 1 us -> 3.22 us  [neighbours(): lax.ppermute(v, 'rows', x_perm(-1))]
  transfers between devices with their start and end apart: 28 -> 28, of which waited for: 7 -> 8; matrix products, arithmetic and copies ran while one was open for 2% -> 1% of each run, Pallas kernels for 22% -> 27%
where the time goes in v6:
time: 109 us; the launch traced here: 108 us
  starting transfers between devices  44.3 us (41%)
  Pallas kernels  40.6 us (37%)
  waiting for transfers between devices  15.7 us (14%)
  local copies, waits for them, and re-layouts  5.14 us (5%)
  other arithmetic  1.77 us (2%)
    all_to_all x2, starting transfers between devices, gather_queries(): lax.all_to_all(copies, 'rows', 0, 0, tiled=True).reshape(feats, count)  14.2 us
    pallas_call x1, Pallas kernels, per_device(): pl.pallas_call(kernel_rows, grid=(rows // bm,), out_shape=jax.ShapeDtypeS...  7.61 us
    ppermute x3, starting transfers between devices, per_device(): lax.ppermute(even if d == 2 else odd, 'rows', [(c, d * N + c) for c in ra...  7.54 us
    pallas_call x1, Pallas kernels, per_device(): pl.pallas_call(last_step, grid=(rows // bm,), out_shape=jax.ShapeDtypeStr...  6.84 us
    ppermute x3, waiting for transfers between devices, per_device(): slices = [mine] + [lax.ppermute(mine, 'pb', z_perm(d)) for d in (1, -1, 2)]  6.67 us
    pallas_call x1, Pallas kernels, per_device(): pl.pallas_call(update, grid=(rows // bm,), out_shape=jax.ShapeDtypeStruct...  6.04 us
    pallas_call x1, Pallas kernels, per_device(): pl.pallas_call(through_second, grid=(blocks * width // BM,), out_shape=ja...  5.89 us
    unnamed x28, local copies, waits for them, and re-layouts  5.12 us
  transfers between devices with their start and end apart: 28, of which 8 were waited for; matrix products, arithmetic and copies ran while one was open for 1% of the time, Pallas kernels for 27%

profile of v6, /device:TPU:6, one launch (start us, length us, event | category | flops | bytes accessed | tf_op | source)
XLA Modules:
  0.0 107.9 jit_solution(842740324460654491)
XLA Ops:
  0.6 2.9 %shard_map.46 = (bf16[1024,128]{1,0:T(8,128)(2,1)}, bf16[1024,128]{1,0:T(8,128)(2,1)}, bf16[1024,128]{1,0:T(8,128)(2,1)}, bf16[1024,128]{1,0:T(8,128)(2,1)}) custom-call(s32[4]{0:T(128)} %pad_add_fusion.at, bf16[2,1024,128]{2,1,0:T(8,128)(2,1)} %env.1, bf16[2,1024,2048]{2,1,0:T(8,128)(2,1)} %low.1), custom_call_target="tpu_custom_call" | custom-call | tf_op jit(solution)/shard_map/pallas_call | solution.py:192
  3.5 1.3 %collective-permute-start = (bf16[1024,128]{1,0:T(8,128)(2,1)}, bf16[1024,128]{1,0:T(8,128)(2,1)S(1)}, u32[]{:S(2)}, u32[]{:S(2)}) collective-permute-start(bf16[1024,128]{1,0:T(8,128)(2,1)} %get-tuple-element.29), channel_id=1, source_target_pairs={{0,24},{8,0},{1,25},{9,1},{2,26},{10,2},{3,27},{11,3},{4,28},{12,4... | collective-permute-start | bytes 786440 | tf_op jit(solution)/shard_map/ppermute | solution.py:228
  4.8 1.3 %collective-permute-start.1 = (bf16[1024,128]{1,0:T(8,128)(2,1)}, bf16[1024,128]{1,0:T(8,128)(2,1)S(1)}, u32[]{:S(2)}, u32[]{:S(2)}) collective-permute-start(bf16[1024,128]{1,0:T(8,128)(2,1)} %get-tuple-element.30), channel_id=1, source_target_pairs={{0,16},{8,24},{1,17},{9,25},{2,18},{10,26},{3,19},{11,27},{4,20},{... | collective-permute-start | bytes 786440 | tf_op jit(solution)/shard_map/ppermute | solution.py:228
  6.8 4.1 %collective-permute-start.7 = (bf16[2048,128]{1,0:T(8,128)(2,1)S(1)}, bf16[2048,128]{1,0:T(8,128)(2,1)}, u32[]{:S(2)}, u32[]{:S(2)}) collective-permute-start(bf16[2048,128]{1,0:T(8,128)(2,1)S(1)} %bitcast.18), channel_id=1, source_target_pairs={{0,6},{1,7},{2,0},{3,1},{4,2},{5,3},{6,4},{7,5},{8,14},{9,15},{10,... | collective-permute-start | bytes 1572872 | tf_op jit(solution)/shard_map/ppermute | solution.py:225
  10.9 1.8 %shard_map.50 = bf16[16,64,256]{2,1,0:T(8,128)(2,1)} custom-call(bf16[64,1024]{1,0:T(8,128)(2,1)} %bitcast.25), custom_call_target="tpu_custom_call" | custom-call | tf_op jit(solution)/shard_map/pallas_call | solution.py:211
  12.7 9.4 %all-to-all-start = ((bf16[16,64,256]{2,1,0:T(8,128)(2,1)}), bf16[16,64,256]{2,1,0:T(8,128)(2,1)S(1)}, u32[]{:S(2)}, u32[]{:S(2)}) async-start(bf16[16,64,256]{2,1,0:T(8,128)(2,1)} %shard_map.50), calls=%async_computation | async-start | bytes 1048576 | tf_op jit(solution)/shard_map/all_to_all | solution.py:219
  23.2 4.9 %collective-permute-start.4 = (bf16[768,128]{1,0:T(8,128)(2,1)S(1)}, bf16[768,128]{1,0:T(8,128)(2,1)S(1)}, u32[]{:S(2)}, u32[]{:S(2)}) collective-permute-start(bf16[768,128]{1,0:T(8,128)(2,1)S(1)} %pad_maximum_fusion.1), channel_id=1, source_target_pairs={{0,64},{8,72},{16,80},{24,88},{1,65},{9,73},{17,81},{25,89},{2,66}... | collective-permute-start | bytes 589832 | tf_op jit(solution)/shard_map/ppermute | solution.py:237
  28.1 1.3 %collective-permute-start.5 = (bf16[768,128]{1,0:T(8,128)(2,1)S(1)}, bf16[768,128]{1,0:T(8,128)(2,1)S(1)}, u32[]{:S(2)}, u32[]{:S(2)}) collective-permute-start(bf16[768,128]{1,0:T(8,128)(2,1)S(1)} %pad_maximum_fusion), channel_id=1, source_target_pairs={{0,32},{8,40},{16,48},{24,56},{1,33},{9,41},{17,49},{25,57},{2,34}... | collective-permute-start | bytes 589832 | tf_op jit(solution)/shard_map/ppermute | solution.py:237
  29.4 1.3 %collective-permute-start.3 = (bf16[768,128]{1,0:T(8,128)(2,1)S(1)}, bf16[768,128]{1,0:T(8,128)(2,1)S(1)}, u32[]{:S(2)}, u32[]{:S(2)}) collective-permute-start(bf16[768,128]{1,0:T(8,128)(2,1)S(1)} %pad_maximum_fusion), channel_id=1, source_target_pairs={{0,96},{8,104},{16,112},{24,120},{1,97},{9,105},{17,113},{25,121},... | collective-permute-start | bytes 589832 | tf_op jit(solution)/shard_map/ppermute | solution.py:237
  30.8 2.2 %shard_map.51 = bf16[16,64,768]{2,1,0:T(8,128)(2,1)} custom-call(bf16[64,1024]{1,0:T(8,128)(2,1)} %bitcast.26), custom_call_target="tpu_custom_call" | custom-call | tf_op jit(solution)/shard_map/pallas_call | solution.py:211
  33.8 4.8 %all-to-all-start.1 = ((bf16[16,64,768]{2,1,0:T(8,128)(2,1)}), bf16[16,64,768]{2,1,0:T(8,128)(2,1)S(1)}, u32[]{:S(2)}, u32[]{:S(2)}) async-start(bf16[16,64,768]{2,1,0:T(8,128)(2,1)} %shard_map.51), calls=%async_computation.1 | async-start | bytes 3145728 | tf_op jit(solution)/shard_map/all_to_all | solution.py:219
  38.8 1.9 %collective-permute-start.10 = (bf16[768,128]{1,0:T(8,128)(2,1)S(1)}, bf16[768,128]{1,0:T(8,128)(2,1)S(1)}, u32[]{:S(2)}, u32[]{:S(2)}) collective-permute-start(bf16[768,128]{1,0:T(8,128)(2,1)S(1)} %select_select_fusion.2.p0), channel_id=1, source_target_pairs={{0,4},{1,5},{2,6},{3,7},{4,0},{5,1},{6,2},{7,3},{8,12},{9,13},{10,... | collective-permute-start | bytes 589832 | tf_op jit(solution)/shard_map/ppermute | solution.py:242
  40.7 1.5 %collective-permute-start.9 = (bf16[768,128]{1,0:T(8,128)(2,1)S(1)}, bf16[768,128]{1,0:T(8,128)(2,1)S(1)}, u32[]{:S(2)}, u32[]{:S(2)}) collective-permute-start(bf16[768,128]{1,0:T(8,128)(2,1)S(1)} %select_select_fusion.2.p0), channel_id=1, source_target_pairs={{0,6},{1,7},{2,0},{3,1},{4,2},{5,3},{6,4},{7,5},{8,14},{9,15},{10,... | collective-permute-start | bytes 589832 | tf_op jit(solution)/shard_map/ppermute | solution.py:242
  43.0 4.3 %collective-permute-done.10.p3 = bf16[768,128]{1,0:T(8,128)(2,1)S(1)} collective-permute-done((bf16[768,128]{1,0:T(8,128)(2,1)S(1)}, bf16[768,128]{1,0:T(8,128)(2,1)S(1)}, u32[]{:S(2)}, u32[]{:S(2)}) %collective-permute-start.10) | collective-permute-done | bytes 196640 | tf_op jit(solution)/shard_map/ppermute | solution.py:242
  47.3 2.4 %collective-permute-done.9.p2 = bf16[768,128]{1,0:T(8,128)(2,1)S(1)} collective-permute-done((bf16[768,128]{1,0:T(8,128)(2,1)S(1)}, bf16[768,128]{1,0:T(8,128)(2,1)S(1)}, u32[]{:S(2)}, u32[]{:S(2)}) %collective-permute-start.9) | collective-permute-done | bytes 196640 | tf_op jit(solution)/shard_map/ppermute | solution.py:242
  50.2 1.6 %collective-permute-start.18 = (bf16[2048,128]{1,0:T(8,128)(2,1)S(1)}, bf16[2048,128]{1,0:T(8,128)(2,1)}, u32[]{:S(2)}, u32[]{:S(2)}) collective-permute-start(bf16[2048,128]{1,0:T(8,128)(2,1)S(1)} %bitcast.20), channel_id=1, source_target_pairs={{0,4},{1,5},{2,6},{3,7},{4,0},{5,1},{6,2},{7,3},{8,12},{9,13},{10,... | collective-permute-start | bytes 1572872 | tf_op jit(solution)/shard_map/ppermute | solution.py:243
  54.5 5.9 %shard_map.49.low = bf16[2048,1024]{1,0:T(8,128)(2,1)S(1)} custom-call(s32[4]{0:T(128)S(1)} %copy-done.7, bf16[2048,2048]{1,0:T(8,128)(2,1)S(1)} %bitcast.12, bf16[2,1024,1024]{2,1,0:T(8,128)(2,1)S(1)} %copy-done), custom_call_target="tpu_custom_call" | custom-call | flops 42949672 | bytes 200000 | tf_op jit(solution)/shard_map/pallas_call | solution.py:268
  60.4 2.0 %copy-done.2 = bf16[2048,1024]{1,0:T(8,128)(2,1)} copy-done((bf16[2048,1024]{1,0:T(8,128)(2,1)}, bf16[2048,1024]{1,0:T(8,128)(2,1)S(1)}, u32[]{:S(2)}) %copy-start.2) | copy-done | bytes 4194328
  64.6 1.3 %shard_map.52 = (bf16[256,1024]{1,0:T(8,128)(2,1)S(1)}, f32[256,1024]{1,0:T(8,128)S(1)}) custom-call(bf16[512,1024]{1,0:T(8,128)(2,1)S(1)} %copy-done.9, bf16[1024,256]{1,0:T(8,128)(2,1)S(1)} %bitcast.23, bf16[1024,768]{1,0:T(8,128)(2,1)S(1)} %bitcast.16), custom_call_target="tpu_custom_call" | custom-call | flops 1073741824 | bytes 5000000 | tf_op jit(solution)/shard_map/pallas_call | solution.py:277
  66.3 2.7 %collective-permute-start.17 = (bf16[256,1024]{1,0:T(8,128)(2,1)S(1)}, bf16[256,1024]{1,0:T(8,128)(2,1)S(1)}, u32[]{:S(2)}, u32[]{:S(2)}) collective-permute-start(bf16[256,1024]{1,0:T(8,128)(2,1)S(1)} %get-tuple-element.42.a), channel_id=1, source_target_pairs={{0,96},{8,104},{16,112},{24,120},{32,0},{40,8},{48,16},{56,24},{64... | collective-permute-start | bytes 1572872 | tf_op jit(solution)/shard_map/ppermute | solution.py:294
  69.6 1.5 %collective-permute-start.15 = (bf16[256,1024]{1,0:T(8,128)(2,1)S(1)}, bf16[256,1024]{1,0:T(8,128)(2,1)S(1)}, u32[]{:S(2)}, u32[]{:S(2)}) collective-permute-start(bf16[256,1024]{1,0:T(8,128)(2,1)S(1)} %get-tuple-element.42.a), channel_id=1, source_target_pairs={{0,24},{8,0},{16,8},{24,16},{32,56},{40,32},{48,40},{56,48},{64,88... | collective-permute-start | bytes 1572872 | tf_op jit(solution)/shard_map/ppermute | solution.py:292
  71.0 7.6 %shard_map.53.k = f32[2048,1024]{1,0:T(8,128)S(1)} custom-call(s32[4]{0:T(128)S(1)} %copy-done.7, bf16[1024,256]{1,0:T(8,128)(2,1)S(1)} %bitcast.24, bf16[1024,768]{1,0:T(8,128)(2,1)S(1)} %bitcast.17, bf16[2048,128]{1,0:T(8,128)(2,1)S(1)} %bitcast.22, bf16[2048,128]{1,0:T(8,128)(2,1)} %collective-permute-done.6.p1, ...), custom_call_target="tpu_custom_call" | custom-call | flops 4294967296 | bytes 14000000 | tf_op jit(solution)/shard_map/pallas_call | solution.py:303
  78.7 1.9 %collective-permute-done.17.d = bf16[256,1024]{1,0:T(8,128)(2,1)S(1)} collective-permute-done((bf16[256,1024]{1,0:T(8,128)(2,1)S(1)}, bf16[256,1024]{1,0:T(8,128)(2,1)S(1)}, u32[]{:S(2)}, u32[]{:S(2)}) %collective-permute-start.17) | collective-permute-done | bytes 524320 | tf_op jit(solution)/shard_map/ppermute | solution.py:294
  80.6 2.2 %collective-permute-done.16.c = bf16[256,1024]{1,0:T(8,128)(2,1)S(1)} collective-permute-done((bf16[256,1024]{1,0:T(8,128)(2,1)S(1)}, bf16[256,1024]{1,0:T(8,128)(2,1)S(1)}, u32[]{:S(2)}, u32[]{:S(2)}) %collective-permute-start.16) | collective-permute-done | bytes 524320 | tf_op jit(solution)/shard_map/ppermute | solution.py:293
  82.8 1.5 %collective-permute-done.15.b = bf16[256,1024]{1,0:T(8,128)(2,1)S(1)} collective-permute-done((bf16[256,1024]{1,0:T(8,128)(2,1)S(1)}, bf16[256,1024]{1,0:T(8,128)(2,1)S(1)}, u32[]{:S(2)}, u32[]{:S(2)}) %collective-permute-start.15) | collective-permute-done | bytes 524320 | tf_op jit(solution)/shard_map/ppermute | solution.py:292
  84.3 2.0 %shard_map.54 = (bf16[256,1024]{1,0:T(8,128)(2,1)S(1)}, bf16[1024,1024]{1,0:T(8,128)(2,1)S(1)}) custom-call(s32[4]{0:T(128)S(1)} %copy-done.7, bf16[256,1024]{1,0:T(8,128)(2,1)S(1)} %get-tuple-element.42.a, bf16[256,1024]{1,0:T(8,128)(2,1)S(1)} %collective-permute-done.15.b, bf16[256,1024]{1,0:T(8,128)(2,1)S(1)} %collective-permute-done.16.c, ...), custom_call_target="tpu_custom_call" | custom-call | flops 1073741824 | bytes 8000000 | tf_op jit(solution)/shard_map/pallas_call | solution.py:313
  87.5 1.8 %collective-permute-start.23 = (bf16[256,1024]{1,0:T(8,128)(2,1)S(1)}, bf16[256,1024]{1,0:T(8,128)(2,1)S(1)}, u32[]{:S(2)}, u32[]{:S(2)}) collective-permute-start(bf16[256,1024]{1,0:T(8,128)(2,1)S(1)} %get-tuple-element.51.a), channel_id=1, source_target_pairs={{0,24},{8,0},{16,8},{24,16},{32,56},{40,32},{48,40},{56,48},{64,88... | collective-permute-start | bytes 1572872 | tf_op jit(solution)/shard_map/ppermute | solution.py:292
  89.3 2.3 %shard_map.55.s0 = bf16[1024,1024]{1,0:T(8,128)(2,1)S(1)} custom-call(bf16[1024,1024]{1,0:T(8,128)(2,1)S(1)} %get-tuple-element.52.rhs, bf16[2,1024,1024]{2,1,0:T(8,128)(2,1)S(1)} %copy-done.1), custom_call_target="tpu_custom_call" | custom-call | flops 2147483648 | bytes 6000000 | tf_op jit(solution)/shard_map/pallas_call | solution.py:324
  91.6 6.0 %shard_map.56.res = f32[2048,1024]{1,0:T(8,128)S(1)} custom-call(bf16[1024,1024]{1,0:T(8,128)(2,1)S(1)} %shard_map.55.s0, bf16[2048,2048]{1,0:T(8,128)(2,1)S(1)} %bitcast.15, f32[2048,1024]{1,0:T(8,128)S(1)} %shard_map.53.k), custom_call_target="tpu_custom_call", output_to_operand_aliasing={{}: (2, {})} | custom-call | flops 4294967296 | bytes 22000000 | tf_op jit(solution)/shard_map/pallas_call | solution.py:334
  97.7 1.3 %collective-permute-done.25.d = bf16[256,1024]{1,0:T(8,128)(2,1)S(1)} collective-permute-done((bf16[256,1024]{1,0:T(8,128)(2,1)S(1)}, bf16[256,1024]{1,0:T(8,128)(2,1)S(1)}, u32[]{:S(2)}, u32[]{:S(2)}) %collective-permute-start.25) | collective-permute-done | bytes 524320 | tf_op jit(solution)/shard_map/ppermute | solution.py:294
  99.5 1.5 %collective-permute-done.23.b = bf16[256,1024]{1,0:T(8,128)(2,1)S(1)} collective-permute-done((bf16[256,1024]{1,0:T(8,128)(2,1)S(1)}, bf16[256,1024]{1,0:T(8,128)(2,1)S(1)}, u32[]{:S(2)}, u32[]{:S(2)}) %collective-permute-start.23) | collective-permute-done | bytes 524320 | tf_op jit(solution)/shard_map/ppermute | solution.py:292
  101.1 6.8 %shard_map.57 = bf16[2048,1024]{1,0:T(8,128)(2,1)} custom-call(s32[4]{0:T(128)S(1)} %copy-done.7, bf16[256,1024]{1,0:T(8,128)(2,1)S(1)} %get-tuple-element.51.a, bf16[256,1024]{1,0:T(8,128)(2,1)S(1)} %collective-permute-done.23.b, bf16[256,1024]{1,0:T(8,128)(2,1)S(1)} %collective-permute-done.24.c, bf16[256,1024]{1,0:T(8,128)(2,1)S(1)} %collective-permute-done.25.d, ...), custom_call_target="tpu_custom_call" | custom-call | flops 4294967296 | bytes 18000000 | tf_op jit(solution)/shard_map/pallas_call | solution.py:349
  (72 shorter events, 12.3 us)
Async XLA Ops:
  3.5 18.6 %collective-permute-start = (bf16[1024,128]{1,0:T(8,128)(2,1)}, bf16[1024,128]{1,0:T(8,128)(2,1)S(1)}, u32[]{:S(2)}, u32[]{:S(2)}) collective-permute-start(bf16[1024,128]{1,0:T(8,128)(2,1)} %get-tuple-element.29), channel_id=1, source_target_pairs={{0,24},{8,0},{1,25},{9,1},{2,26},{10,2},{3,27},{11,3},{4,28},{12,4... | collective-permute-start | bytes 786440 | tf_op jit(solution)/shard_map/ppermute | solution.py:228
  4.8 17.3 %collective-permute-start.1 = (bf16[1024,128]{1,0:T(8,128)(2,1)}, bf16[1024,128]{1,0:T(8,128)(2,1)S(1)}, u32[]{:S(2)}, u32[]{:S(2)}) collective-permute-start(bf16[1024,128]{1,0:T(8,128)(2,1)} %get-tuple-element.30), channel_id=1, source_target_pairs={{0,16},{8,24},{1,17},{9,25},{2,18},{10,26},{3,19},{11,27},{4,20},{... | collective-permute-start | bytes 786440 | tf_op jit(solution)/shard_map/ppermute | solution.py:228
  6.1 16.0 %collective-permute-start.2 = (bf16[1024,128]{1,0:T(8,128)(2,1)}, bf16[1024,128]{1,0:T(8,128)(2,1)S(1)}, u32[]{:S(2)}, u32[]{:S(2)}) collective-permute-start(bf16[1024,128]{1,0:T(8,128)(2,1)} %get-tuple-element.31), channel_id=1, source_target_pairs={{0,8},{8,16},{1,9},{9,17},{2,10},{10,18},{3,11},{11,19},{4,12},{12... | collective-permute-start | bytes 786440 | tf_op jit(solution)/shard_map/ppermute | solution.py:228
  6.8 32.0 %collective-permute-start.7 = (bf16[2048,128]{1,0:T(8,128)(2,1)S(1)}, bf16[2048,128]{1,0:T(8,128)(2,1)}, u32[]{:S(2)}, u32[]{:S(2)}) collective-permute-start(bf16[2048,128]{1,0:T(8,128)(2,1)S(1)} %bitcast.18), channel_id=1, source_target_pairs={{0,6},{1,7},{2,0},{3,1},{4,2},{5,3},{6,4},{7,5},{8,14},{9,15},{10,... | collective-permute-start | bytes 1572872 | tf_op jit(solution)/shard_map/ppermute | solution.py:225
  10.9 27.9 %collective-permute-start.6 = (bf16[2048,128]{1,0:T(8,128)(2,1)S(1)}, bf16[2048,128]{1,0:T(8,128)(2,1)}, u32[]{:S(2)}, u32[]{:S(2)}) collective-permute-start(bf16[2048,128]{1,0:T(8,128)(2,1)S(1)} %bitcast.19), channel_id=1, source_target_pairs={{0,2},{1,3},{2,4},{3,5},{4,6},{5,7},{6,0},{7,1},{8,10},{9,11},{10,... | collective-permute-start | bytes 1572872 | tf_op jit(solution)/shard_map/ppermute | solution.py:225
  12.7 20.3 %all-to-all-start = ((bf16[16,64,256]{2,1,0:T(8,128)(2,1)}), bf16[16,64,256]{2,1,0:T(8,128)(2,1)S(1)}, u32[]{:S(2)}, u32[]{:S(2)}) async-start(bf16[16,64,256]{2,1,0:T(8,128)(2,1)} %shard_map.50), calls=%async_computation | async-start | bytes 1048576 | tf_op jit(solution)/shard_map/all_to_all | solution.py:219
  22.0 29.8 %copy-start.7 = (s32[4]{0:T(128)S(1)}, s32[4]{0:T(128)}, u32[]{:S(2)}) copy-start(s32[4]{0:T(128)} %pad_add_fusion.at) | copy-start | bytes 52
  23.2 15.4 %collective-permute-start.4 = (bf16[768,128]{1,0:T(8,128)(2,1)S(1)}, bf16[768,128]{1,0:T(8,128)(2,1)S(1)}, u32[]{:S(2)}, u32[]{:S(2)}) collective-permute-start(bf16[768,128]{1,0:T(8,128)(2,1)S(1)} %pad_maximum_fusion.1), channel_id=1, source_target_pairs={{0,64},{8,72},{16,80},{24,88},{1,65},{9,73},{17,81},{25,89},{2,66}... | collective-permute-start | bytes 589832 | tf_op jit(solution)/shard_map/ppermute | solution.py:237
  28.1 10.5 %collective-permute-start.5 = (bf16[768,128]{1,0:T(8,128)(2,1)S(1)}, bf16[768,128]{1,0:T(8,128)(2,1)S(1)}, u32[]{:S(2)}, u32[]{:S(2)}) collective-permute-start(bf16[768,128]{1,0:T(8,128)(2,1)S(1)} %pad_maximum_fusion), channel_id=1, source_target_pairs={{0,32},{8,40},{16,48},{24,56},{1,33},{9,41},{17,49},{25,57},{2,34}... | collective-permute-start | bytes 589832 | tf_op jit(solution)/shard_map/ppermute | solution.py:237
  29.4 9.2 %collective-permute-start.3 = (bf16[768,128]{1,0:T(8,128)(2,1)S(1)}, bf16[768,128]{1,0:T(8,128)(2,1)S(1)}, u32[]{:S(2)}, u32[]{:S(2)}) collective-permute-start(bf16[768,128]{1,0:T(8,128)(2,1)S(1)} %pad_maximum_fusion), channel_id=1, source_target_pairs={{0,96},{8,104},{16,112},{24,120},{1,97},{9,105},{17,113},{25,121},... | collective-permute-start | bytes 589832 | tf_op jit(solution)/shard_map/ppermute | solution.py:237
  33.8 28.6 %all-to-all-start.1 = ((bf16[16,64,768]{2,1,0:T(8,128)(2,1)}), bf16[16,64,768]{2,1,0:T(8,128)(2,1)S(1)}, u32[]{:S(2)}, u32[]{:S(2)}) async-start(bf16[16,64,768]{2,1,0:T(8,128)(2,1)} %shard_map.51), calls=%async_computation.1 | async-start | bytes 3145728 | tf_op jit(solution)/shard_map/all_to_all | solution.py:219
  38.6 15.8 %slice-start = ((s8[8388608]{0:T(1024)(128)(4,1)}), s8[4194304]{0:T(1024)(128)(4,1)S(1)}, s32[]{:S(2)}) async-start(s8[8388608]{0:T(1024)(128)(4,1)} %bitcast.10), calls=%async_computation.2 | async-start | bytes 8388608
  38.8 8.5 %collective-permute-start.10 = (bf16[768,128]{1,0:T(8,128)(2,1)S(1)}, bf16[768,128]{1,0:T(8,128)(2,1)S(1)}, u32[]{:S(2)}, u32[]{:S(2)}) collective-permute-start(bf16[768,128]{1,0:T(8,128)(2,1)S(1)} %select_select_fusion.2.p0), channel_id=1, source_target_pairs={{0,4},{1,5},{2,6},{3,7},{4,0},{5,1},{6,2},{7,3},{8,12},{9,13},{10,... | collective-permute-start | bytes 589832 | tf_op jit(solution)/shard_map/ppermute | solution.py:242
  40.7 8.9 %collective-permute-start.9 = (bf16[768,128]{1,0:T(8,128)(2,1)S(1)}, bf16[768,128]{1,0:T(8,128)(2,1)S(1)}, u32[]{:S(2)}, u32[]{:S(2)}) collective-permute-start(bf16[768,128]{1,0:T(8,128)(2,1)S(1)} %select_select_fusion.2.p0), channel_id=1, source_target_pairs={{0,6},{1,7},{2,0},{3,1},{4,2},{5,3},{6,4},{7,5},{8,14},{9,15},{10,... | collective-permute-start | bytes 589832 | tf_op jit(solution)/shard_map/ppermute | solution.py:242
  42.2 7.5 %collective-permute-start.8 = (bf16[768,128]{1,0:T(8,128)(2,1)S(1)}, bf16[768,128]{1,0:T(8,128)(2,1)S(1)}, u32[]{:S(2)}, u32[]{:S(2)}) collective-permute-start(bf16[768,128]{1,0:T(8,128)(2,1)S(1)} %select_select_fusion.2.p0), channel_id=1, source_target_pairs={{0,2},{1,3},{2,4},{3,5},{4,6},{5,7},{6,0},{7,1},{8,10},{9,11},{10,... | collective-permute-start | bytes 589832 | tf_op jit(solution)/shard_map/ppermute | solution.py:242
  43.0 8.8 %collective-permute-start.11 = (bf16[768,128]{1,0:T(8,128)(2,1)S(1)}, bf16[768,128]{1,0:T(8,128)(2,1)S(1)}, u32[]{:S(2)}, u32[]{:S(2)}) collective-permute-start(bf16[768,128]{1,0:T(8,128)(2,1)S(1)} %select_select_fusion.2.p0), channel_id=1, source_target_pairs={{0,1},{1,0},{2,3},{3,2},{4,5},{5,4},{6,7},{7,6},{8,9},{9,8},{10,11... | collective-permute-start | bytes 589832 | tf_op jit(solution)/shard_map/ppermute | solution.py:244
  47.3 4.5 %collective-permute-start.14 = (bf16[768,128]{1,0:T(8,128)(2,1)S(1)}, bf16[768,128]{1,0:T(8,128)(2,1)S(1)}, u32[]{:S(2)}, u32[]{:S(2)}) collective-permute-start(bf16[768,128]{1,0:T(8,128)(2,1)S(1)} %collective-permute-done.10.p3), channel_id=1, source_target_pairs={{0,1},{1,0},{2,3},{3,2},{4,5},{5,4},{6,7},{7,6},{8,9},{9,8},{10,11... | collective-permute-start | bytes 589832 | tf_op jit(solution)/shard_map/ppermute | solution.py:244
  49.6 2.1 %collective-permute-start.13 = (bf16[768,128]{1,0:T(8,128)(2,1)S(1)}, bf16[768,128]{1,0:T(8,128)(2,1)S(1)}, u32[]{:S(2)}, u32[]{:S(2)}) collective-permute-start(bf16[768,128]{1,0:T(8,128)(2,1)S(1)} %collective-permute-done.9.p2), channel_id=1, source_target_pairs={{0,1},{1,0},{2,3},{3,2},{4,5},{5,4},{6,7},{7,6},{8,9},{9,8},{10,11... | collective-permute-start | bytes 589832 | tf_op jit(solution)/shard_map/ppermute | solution.py:244
  49.6 2.1 %collective-permute-start.12 = (bf16[768,128]{1,0:T(8,128)(2,1)S(1)}, bf16[768,128]{1,0:T(8,128)(2,1)S(1)}, u32[]{:S(2)}, u32[]{:S(2)}) collective-permute-start(bf16[768,128]{1,0:T(8,128)(2,1)S(1)} %collective-permute-done.8.p1), channel_id=1, source_target_pairs={{0,1},{1,0},{2,3},{3,2},{4,5},{5,4},{6,7},{7,6},{8,9},{9,8},{10,11... | collective-permute-start | bytes 589832 | tf_op jit(solution)/shard_map/ppermute | solution.py:244
  50.2 15.8 %collective-permute-start.18 = (bf16[2048,128]{1,0:T(8,128)(2,1)S(1)}, bf16[2048,128]{1,0:T(8,128)(2,1)}, u32[]{:S(2)}, u32[]{:S(2)}) collective-permute-start(bf16[2048,128]{1,0:T(8,128)(2,1)S(1)} %bitcast.20), channel_id=1, source_target_pairs={{0,4},{1,5},{2,6},{3,7},{4,0},{5,1},{6,2},{7,3},{8,12},{9,13},{10,... | collective-permute-start | bytes 1572872 | tf_op jit(solution)/shard_map/ppermute | solution.py:243
  52.8 16.2 %collective-permute-start.19 = (bf16[2048,128]{1,0:T(8,128)(2,1)S(1)}, bf16[2048,128]{1,0:T(8,128)(2,1)}, u32[]{:S(2)}, u32[]{:S(2)}) collective-permute-start(bf16[2048,128]{1,0:T(8,128)(2,1)S(1)} %bitcast.21), channel_id=1, source_target_pairs={{0,1},{1,0},{2,3},{3,2},{4,5},{5,4},{6,7},{7,6},{8,9},{9,8},{10,11... | collective-permute-start | bytes 1572872 | tf_op jit(solution)/shard_map/ppermute | solution.py:298
  53.1 16.4 %collective-permute-start.20 = (bf16[2048,128]{1,0:T(8,128)(2,1)}, bf16[2048,128]{1,0:T(8,128)(2,1)}, u32[]{:S(2)}, u32[]{:S(2)}) collective-permute-start(bf16[2048,128]{1,0:T(8,128)(2,1)} %collective-permute-done.6.p1), channel_id=1, source_target_pairs={{0,1},{1,0},{2,3},{3,2},{4,5},{5,4},{6,7},{7,6},{8,9},{9,8},{10,11... | collective-permute-start | bytes 1572872 | tf_op jit(solution)/shard_map/ppermute | solution.py:298
  54.1 16.9 %collective-permute-start.21 = (bf16[2048,128]{1,0:T(8,128)(2,1)}, bf16[2048,128]{1,0:T(8,128)(2,1)}, u32[]{:S(2)}, u32[]{:S(2)}) collective-permute-start(bf16[2048,128]{1,0:T(8,128)(2,1)} %collective-permute-done.7.p2), channel_id=1, source_target_pairs={{0,1},{1,0},{2,3},{3,2},{4,5},{5,4},{6,7},{7,6},{8,9},{9,8},{10,11... | collective-permute-start | bytes 1572872 | tf_op jit(solution)/shard_map/ppermute | solution.py:298
  64.6 26.9 %slice-start.2 = ((s8[8388608]{0:T(1024)(128)(4,1)}), s8[4194304]{0:T(1024)(128)(4,1)S(1)}, s32[]{:S(2)}) async-start(s8[8388608]{0:T(1024)(128)(4,1)} %bitcast.13), calls=%async_computation.4 | async-start | bytes 8388608
  65.9 25.7 %slice-start.3 = ((s8[8388608]{0:T(1024)(128)(4,1)}), s8[4194304]{0:T(1024)(128)(4,1)S(1)}, s32[]{:S(2)}) async-start(s8[8388608]{0:T(1024)(128)(4,1)} %bitcast.13), calls=%async_computation.5 | async-start | bytes 8388608
  65.9 5.1 %collective-permute-start.22 = (bf16[2048,128]{1,0:T(8,128)(2,1)}, bf16[2048,128]{1,0:T(8,128)(2,1)S(1)}, u32[]{:S(2)}, u32[]{:S(2)}) collective-permute-start(bf16[2048,128]{1,0:T(8,128)(2,1)} %collective-permute-done.18.p3), channel_id=1, source_target_pairs={{0,1},{1,0},{2,3},{3,2},{4,5},{5,4},{6,7},{7,6},{8,9},{9,8},{10,11... | collective-permute-start | bytes 1572872 | tf_op jit(solution)/shard_map/ppermute | solution.py:298
  66.3 14.3 %collective-permute-start.17 = (bf16[256,1024]{1,0:T(8,128)(2,1)S(1)}, bf16[256,1024]{1,0:T(8,128)(2,1)S(1)}, u32[]{:S(2)}, u32[]{:S(2)}) collective-permute-start(bf16[256,1024]{1,0:T(8,128)(2,1)S(1)} %get-tuple-element.42.a), channel_id=1, source_target_pairs={{0,96},{8,104},{16,112},{24,120},{32,0},{40,8},{48,16},{56,24},{64... | collective-permute-start | bytes 1572872 | tf_op jit(solution)/shard_map/ppermute | solution.py:294
  69.0 13.8 %collective-permute-start.16 = (bf16[256,1024]{1,0:T(8,128)(2,1)S(1)}, bf16[256,1024]{1,0:T(8,128)(2,1)S(1)}, u32[]{:S(2)}, u32[]{:S(2)}) collective-permute-start(bf16[256,1024]{1,0:T(8,128)(2,1)S(1)} %get-tuple-element.42.a), channel_id=1, source_target_pairs={{0,8},{8,16},{16,24},{24,0},{32,40},{40,48},{48,56},{56,32},{64,72... | collective-permute-start | bytes 1572872 | tf_op jit(solution)/shard_map/ppermute | solution.py:293
  69.6 14.7 %collective-permute-start.15 = (bf16[256,1024]{1,0:T(8,128)(2,1)S(1)}, bf16[256,1024]{1,0:T(8,128)(2,1)S(1)}, u32[]{:S(2)}, u32[]{:S(2)}) collective-permute-start(bf16[256,1024]{1,0:T(8,128)(2,1)S(1)} %get-tuple-element.42.a), channel_id=1, source_target_pairs={{0,24},{8,0},{16,8},{24,16},{32,56},{40,32},{48,40},{56,48},{64,88... | collective-permute-start | bytes 1572872 | tf_op jit(solution)/shard_map/ppermute | solution.py:292
  86.3 12.7 %collective-permute-start.25 = (bf16[256,1024]{1,0:T(8,128)(2,1)S(1)}, bf16[256,1024]{1,0:T(8,128)(2,1)S(1)}, u32[]{:S(2)}, u32[]{:S(2)}) collective-permute-start(bf16[256,1024]{1,0:T(8,128)(2,1)S(1)} %get-tuple-element.51.a), channel_id=1, source_target_pairs={{0,96},{8,104},{16,112},{24,120},{32,0},{40,8},{48,16},{56,24},{64... | collective-permute-start | bytes 1572872 | tf_op jit(solution)/shard_map/ppermute | solution.py:294
  87.2 12.3 %collective-permute-start.24 = (bf16[256,1024]{1,0:T(8,128)(2,1)S(1)}, bf16[256,1024]{1,0:T(8,128)(2,1)S(1)}, u32[]{:S(2)}, u32[]{:S(2)}) collective-permute-start(bf16[256,1024]{1,0:T(8,128)(2,1)S(1)} %get-tuple-element.51.a), channel_id=1, source_target_pairs={{0,8},{8,16},{16,24},{24,0},{32,40},{40,48},{48,56},{56,32},{64,72... | collective-permute-start | bytes 1572872 | tf_op jit(solution)/shard_map/ppermute | solution.py:293
  87.5 13.6 %collective-permute-start.23 = (bf16[256,1024]{1,0:T(8,128)(2,1)S(1)}, bf16[256,1024]{1,0:T(8,128)(2,1)S(1)}, u32[]{:S(2)}, u32[]{:S(2)}) collective-permute-start(bf16[256,1024]{1,0:T(8,128)(2,1)S(1)} %get-tuple-element.51.a), channel_id=1, source_target_pairs={{0,24},{8,0},{16,8},{24,16},{32,56},{40,32},{48,40},{56,48},{64,88... | collective-permute-start | bytes 1572872 | tf_op jit(solution)/shard_map/ppermute | solution.py:292
  (10 other events, 63.3 us)

commit v7 on v6

--- a/solution.py
+++ b/solution.py
@@ -98,7 +98,15 @@
     return dots * dots
 
 
-def kernel_slices(feats, qa, qb, k0, k1):
+def kernel_slices(feats_hbm, qa_hbm, qb, k0, k1, feats, qa, sems):
+    copies = [
+        pltpu.make_async_copy(feats_hbm, feats, sems.at[0]),
+        pltpu.make_async_copy(qa_hbm, qa, sems.at[1]),
+    ]
+    for copy in copies:
+        copy.start()
+    for copy in copies:
+        copy.wait()
     n, start = k0.shape[0], 0
     for q in (qa, qb):
         cols = slice(start, start + q.shape[1])
@@ -250,7 +258,7 @@
     narrow = jax.ShapeDtypeStruct((quarter, width), BF16)
     slice_feats, low = pl.pallas_call(
         assemble,
-        out_shape=(jax.ShapeDtypeStruct((2 * quarter, feats), BF16), narrow),
+        out_shape=(pltpu.HBM((2 * quarter, feats), BF16), narrow),
         in_specs=[smem] + [whole()] * 8,
         out_specs=(whole(),) * 2,
         compiler_params=params(16),
@@ -268,7 +276,7 @@
     second = pl.pallas_call(
         through_second,
         grid=(blocks * width // BM,),
-        out_shape=jax.ShapeDtypeStruct((blocks * width, width), BF16),
+        out_shape=pltpu.HBM((blocks * width, width), BF16),
         in_specs=[smem, pl.BlockSpec((BM, width), lambda i: (i, 1)), block(1)],
         out_specs=pl.BlockSpec((BM, width), lambda i: (i, 0)),
         compiler_params=params(20),
@@ -280,8 +288,13 @@
             jax.ShapeDtypeStruct((quarter, queries), BF16),
             jax.ShapeDtypeStruct((quarter, queries), F32),
         ),
-        in_specs=[whole()] * 3,
+        in_specs=[pl.BlockSpec(memory_space=pltpu.HBM)] * 2 + [whole()],
         out_specs=(whole(), whole()),
+        scratch_shapes=[
+            pltpu.VMEM((2 * quarter, feats), BF16),
+            pltpu.VMEM((feats, first_part), BF16),
+            pltpu.SemaphoreType.DMA((2,)),
+        ],
         compiler_params=params(16),
         cost_estimate=cost(unit / 2, 5e6),
     )(after(slice_feats, high, second), qa, qb)

time: 109 us -> 108 us (level)
  Pallas kernels: 40.6 us -> 42.7 us
  local copies, waits for them, and re-layouts: 5.14 us -> 3.14 us
    unnamed x28 -> x24, local copies, waits for them, and re-layouts: 5.12 us -> 3.11 us
    pallas_call x2, Pallas kernels: 6.9 us -> 8.86 us  [the longest x1 6.86 us: per_device(): pl.pallas_call(through_second, grid=(blocks * width // BM,), out_shape=pl...]
  transfers between devices with their start and end apart: 28 -> 28, of which waited for: 8 -> 8; matrix products, arithmetic and copies ran while one was open for 1% -> 1% of each run, Pallas kernels for 27% -> 29%
where the time goes in v7:
time: 108 us
  starting transfers between devices  44.2 us (41%)
  Pallas kernels  42.7 us (40%)
  waiting for transfers between devices  15.7 us (15%)
  local copies, waits for them, and re-layouts  3.14 us (3%)
  other arithmetic  1.75 us (2%)
    all_to_all x2, starting transfers between devices, gather_queries(): lax.all_to_all(copies, 'rows', 0, 0, tiled=True).reshape(feats, count)  14.2 us
    pallas_call x1, Pallas kernels, per_device(): pl.pallas_call(kernel_rows, grid=(rows // bm,), out_shape=jax.ShapeDtypeS...  7.61 us
    ppermute x3, starting transfers between devices, per_device(): lax.ppermute(even if d == 2 else odd, 'rows', [(c, d * N + c) for c in ra...  7.54 us
    pallas_call x1, Pallas kernels, per_device(): pl.pallas_call(through_second, grid=(blocks * width // BM,), out_shape=pl...  6.86 us
    pallas_call x1, Pallas kernels, per_device(): pl.pallas_call(last_step, grid=(rows // bm,), out_shape=jax.ShapeDtypeStr...  6.84 us
    ppermute x3, waiting for transfers between devices, per_device(): slices = [mine] + [lax.ppermute(mine, 'pb', z_perm(d)) for d in (1, -1, 2)]  6.67 us
    pallas_call x1, Pallas kernels, per_device(): pl.pallas_call(update, grid=(rows // bm,), out_shape=jax.ShapeDtypeStruct...  6.04 us
    ppermute x3, starting transfers between devices, per_device(): slices = [mine] + [lax.ppermute(mine, 'pb', z_perm(d)) for d in (1, -1, 2)]  4.17 us
  transfers between devices with their start and end apart: 28, of which 8 were waited for; matrix products, arithmetic and copies ran while one was open for 1% of the time, Pallas kernels for 29%

profile of v7, /device:TPU:6, one launch (start us, length us, event | category | flops | bytes accessed | tf_op | source)
XLA Modules:
  0.0 107.9 jit_solution(4294067639071483321)
XLA Ops:
  0.6 2.9 %shard_map.46 = (bf16[1024,128]{1,0:T(8,128)(2,1)}, bf16[1024,128]{1,0:T(8,128)(2,1)}, bf16[1024,128]{1,0:T(8,128)(2,1)}, bf16[1024,128]{1,0:T(8,128)(2,1)}) custom-call(s32[4]{0:T(128)} %pad_add_fusion.at, bf16[2,1024,128]{2,1,0:T(8,128)(2,1)} %env.1, bf16[2,1024,2048]{2,1,0:T(8,128)(2,1)} %low.1), custom_call_target="tpu_custom_call" | custom-call | tf_op jit(solution)/shard_map/pallas_call | solution.py:200
  3.5 1.3 %collective-permute-start = (bf16[1024,128]{1,0:T(8,128)(2,1)}, bf16[1024,128]{1,0:T(8,128)(2,1)S(1)}, u32[]{:S(2)}, u32[]{:S(2)}) collective-permute-start(bf16[1024,128]{1,0:T(8,128)(2,1)} %get-tuple-element.29), channel_id=1, source_target_pairs={{0,24},{8,0},{1,25},{9,1},{2,26},{10,2},{3,27},{11,3},{4,28},{12,4... | collective-permute-start | bytes 786440 | tf_op jit(solution)/shard_map/ppermute | solution.py:236
  4.8 1.3 %collective-permute-start.1 = (bf16[1024,128]{1,0:T(8,128)(2,1)}, bf16[1024,128]{1,0:T(8,128)(2,1)S(1)}, u32[]{:S(2)}, u32[]{:S(2)}) collective-permute-start(bf16[1024,128]{1,0:T(8,128)(2,1)} %get-tuple-element.30), channel_id=1, source_target_pairs={{0,16},{8,24},{1,17},{9,25},{2,18},{10,26},{3,19},{11,27},{4,20},{... | collective-permute-start | bytes 786440 | tf_op jit(solution)/shard_map/ppermute | solution.py:236
  6.8 4.1 %collective-permute-start.7 = (bf16[2048,128]{1,0:T(8,128)(2,1)S(1)}, bf16[2048,128]{1,0:T(8,128)(2,1)}, u32[]{:S(2)}, u32[]{:S(2)}) collective-permute-start(bf16[2048,128]{1,0:T(8,128)(2,1)S(1)} %bitcast.18), channel_id=1, source_target_pairs={{0,6},{1,7},{2,0},{3,1},{4,2},{5,3},{6,4},{7,5},{8,14},{9,15},{10,... | collective-permute-start | bytes 1572872 | tf_op jit(solution)/shard_map/ppermute | solution.py:233
  10.9 1.8 %shard_map.50 = bf16[16,64,256]{2,1,0:T(8,128)(2,1)} custom-call(bf16[64,1024]{1,0:T(8,128)(2,1)} %bitcast.25), custom_call_target="tpu_custom_call" | custom-call | tf_op jit(solution)/shard_map/pallas_call | solution.py:219
  12.7 9.4 %all-to-all-start = ((bf16[16,64,256]{2,1,0:T(8,128)(2,1)}), bf16[16,64,256]{2,1,0:T(8,128)(2,1)S(1)}, u32[]{:S(2)}, u32[]{:S(2)}) async-start(bf16[16,64,256]{2,1,0:T(8,128)(2,1)} %shard_map.50), calls=%async_computation | async-start | bytes 1048576 | tf_op jit(solution)/shard_map/all_to_all | solution.py:227
  23.2 4.9 %collective-permute-start.4 = (bf16[768,128]{1,0:T(8,128)(2,1)S(1)}, bf16[768,128]{1,0:T(8,128)(2,1)S(1)}, u32[]{:S(2)}, u32[]{:S(2)}) collective-permute-start(bf16[768,128]{1,0:T(8,128)(2,1)S(1)} %pad_maximum_fusion.1), channel_id=1, source_target_pairs={{0,64},{8,72},{16,80},{24,88},{1,65},{9,73},{17,81},{25,89},{2,66}... | collective-permute-start | bytes 589832 | tf_op jit(solution)/shard_map/ppermute | solution.py:245
  28.1 1.3 %collective-permute-start.5 = (bf16[768,128]{1,0:T(8,128)(2,1)S(1)}, bf16[768,128]{1,0:T(8,128)(2,1)S(1)}, u32[]{:S(2)}, u32[]{:S(2)}) collective-permute-start(bf16[768,128]{1,0:T(8,128)(2,1)S(1)} %pad_maximum_fusion), channel_id=1, source_target_pairs={{0,32},{8,40},{16,48},{24,56},{1,33},{9,41},{17,49},{25,57},{2,34}... | collective-permute-start | bytes 589832 | tf_op jit(solution)/shard_map/ppermute | solution.py:245
  29.5 1.3 %collective-permute-start.3 = (bf16[768,128]{1,0:T(8,128)(2,1)S(1)}, bf16[768,128]{1,0:T(8,128)(2,1)S(1)}, u32[]{:S(2)}, u32[]{:S(2)}) collective-permute-start(bf16[768,128]{1,0:T(8,128)(2,1)S(1)} %pad_maximum_fusion), channel_id=1, source_target_pairs={{0,96},{8,104},{16,112},{24,120},{1,97},{9,105},{17,113},{25,121},... | collective-permute-start | bytes 589832 | tf_op jit(solution)/shard_map/ppermute | solution.py:245
  30.8 2.2 %shard_map.51 = bf16[16,64,768]{2,1,0:T(8,128)(2,1)} custom-call(bf16[64,1024]{1,0:T(8,128)(2,1)} %bitcast.26), custom_call_target="tpu_custom_call" | custom-call | tf_op jit(solution)/shard_map/pallas_call | solution.py:219
  33.8 4.8 %all-to-all-start.1 = ((bf16[16,64,768]{2,1,0:T(8,128)(2,1)}), bf16[16,64,768]{2,1,0:T(8,128)(2,1)S(1)}, u32[]{:S(2)}, u32[]{:S(2)}) async-start(bf16[16,64,768]{2,1,0:T(8,128)(2,1)} %shard_map.51), calls=%async_computation.1 | async-start | bytes 3145728 | tf_op jit(solution)/shard_map/all_to_all | solution.py:227
  38.8 1.9 %collective-permute-start.10 = (bf16[768,128]{1,0:T(8,128)(2,1)S(1)}, bf16[768,128]{1,0:T(8,128)(2,1)S(1)}, u32[]{:S(2)}, u32[]{:S(2)}) collective-permute-start(bf16[768,128]{1,0:T(8,128)(2,1)S(1)} %select_select_fusion.2.p0), channel_id=1, source_target_pairs={{0,4},{1,5},{2,6},{3,7},{4,0},{5,1},{6,2},{7,3},{8,12},{9,13},{10,... | collective-permute-start | bytes 589832 | tf_op jit(solution)/shard_map/ppermute | solution.py:250
  40.8 1.5 %collective-permute-start.9 = (bf16[768,128]{1,0:T(8,128)(2,1)S(1)}, bf16[768,128]{1,0:T(8,128)(2,1)S(1)}, u32[]{:S(2)}, u32[]{:S(2)}) collective-permute-start(bf16[768,128]{1,0:T(8,128)(2,1)S(1)} %select_select_fusion.2.p0), channel_id=1, source_target_pairs={{0,6},{1,7},{2,0},{3,1},{4,2},{5,3},{6,4},{7,5},{8,14},{9,15},{10,... | collective-permute-start | bytes 589832 | tf_op jit(solution)/shard_map/ppermute | solution.py:250
  43.0 4.3 %collective-permute-done.10.p3 = bf16[768,128]{1,0:T(8,128)(2,1)S(1)} collective-permute-done((bf16[768,128]{1,0:T(8,128)(2,1)S(1)}, bf16[768,128]{1,0:T(8,128)(2,1)S(1)}, u32[]{:S(2)}, u32[]{:S(2)}) %collective-permute-start.10) | collective-permute-done | bytes 196640 | tf_op jit(solution)/shard_map/ppermute | solution.py:250
  47.3 2.4 %collective-permute-done.9.p2 = bf16[768,128]{1,0:T(8,128)(2,1)S(1)} collective-permute-done((bf16[768,128]{1,0:T(8,128)(2,1)S(1)}, bf16[768,128]{1,0:T(8,128)(2,1)S(1)}, u32[]{:S(2)}, u32[]{:S(2)}) %collective-permute-start.9) | collective-permute-done | bytes 196640 | tf_op jit(solution)/shard_map/ppermute | solution.py:250
  50.2 1.6 %collective-permute-start.18 = (bf16[2048,128]{1,0:T(8,128)(2,1)S(1)}, bf16[2048,128]{1,0:T(8,128)(2,1)}, u32[]{:S(2)}, u32[]{:S(2)}) collective-permute-start(bf16[2048,128]{1,0:T(8,128)(2,1)S(1)} %bitcast.20), channel_id=1, source_target_pairs={{0,4},{1,5},{2,6},{3,7},{4,0},{5,1},{6,2},{7,3},{8,12},{9,13},{10,... | collective-permute-start | bytes 1572872 | tf_op jit(solution)/shard_map/ppermute | solution.py:251
  51.8 2.0 %shard_map.47 = (bf16[512,1024]{1,0:T(8,128)(2,1)}, bf16[256,1024]{1,0:T(8,128)(2,1)S(1)}) custom-call(s32[4]{0:T(128)S(1)} %copy-done.6, bf16[768,128]{1,0:T(8,128)(2,1)S(1)} %select_select_fusion.2.p0, bf16[768,128]{1,0:T(8,128)(2,1)S(1)} %collective-permute-done.8.p1, bf16[768,128]{1,0:T(8,128)(2,1)S(1)} %collective-permute-done.9.p2, ...), custom_call_target="tpu_custom_call" | custom-call | flops 6899999744 | bytes 22200000 | tf_op jit(solution)/shard_map/pallas_call | solution.py:259
  55.4 6.9 %shard_map.49.low = bf16[2048,1024]{1,0:T(8,128)(2,1)} custom-call(s32[4]{0:T(128)S(1)} %copy-done.6, bf16[2048,2048]{1,0:T(8,128)(2,1)S(1)} %bitcast.12, bf16[2,1024,1024]{2,1,0:T(8,128)(2,1)S(1)} %copy-done), custom_call_target="tpu_custom_call" | custom-call | flops 42949672 | bytes 200000 | tf_op jit(solution)/shard_map/pallas_call | solution.py:276
  64.5 1.4 %shard_map.52 = (bf16[256,1024]{1,0:T(8,128)(2,1)S(1)}, f32[256,1024]{1,0:T(8,128)S(1)}) custom-call(bf16[512,1024]{1,0:T(8,128)(2,1)S(1)} %copy-done.7, bf16[1024,256]{1,0:T(8,128)(2,1)S(1)} %bitcast.23, bf16[1024,768]{1,0:T(8,128)(2,1)S(1)} %bitcast.16), custom_call_target="tpu_custom_call" | custom-call | flops 1073741824 | bytes 5000000 | tf_op jit(solution)/shard_map/pallas_call | solution.py:285
  66.3 2.7 %collective-permute-start.17 = (bf16[256,1024]{1,0:T(8,128)(2,1)S(1)}, bf16[256,1024]{1,0:T(8,128)(2,1)S(1)}, u32[]{:S(2)}, u32[]{:S(2)}) collective-permute-start(bf16[256,1024]{1,0:T(8,128)(2,1)S(1)} %get-tuple-element.42.a), channel_id=1, source_target_pairs={{0,96},{8,104},{16,112},{24,120},{32,0},{40,8},{48,16},{56,24},{64... | collective-permute-start | bytes 1572872 | tf_op jit(solution)/shard_map/ppermute | solution.py:307
  69.5 1.5 %collective-permute-start.15 = (bf16[256,1024]{1,0:T(8,128)(2,1)S(1)}, bf16[256,1024]{1,0:T(8,128)(2,1)S(1)}, u32[]{:S(2)}, u32[]{:S(2)}) collective-permute-start(bf16[256,1024]{1,0:T(8,128)(2,1)S(1)} %get-tuple-element.42.a), channel_id=1, source_target_pairs={{0,24},{8,0},{16,8},{24,16},{32,56},{40,32},{48,40},{56,48},{64,88... | collective-permute-start | bytes 1572872 | tf_op jit(solution)/shard_map/ppermute | solution.py:305
  71.0 7.6 %shard_map.53.k = f32[2048,1024]{1,0:T(8,128)S(1)} custom-call(s32[4]{0:T(128)S(1)} %copy-done.6, bf16[1024,256]{1,0:T(8,128)(2,1)S(1)} %bitcast.24, bf16[1024,768]{1,0:T(8,128)(2,1)S(1)} %bitcast.17, bf16[2048,128]{1,0:T(8,128)(2,1)S(1)} %bitcast.22, bf16[2048,128]{1,0:T(8,128)(2,1)} %collective-permute-done.6.p1, ...), custom_call_target="tpu_custom_call" | custom-call | flops 4294967296 | bytes 14000000 | tf_op jit(solution)/shard_map/pallas_call | solution.py:316
  78.6 1.9 %collective-permute-done.17.d = bf16[256,1024]{1,0:T(8,128)(2,1)S(1)} collective-permute-done((bf16[256,1024]{1,0:T(8,128)(2,1)S(1)}, bf16[256,1024]{1,0:T(8,128)(2,1)S(1)}, u32[]{:S(2)}, u32[]{:S(2)}) %collective-permute-start.17) | collective-permute-done | bytes 524320 | tf_op jit(solution)/shard_map/ppermute | solution.py:307
  80.6 2.2 %collective-permute-done.16.c = bf16[256,1024]{1,0:T(8,128)(2,1)S(1)} collective-permute-done((bf16[256,1024]{1,0:T(8,128)(2,1)S(1)}, bf16[256,1024]{1,0:T(8,128)(2,1)S(1)}, u32[]{:S(2)}, u32[]{:S(2)}) %collective-permute-start.16) | collective-permute-done | bytes 524320 | tf_op jit(solution)/shard_map/ppermute | solution.py:306
  82.8 1.5 %collective-permute-done.15.b = bf16[256,1024]{1,0:T(8,128)(2,1)S(1)} collective-permute-done((bf16[256,1024]{1,0:T(8,128)(2,1)S(1)}, bf16[256,1024]{1,0:T(8,128)(2,1)S(1)}, u32[]{:S(2)}, u32[]{:S(2)}) %collective-permute-start.15) | collective-permute-done | bytes 524320 | tf_op jit(solution)/shard_map/ppermute | solution.py:305
  84.3 2.0 %shard_map.54 = (bf16[256,1024]{1,0:T(8,128)(2,1)S(1)}, bf16[1024,1024]{1,0:T(8,128)(2,1)S(1)}) custom-call(s32[4]{0:T(128)S(1)} %copy-done.6, bf16[256,1024]{1,0:T(8,128)(2,1)S(1)} %get-tuple-element.42.a, bf16[256,1024]{1,0:T(8,128)(2,1)S(1)} %collective-permute-done.15.b, bf16[256,1024]{1,0:T(8,128)(2,1)S(1)} %collective-permute-done.16.c, ...), custom_call_target="tpu_custom_call" | custom-call | flops 1073741824 | bytes 8000000 | tf_op jit(solution)/shard_map/pallas_call | solution.py:326
  87.5 1.7 %collective-permute-start.23 = (bf16[256,1024]{1,0:T(8,128)(2,1)S(1)}, bf16[256,1024]{1,0:T(8,128)(2,1)S(1)}, u32[]{:S(2)}, u32[]{:S(2)}) collective-permute-start(bf16[256,1024]{1,0:T(8,128)(2,1)S(1)} %get-tuple-element.51.a), channel_id=1, source_target_pairs={{0,24},{8,0},{16,8},{24,16},{32,56},{40,32},{48,40},{56,48},{64,88... | collective-permute-start | bytes 1572872 | tf_op jit(solution)/shard_map/ppermute | solution.py:305
  89.2 2.3 %shard_map.55.s0 = bf16[1024,1024]{1,0:T(8,128)(2,1)S(1)} custom-call(bf16[1024,1024]{1,0:T(8,128)(2,1)S(1)} %get-tuple-element.52.rhs, bf16[2,1024,1024]{2,1,0:T(8,128)(2,1)S(1)} %copy-done.1), custom_call_target="tpu_custom_call" | custom-call | flops 2147483648 | bytes 6000000 | tf_op jit(solution)/shard_map/pallas_call | solution.py:337
  91.6 6.0 %shard_map.56.res = f32[2048,1024]{1,0:T(8,128)S(1)} custom-call(bf16[1024,1024]{1,0:T(8,128)(2,1)S(1)} %shard_map.55.s0, bf16[2048,2048]{1,0:T(8,128)(2,1)S(1)} %bitcast.15, f32[2048,1024]{1,0:T(8,128)S(1)} %shard_map.53.k), custom_call_target="tpu_custom_call", output_to_operand_aliasing={{}: (2, {})} | custom-call | flops 4294967296 | bytes 22000000 | tf_op jit(solution)/shard_map/pallas_call | solution.py:347
  97.6 1.3 %collective-permute-done.25.d = bf16[256,1024]{1,0:T(8,128)(2,1)S(1)} collective-permute-done((bf16[256,1024]{1,0:T(8,128)(2,1)S(1)}, bf16[256,1024]{1,0:T(8,128)(2,1)S(1)}, u32[]{:S(2)}, u32[]{:S(2)}) %collective-permute-start.25) | collective-permute-done | bytes 524320 | tf_op jit(solution)/shard_map/ppermute | solution.py:307
  99.5 1.5 %collective-permute-done.23.b = bf16[256,1024]{1,0:T(8,128)(2,1)S(1)} collective-permute-done((bf16[256,1024]{1,0:T(8,128)(2,1)S(1)}, bf16[256,1024]{1,0:T(8,128)(2,1)S(1)}, u32[]{:S(2)}, u32[]{:S(2)}) %collective-permute-start.23) | collective-permute-done | bytes 524320 | tf_op jit(solution)/shard_map/ppermute | solution.py:305
  101.1 6.8 %shard_map.57 = bf16[2048,1024]{1,0:T(8,128)(2,1)} custom-call(s32[4]{0:T(128)S(1)} %copy-done.6, bf16[256,1024]{1,0:T(8,128)(2,1)S(1)} %get-tuple-element.51.a, bf16[256,1024]{1,0:T(8,128)(2,1)S(1)} %collective-permute-done.23.b, bf16[256,1024]{1,0:T(8,128)(2,1)S(1)} %collective-permute-done.24.c, bf16[256,1024]{1,0:T(8,128)(2,1)S(1)} %collective-permute-done.25.d, ...), custom_call_target="tpu_custom_call" | custom-call | flops 4294967296 | bytes 18000000 | tf_op jit(solution)/shard_map/pallas_call | solution.py:362
  (68 shorter events, 11.1 us)
Async XLA Ops:
  3.5 18.6 %collective-permute-start = (bf16[1024,128]{1,0:T(8,128)(2,1)}, bf16[1024,128]{1,0:T(8,128)(2,1)S(1)}, u32[]{:S(2)}, u32[]{:S(2)}) collective-permute-start(bf16[1024,128]{1,0:T(8,128)(2,1)} %get-tuple-element.29), channel_id=1, source_target_pairs={{0,24},{8,0},{1,25},{9,1},{2,26},{10,2},{3,27},{11,3},{4,28},{12,4... | collective-permute-start | bytes 786440 | tf_op jit(solution)/shard_map/ppermute | solution.py:236
  4.8 17.3 %collective-permute-start.1 = (bf16[1024,128]{1,0:T(8,128)(2,1)}, bf16[1024,128]{1,0:T(8,128)(2,1)S(1)}, u32[]{:S(2)}, u32[]{:S(2)}) collective-permute-start(bf16[1024,128]{1,0:T(8,128)(2,1)} %get-tuple-element.30), channel_id=1, source_target_pairs={{0,16},{8,24},{1,17},{9,25},{2,18},{10,26},{3,19},{11,27},{4,20},{... | collective-permute-start | bytes 786440 | tf_op jit(solution)/shard_map/ppermute | solution.py:236
  6.1 16.0 %collective-permute-start.2 = (bf16[1024,128]{1,0:T(8,128)(2,1)}, bf16[1024,128]{1,0:T(8,128)(2,1)S(1)}, u32[]{:S(2)}, u32[]{:S(2)}) collective-permute-start(bf16[1024,128]{1,0:T(8,128)(2,1)} %get-tuple-element.31), channel_id=1, source_target_pairs={{0,8},{8,16},{1,9},{9,17},{2,10},{10,18},{3,11},{11,19},{4,12},{12... | collective-permute-start | bytes 786440 | tf_op jit(solution)/shard_map/ppermute | solution.py:236
  6.8 32.0 %collective-permute-start.7 = (bf16[2048,128]{1,0:T(8,128)(2,1)S(1)}, bf16[2048,128]{1,0:T(8,128)(2,1)}, u32[]{:S(2)}, u32[]{:S(2)}) collective-permute-start(bf16[2048,128]{1,0:T(8,128)(2,1)S(1)} %bitcast.18), channel_id=1, source_target_pairs={{0,6},{1,7},{2,0},{3,1},{4,2},{5,3},{6,4},{7,5},{8,14},{9,15},{10,... | collective-permute-start | bytes 1572872 | tf_op jit(solution)/shard_map/ppermute | solution.py:233
  10.9 27.9 %collective-permute-start.6 = (bf16[2048,128]{1,0:T(8,128)(2,1)S(1)}, bf16[2048,128]{1,0:T(8,128)(2,1)}, u32[]{:S(2)}, u32[]{:S(2)}) collective-permute-start(bf16[2048,128]{1,0:T(8,128)(2,1)S(1)} %bitcast.19), channel_id=1, source_target_pairs={{0,2},{1,3},{2,4},{3,5},{4,6},{5,7},{6,0},{7,1},{8,10},{9,11},{10,... | collective-permute-start | bytes 1572872 | tf_op jit(solution)/shard_map/ppermute | solution.py:233
  12.7 20.3 %all-to-all-start = ((bf16[16,64,256]{2,1,0:T(8,128)(2,1)}), bf16[16,64,256]{2,1,0:T(8,128)(2,1)S(1)}, u32[]{:S(2)}, u32[]{:S(2)}) async-start(bf16[16,64,256]{2,1,0:T(8,128)(2,1)} %shard_map.50), calls=%async_computation | async-start | bytes 1048576 | tf_op jit(solution)/shard_map/all_to_all | solution.py:227
  22.0 29.8 %copy-start.6 = (s32[4]{0:T(128)S(1)}, s32[4]{0:T(128)}, u32[]{:S(2)}) copy-start(s32[4]{0:T(128)} %pad_add_fusion.at) | copy-start | bytes 52
  23.2 15.4 %collective-permute-start.4 = (bf16[768,128]{1,0:T(8,128)(2,1)S(1)}, bf16[768,128]{1,0:T(8,128)(2,1)S(1)}, u32[]{:S(2)}, u32[]{:S(2)}) collective-permute-start(bf16[768,128]{1,0:T(8,128)(2,1)S(1)} %pad_maximum_fusion.1), channel_id=1, source_target_pairs={{0,64},{8,72},{16,80},{24,88},{1,65},{9,73},{17,81},{25,89},{2,66}... | collective-permute-start | bytes 589832 | tf_op jit(solution)/shard_map/ppermute | solution.py:245
  28.1 10.5 %collective-permute-start.5 = (bf16[768,128]{1,0:T(8,128)(2,1)S(1)}, bf16[768,128]{1,0:T(8,128)(2,1)S(1)}, u32[]{:S(2)}, u32[]{:S(2)}) collective-permute-start(bf16[768,128]{1,0:T(8,128)(2,1)S(1)} %pad_maximum_fusion), channel_id=1, source_target_pairs={{0,32},{8,40},{16,48},{24,56},{1,33},{9,41},{17,49},{25,57},{2,34}... | collective-permute-start | bytes 589832 | tf_op jit(solution)/shard_map/ppermute | solution.py:245
  29.5 9.2 %collective-permute-start.3 = (bf16[768,128]{1,0:T(8,128)(2,1)S(1)}, bf16[768,128]{1,0:T(8,128)(2,1)S(1)}, u32[]{:S(2)}, u32[]{:S(2)}) collective-permute-start(bf16[768,128]{1,0:T(8,128)(2,1)S(1)} %pad_maximum_fusion), channel_id=1, source_target_pairs={{0,96},{8,104},{16,112},{24,120},{1,97},{9,105},{17,113},{25,121},... | collective-permute-start | bytes 589832 | tf_op jit(solution)/shard_map/ppermute | solution.py:245
  33.8 28.4 %all-to-all-start.1 = ((bf16[16,64,768]{2,1,0:T(8,128)(2,1)}), bf16[16,64,768]{2,1,0:T(8,128)(2,1)S(1)}, u32[]{:S(2)}, u32[]{:S(2)}) async-start(bf16[16,64,768]{2,1,0:T(8,128)(2,1)} %shard_map.51), calls=%async_computation.1 | async-start | bytes 3145728 | tf_op jit(solution)/shard_map/all_to_all | solution.py:227
  38.6 16.7 %slice-start = ((s8[8388608]{0:T(1024)(128)(4,1)}), s8[4194304]{0:T(1024)(128)(4,1)S(1)}, s32[]{:S(2)}) async-start(s8[8388608]{0:T(1024)(128)(4,1)} %bitcast.10), calls=%async_computation.2 | async-start | bytes 8388608
  38.8 8.5 %collective-permute-start.10 = (bf16[768,128]{1,0:T(8,128)(2,1)S(1)}, bf16[768,128]{1,0:T(8,128)(2,1)S(1)}, u32[]{:S(2)}, u32[]{:S(2)}) collective-permute-start(bf16[768,128]{1,0:T(8,128)(2,1)S(1)} %select_select_fusion.2.p0), channel_id=1, source_target_pairs={{0,4},{1,5},{2,6},{3,7},{4,0},{5,1},{6,2},{7,3},{8,12},{9,13},{10,... | collective-permute-start | bytes 589832 | tf_op jit(solution)/shard_map/ppermute | solution.py:250
  40.8 8.9 %collective-permute-start.9 = (bf16[768,128]{1,0:T(8,128)(2,1)S(1)}, bf16[768,128]{1,0:T(8,128)(2,1)S(1)}, u32[]{:S(2)}, u32[]{:S(2)}) collective-permute-start(bf16[768,128]{1,0:T(8,128)(2,1)S(1)} %select_select_fusion.2.p0), channel_id=1, source_target_pairs={{0,6},{1,7},{2,0},{3,1},{4,2},{5,3},{6,4},{7,5},{8,14},{9,15},{10,... | collective-permute-start | bytes 589832 | tf_op jit(solution)/shard_map/ppermute | solution.py:250
  42.2 7.5 %collective-permute-start.8 = (bf16[768,128]{1,0:T(8,128)(2,1)S(1)}, bf16[768,128]{1,0:T(8,128)(2,1)S(1)}, u32[]{:S(2)}, u32[]{:S(2)}) collective-permute-start(bf16[768,128]{1,0:T(8,128)(2,1)S(1)} %select_select_fusion.2.p0), channel_id=1, source_target_pairs={{0,2},{1,3},{2,4},{3,5},{4,6},{5,7},{6,0},{7,1},{8,10},{9,11},{10,... | collective-permute-start | bytes 589832 | tf_op jit(solution)/shard_map/ppermute | solution.py:250
  43.0 8.8 %collective-permute-start.11 = (bf16[768,128]{1,0:T(8,128)(2,1)S(1)}, bf16[768,128]{1,0:T(8,128)(2,1)S(1)}, u32[]{:S(2)}, u32[]{:S(2)}) collective-permute-start(bf16[768,128]{1,0:T(8,128)(2,1)S(1)} %select_select_fusion.2.p0), channel_id=1, source_target_pairs={{0,1},{1,0},{2,3},{3,2},{4,5},{5,4},{6,7},{7,6},{8,9},{9,8},{10,11... | collective-permute-start | bytes 589832 | tf_op jit(solution)/shard_map/ppermute | solution.py:252
  47.3 4.5 %collective-permute-start.14 = (bf16[768,128]{1,0:T(8,128)(2,1)S(1)}, bf16[768,128]{1,0:T(8,128)(2,1)S(1)}, u32[]{:S(2)}, u32[]{:S(2)}) collective-permute-start(bf16[768,128]{1,0:T(8,128)(2,1)S(1)} %collective-permute-done.10.p3), channel_id=1, source_target_pairs={{0,1},{1,0},{2,3},{3,2},{4,5},{5,4},{6,7},{7,6},{8,9},{9,8},{10,11... | collective-permute-start | bytes 589832 | tf_op jit(solution)/shard_map/ppermute | solution.py:252
  49.7 2.1 %collective-permute-start.13 = (bf16[768,128]{1,0:T(8,128)(2,1)S(1)}, bf16[768,128]{1,0:T(8,128)(2,1)S(1)}, u32[]{:S(2)}, u32[]{:S(2)}) collective-permute-start(bf16[768,128]{1,0:T(8,128)(2,1)S(1)} %collective-permute-done.9.p2), channel_id=1, source_target_pairs={{0,1},{1,0},{2,3},{3,2},{4,5},{5,4},{6,7},{7,6},{8,9},{9,8},{10,11... | collective-permute-start | bytes 589832 | tf_op jit(solution)/shard_map/ppermute | solution.py:252
  49.7 2.1 %collective-permute-start.12 = (bf16[768,128]{1,0:T(8,128)(2,1)S(1)}, bf16[768,128]{1,0:T(8,128)(2,1)S(1)}, u32[]{:S(2)}, u32[]{:S(2)}) collective-permute-start(bf16[768,128]{1,0:T(8,128)(2,1)S(1)} %collective-permute-done.8.p1), channel_id=1, source_target_pairs={{0,1},{1,0},{2,3},{3,2},{4,5},{5,4},{6,7},{7,6},{8,9},{9,8},{10,11... | collective-permute-start | bytes 589832 | tf_op jit(solution)/shard_map/ppermute | solution.py:252
  50.2 15.7 %collective-permute-start.18 = (bf16[2048,128]{1,0:T(8,128)(2,1)S(1)}, bf16[2048,128]{1,0:T(8,128)(2,1)}, u32[]{:S(2)}, u32[]{:S(2)}) collective-permute-start(bf16[2048,128]{1,0:T(8,128)(2,1)S(1)} %bitcast.20), channel_id=1, source_target_pairs={{0,4},{1,5},{2,6},{3,7},{4,0},{5,1},{6,2},{7,3},{8,12},{9,13},{10,... | collective-permute-start | bytes 1572872 | tf_op jit(solution)/shard_map/ppermute | solution.py:251
  53.8 15.2 %collective-permute-start.19 = (bf16[2048,128]{1,0:T(8,128)(2,1)S(1)}, bf16[2048,128]{1,0:T(8,128)(2,1)}, u32[]{:S(2)}, u32[]{:S(2)}) collective-permute-start(bf16[2048,128]{1,0:T(8,128)(2,1)S(1)} %bitcast.21), channel_id=1, source_target_pairs={{0,1},{1,0},{2,3},{3,2},{4,5},{5,4},{6,7},{7,6},{8,9},{9,8},{10,11... | collective-permute-start | bytes 1572872 | tf_op jit(solution)/shard_map/ppermute | solution.py:311
  54.1 15.5 %collective-permute-start.20 = (bf16[2048,128]{1,0:T(8,128)(2,1)}, bf16[2048,128]{1,0:T(8,128)(2,1)}, u32[]{:S(2)}, u32[]{:S(2)}) collective-permute-start(bf16[2048,128]{1,0:T(8,128)(2,1)} %collective-permute-done.6.p1), channel_id=1, source_target_pairs={{0,1},{1,0},{2,3},{3,2},{4,5},{5,4},{6,7},{7,6},{8,9},{9,8},{10,11... | collective-permute-start | bytes 1572872 | tf_op jit(solution)/shard_map/ppermute | solution.py:311
  55.1 16.0 %collective-permute-start.21 = (bf16[2048,128]{1,0:T(8,128)(2,1)}, bf16[2048,128]{1,0:T(8,128)(2,1)}, u32[]{:S(2)}, u32[]{:S(2)}) collective-permute-start(bf16[2048,128]{1,0:T(8,128)(2,1)} %collective-permute-done.7.p2), channel_id=1, source_target_pairs={{0,1},{1,0},{2,3},{3,2},{4,5},{5,4},{6,7},{7,6},{8,9},{9,8},{10,11... | collective-permute-start | bytes 1572872 | tf_op jit(solution)/shard_map/ppermute | solution.py:311
  64.5 27.1 %slice-start.2 = ((s8[8388608]{0:T(1024)(128)(4,1)}), s8[4194304]{0:T(1024)(128)(4,1)S(1)}, s32[]{:S(2)}) async-start(s8[8388608]{0:T(1024)(128)(4,1)} %bitcast.13), calls=%async_computation.4 | async-start | bytes 8388608
  65.9 25.7 %slice-start.3 = ((s8[8388608]{0:T(1024)(128)(4,1)}), s8[4194304]{0:T(1024)(128)(4,1)S(1)}, s32[]{:S(2)}) async-start(s8[8388608]{0:T(1024)(128)(4,1)} %bitcast.13), calls=%async_computation.5 | async-start | bytes 8388608
  65.9 5.1 %collective-permute-start.22 = (bf16[2048,128]{1,0:T(8,128)(2,1)}, bf16[2048,128]{1,0:T(8,128)(2,1)S(1)}, u32[]{:S(2)}, u32[]{:S(2)}) collective-permute-start(bf16[2048,128]{1,0:T(8,128)(2,1)} %collective-permute-done.18.p3), channel_id=1, source_target_pairs={{0,1},{1,0},{2,3},{3,2},{4,5},{5,4},{6,7},{7,6},{8,9},{9,8},{10,11... | collective-permute-start | bytes 1572872 | tf_op jit(solution)/shard_map/ppermute | solution.py:311
  66.3 14.3 %collective-permute-start.17 = (bf16[256,1024]{1,0:T(8,128)(2,1)S(1)}, bf16[256,1024]{1,0:T(8,128)(2,1)S(1)}, u32[]{:S(2)}, u32[]{:S(2)}) collective-permute-start(bf16[256,1024]{1,0:T(8,128)(2,1)S(1)} %get-tuple-element.42.a), channel_id=1, source_target_pairs={{0,96},{8,104},{16,112},{24,120},{32,0},{40,8},{48,16},{56,24},{64... | collective-permute-start | bytes 1572872 | tf_op jit(solution)/shard_map/ppermute | solution.py:307
  69.0 13.8 %collective-permute-start.16 = (bf16[256,1024]{1,0:T(8,128)(2,1)S(1)}, bf16[256,1024]{1,0:T(8,128)(2,1)S(1)}, u32[]{:S(2)}, u32[]{:S(2)}) collective-permute-start(bf16[256,1024]{1,0:T(8,128)(2,1)S(1)} %get-tuple-element.42.a), channel_id=1, source_target_pairs={{0,8},{8,16},{16,24},{24,0},{32,40},{40,48},{48,56},{56,32},{64,72... | collective-permute-start | bytes 1572872 | tf_op jit(solution)/shard_map/ppermute | solution.py:306
  69.5 14.7 %collective-permute-start.15 = (bf16[256,1024]{1,0:T(8,128)(2,1)S(1)}, bf16[256,1024]{1,0:T(8,128)(2,1)S(1)}, u32[]{:S(2)}, u32[]{:S(2)}) collective-permute-start(bf16[256,1024]{1,0:T(8,128)(2,1)S(1)} %get-tuple-element.42.a), channel_id=1, source_target_pairs={{0,24},{8,0},{16,8},{24,16},{32,56},{40,32},{48,40},{56,48},{64,88... | collective-permute-start | bytes 1572872 | tf_op jit(solution)/shard_map/ppermute | solution.py:305
  86.3 12.7 %collective-permute-start.25 = (bf16[256,1024]{1,0:T(8,128)(2,1)S(1)}, bf16[256,1024]{1,0:T(8,128)(2,1)S(1)}, u32[]{:S(2)}, u32[]{:S(2)}) collective-permute-start(bf16[256,1024]{1,0:T(8,128)(2,1)S(1)} %get-tuple-element.51.a), channel_id=1, source_target_pairs={{0,96},{8,104},{16,112},{24,120},{32,0},{40,8},{48,16},{56,24},{64... | collective-permute-start | bytes 1572872 | tf_op jit(solution)/shard_map/ppermute | solution.py:307
  87.2 12.3 %collective-permute-start.24 = (bf16[256,1024]{1,0:T(8,128)(2,1)S(1)}, bf16[256,1024]{1,0:T(8,128)(2,1)S(1)}, u32[]{:S(2)}, u32[]{:S(2)}) collective-permute-start(bf16[256,1024]{1,0:T(8,128)(2,1)S(1)} %get-tuple-element.51.a), channel_id=1, source_target_pairs={{0,8},{8,16},{16,24},{24,0},{32,40},{40,48},{48,56},{56,32},{64,72... | collective-permute-start | bytes 1572872 | tf_op jit(solution)/shard_map/ppermute | solution.py:306
  87.5 13.6 %collective-permute-start.23 = (bf16[256,1024]{1,0:T(8,128)(2,1)S(1)}, bf16[256,1024]{1,0:T(8,128)(2,1)S(1)}, u32[]{:S(2)}, u32[]{:S(2)}) collective-permute-start(bf16[256,1024]{1,0:T(8,128)(2,1)S(1)} %get-tuple-element.51.a), channel_id=1, source_target_pairs={{0,24},{8,0},{16,8},{24,16},{32,56},{40,32},{48,40},{56,48},{64,88... | collective-permute-start | bytes 1572872 | tf_op jit(solution)/shard_map/ppermute | solution.py:305
  (8 other events, 61.5 us)

commit v8 on v6

--- a/solution.py
+++ b/solution.py
@@ -205,7 +205,7 @@
     )(at, sparse_desc, lower_panel)
 
     own_q = query_desc.T
-    first_part = queries // 4
+    first_part = queries // 8
 
     def gather_queries(start, count, source):
         copies = pl.pallas_call(
@@ -254,7 +254,7 @@
         in_specs=[smem] + [whole()] * 8,
         out_specs=(whole(),) * 2,
         compiler_params=params(16),
-        cost_estimate=cost(6900000000, 22200000),
+        cost_estimate=cost(9200000000, 29600000),
     )(at, *slices)
     high, rest = pl.pallas_call(
         through_first,

time: 109 us -> 108 us (level)
  Pallas kernels: 40.6 us -> 42 us
  transfers between devices with their start and end apart: 28 -> 28, of which waited for: 8 -> 8; matrix products, arithmetic and copies ran while one was open for 1% -> 1% of each run, Pallas kernels for 27% -> 28%
where the time goes in v8:
time: 108 us
  starting transfers between devices  43.9 us (41%)
  Pallas kernels  42 us (39%)
  waiting for transfers between devices  14.7 us (14%)
  local copies, waits for them, and re-layouts  4.96 us (5%)
  other arithmetic  1.81 us (2%)
    all_to_all x2, starting transfers between devices, gather_queries(): lax.all_to_all(copies, 'rows', 0, 0, tiled=True).reshape(feats, count)  14.1 us
    pallas_call x1, Pallas kernels, per_device(): pl.pallas_call(kernel_rows, grid=(rows // bm,), out_shape=jax.ShapeDtypeS...  8.67 us
    ppermute x3, starting transfers between devices, per_device(): lax.ppermute(even if d == 2 else odd, 'rows', [(c, d * N + c) for c in ra...  7.54 us
    pallas_call x1, Pallas kernels, per_device(): pl.pallas_call(last_step, grid=(rows // bm,), out_shape=jax.ShapeDtypeStr...  6.84 us
    ppermute x3, waiting for transfers between devices, per_device(): slices = [mine] + [lax.ppermute(mine, 'pb', z_perm(d)) for d in (1, -1, 2)]  6.67 us
    pallas_call x1, Pallas kernels, per_device(): pl.pallas_call(update, grid=(rows // bm,), out_shape=jax.ShapeDtypeStruct...  6.04 us
    pallas_call x1, Pallas kernels, per_device(): pl.pallas_call(through_second, grid=(blocks * width // BM,), out_shape=ja...  5.89 us
    unnamed x28, local copies, waits for them, and re-layouts  4.93 us
  transfers between devices with their start and end apart: 28, of which 8 were waited for; matrix products, arithmetic and copies ran while one was open for 1% of the time, Pallas kernels for 28%

profile of v8, /device:TPU:6, one launch (start us, length us, event | category | flops | bytes accessed | tf_op | source)
XLA Modules:
  0.0 107.7 jit_solution(8950206443506094646)
XLA Ops:
  0.6 2.8 %shard_map.46 = (bf16[1024,128]{1,0:T(8,128)(2,1)}, bf16[1024,128]{1,0:T(8,128)(2,1)}, bf16[1024,128]{1,0:T(8,128)(2,1)}, bf16[1024,128]{1,0:T(8,128)(2,1)}) custom-call(s32[4]{0:T(128)} %pad_add_fusion.at, bf16[2,1024,128]{2,1,0:T(8,128)(2,1)} %env.1, bf16[2,1024,2048]{2,1,0:T(8,128)(2,1)} %low.1), custom_call_target="tpu_custom_call" | custom-call | tf_op jit(solution)/shard_map/pallas_call | solution.py:192
  3.5 1.3 %collective-permute-start = (bf16[1024,128]{1,0:T(8,128)(2,1)}, bf16[1024,128]{1,0:T(8,128)(2,1)S(1)}, u32[]{:S(2)}, u32[]{:S(2)}) collective-permute-start(bf16[1024,128]{1,0:T(8,128)(2,1)} %get-tuple-element.29), channel_id=1, source_target_pairs={{0,24},{8,0},{1,25},{9,1},{2,26},{10,2},{3,27},{11,3},{4,28},{12,4... | collective-permute-start | bytes 786440 | tf_op jit(solution)/shard_map/ppermute | solution.py:228
  4.8 1.3 %collective-permute-start.1 = (bf16[1024,128]{1,0:T(8,128)(2,1)}, bf16[1024,128]{1,0:T(8,128)(2,1)S(1)}, u32[]{:S(2)}, u32[]{:S(2)}) collective-permute-start(bf16[1024,128]{1,0:T(8,128)(2,1)} %get-tuple-element.30), channel_id=1, source_target_pairs={{0,16},{8,24},{1,17},{9,25},{2,18},{10,26},{3,19},{11,27},{4,20},{... | collective-permute-start | bytes 786440 | tf_op jit(solution)/shard_map/ppermute | solution.py:228
  6.8 4.1 %collective-permute-start.7 = (bf16[2048,128]{1,0:T(8,128)(2,1)S(1)}, bf16[2048,128]{1,0:T(8,128)(2,1)}, u32[]{:S(2)}, u32[]{:S(2)}) collective-permute-start(bf16[2048,128]{1,0:T(8,128)(2,1)S(1)} %bitcast.18), channel_id=1, source_target_pairs={{0,6},{1,7},{2,0},{3,1},{4,2},{5,3},{6,4},{7,5},{8,14},{9,15},{10,... | collective-permute-start | bytes 1572872 | tf_op jit(solution)/shard_map/ppermute | solution.py:225
  10.9 1.7 %shard_map.50 = bf16[16,64,128]{2,1,0:T(8,128)(2,1)} custom-call(bf16[64,1024]{1,0:T(8,128)(2,1)} %bitcast.25), custom_call_target="tpu_custom_call" | custom-call | tf_op jit(solution)/shard_map/pallas_call | solution.py:211
  12.6 9.3 %all-to-all-start = ((bf16[16,64,128]{2,1,0:T(8,128)(2,1)}), bf16[16,64,128]{2,1,0:T(8,128)(2,1)S(1)}, u32[]{:S(2)}, u32[]{:S(2)}) async-start(bf16[16,64,128]{2,1,0:T(8,128)(2,1)} %shard_map.50), calls=%async_computation | async-start | bytes 524288 | tf_op jit(solution)/shard_map/all_to_all | solution.py:219
  23.1 4.9 %collective-permute-start.4 = (bf16[768,128]{1,0:T(8,128)(2,1)S(1)}, bf16[768,128]{1,0:T(8,128)(2,1)S(1)}, u32[]{:S(2)}, u32[]{:S(2)}) collective-permute-start(bf16[768,128]{1,0:T(8,128)(2,1)S(1)} %pad_maximum_fusion.1), channel_id=1, source_target_pairs={{0,64},{8,72},{16,80},{24,88},{1,65},{9,73},{17,81},{25,89},{2,66}... | collective-permute-start | bytes 589832 | tf_op jit(solution)/shard_map/ppermute | solution.py:237
  28.0 1.3 %collective-permute-start.5 = (bf16[768,128]{1,0:T(8,128)(2,1)S(1)}, bf16[768,128]{1,0:T(8,128)(2,1)S(1)}, u32[]{:S(2)}, u32[]{:S(2)}) collective-permute-start(bf16[768,128]{1,0:T(8,128)(2,1)S(1)} %pad_maximum_fusion), channel_id=1, source_target_pairs={{0,32},{8,40},{16,48},{24,56},{1,33},{9,41},{17,49},{25,57},{2,34}... | collective-permute-start | bytes 589832 | tf_op jit(solution)/shard_map/ppermute | solution.py:237
  29.4 1.3 %collective-permute-start.3 = (bf16[768,128]{1,0:T(8,128)(2,1)S(1)}, bf16[768,128]{1,0:T(8,128)(2,1)S(1)}, u32[]{:S(2)}, u32[]{:S(2)}) collective-permute-start(bf16[768,128]{1,0:T(8,128)(2,1)S(1)} %pad_maximum_fusion), channel_id=1, source_target_pairs={{0,96},{8,104},{16,112},{24,120},{1,97},{9,105},{17,113},{25,121},... | collective-permute-start | bytes 589832 | tf_op jit(solution)/shard_map/ppermute | solution.py:237
  30.7 2.3 %shard_map.51 = bf16[16,64,896]{2,1,0:T(8,128)(2,1)} custom-call(bf16[64,1024]{1,0:T(8,128)(2,1)} %bitcast.26), custom_call_target="tpu_custom_call" | custom-call | tf_op jit(solution)/shard_map/pallas_call | solution.py:211
  33.7 4.8 %all-to-all-start.1 = ((bf16[16,64,896]{2,1,0:T(8,128)(2,1)}), bf16[16,64,896]{2,1,0:T(8,128)(2,1)S(1)}, u32[]{:S(2)}, u32[]{:S(2)}) async-start(bf16[16,64,896]{2,1,0:T(8,128)(2,1)} %shard_map.51), calls=%async_computation.1 | async-start | bytes 3670016 | tf_op jit(solution)/shard_map/all_to_all | solution.py:219
  38.7 1.9 %collective-permute-start.10 = (bf16[768,128]{1,0:T(8,128)(2,1)S(1)}, bf16[768,128]{1,0:T(8,128)(2,1)S(1)}, u32[]{:S(2)}, u32[]{:S(2)}) collective-permute-start(bf16[768,128]{1,0:T(8,128)(2,1)S(1)} %select_select_fusion.2.p0), channel_id=1, source_target_pairs={{0,4},{1,5},{2,6},{3,7},{4,0},{5,1},{6,2},{7,3},{8,12},{9,13},{10,... | collective-permute-start | bytes 589832 | tf_op jit(solution)/shard_map/ppermute | solution.py:242
  40.7 1.5 %collective-permute-start.9 = (bf16[768,128]{1,0:T(8,128)(2,1)S(1)}, bf16[768,128]{1,0:T(8,128)(2,1)S(1)}, u32[]{:S(2)}, u32[]{:S(2)}) collective-permute-start(bf16[768,128]{1,0:T(8,128)(2,1)S(1)} %select_select_fusion.2.p0), channel_id=1, source_target_pairs={{0,6},{1,7},{2,0},{3,1},{4,2},{5,3},{6,4},{7,5},{8,14},{9,15},{10,... | collective-permute-start | bytes 589832 | tf_op jit(solution)/shard_map/ppermute | solution.py:242
  42.9 4.3 %collective-permute-done.10.p3 = bf16[768,128]{1,0:T(8,128)(2,1)S(1)} collective-permute-done((bf16[768,128]{1,0:T(8,128)(2,1)S(1)}, bf16[768,128]{1,0:T(8,128)(2,1)S(1)}, u32[]{:S(2)}, u32[]{:S(2)}) %collective-permute-start.10) | collective-permute-done | bytes 196640 | tf_op jit(solution)/shard_map/ppermute | solution.py:242
  47.2 2.4 %collective-permute-done.9.p2 = bf16[768,128]{1,0:T(8,128)(2,1)S(1)} collective-permute-done((bf16[768,128]{1,0:T(8,128)(2,1)S(1)}, bf16[768,128]{1,0:T(8,128)(2,1)S(1)}, u32[]{:S(2)}, u32[]{:S(2)}) %collective-permute-start.9) | collective-permute-done | bytes 196640 | tf_op jit(solution)/shard_map/ppermute | solution.py:242
  50.1 1.3 %collective-permute-start.18 = (bf16[2048,128]{1,0:T(8,128)(2,1)S(1)}, bf16[2048,128]{1,0:T(8,128)(2,1)}, u32[]{:S(2)}, u32[]{:S(2)}) collective-permute-start(bf16[2048,128]{1,0:T(8,128)(2,1)S(1)} %bitcast.20), channel_id=1, source_target_pairs={{0,4},{1,5},{2,6},{3,7},{4,0},{5,1},{6,2},{7,3},{8,12},{9,13},{10,... | collective-permute-start | bytes 1572872 | tf_op jit(solution)/shard_map/ppermute | solution.py:243
  54.0 5.9 %shard_map.49.low = bf16[2048,1024]{1,0:T(8,128)(2,1)S(1)} custom-call(s32[4]{0:T(128)S(1)} %copy-done.7, bf16[2048,2048]{1,0:T(8,128)(2,1)S(1)} %bitcast.12, bf16[2,1024,1024]{2,1,0:T(8,128)(2,1)S(1)} %copy-done), custom_call_target="tpu_custom_call" | custom-call | flops 42949672 | bytes 200000 | tf_op jit(solution)/shard_map/pallas_call | solution.py:268
  60.0 2.0 %copy-done.2 = bf16[2048,1024]{1,0:T(8,128)(2,1)} copy-done((bf16[2048,1024]{1,0:T(8,128)(2,1)}, bf16[2048,1024]{1,0:T(8,128)(2,1)S(1)}, u32[]{:S(2)}) %copy-start.2) | copy-done | bytes 4194328
  62.9 1.2 %copy-done.9 = bf16[512,1024]{1,0:T(8,128)(2,1)S(1)} copy-done((bf16[512,1024]{1,0:T(8,128)(2,1)S(1)}, bf16[512,1024]{1,0:T(8,128)(2,1)}, u32[]{:S(2)}) %copy-start.9) | copy-done | bytes 1048600
  64.1 1.5 %shard_map.52 = (bf16[256,1024]{1,0:T(8,128)(2,1)S(1)}, f32[256,1024]{1,0:T(8,128)S(1)}) custom-call(bf16[512,1024]{1,0:T(8,128)(2,1)S(1)} %copy-done.9, bf16[1024,128]{1,0:T(8,128)(2,1)S(1)} %bitcast.23, bf16[1024,896]{1,0:T(8,128)(2,1)S(1)} %bitcast.16), custom_call_target="tpu_custom_call" | custom-call | flops 1073741824 | bytes 5000000 | tf_op jit(solution)/shard_map/pallas_call | solution.py:277
  66.1 2.7 %collective-permute-start.17 = (bf16[256,1024]{1,0:T(8,128)(2,1)S(1)}, bf16[256,1024]{1,0:T(8,128)(2,1)S(1)}, u32[]{:S(2)}, u32[]{:S(2)}) collective-permute-start(bf16[256,1024]{1,0:T(8,128)(2,1)S(1)} %get-tuple-element.42.a), channel_id=1, source_target_pairs={{0,96},{8,104},{16,112},{24,120},{32,0},{40,8},{48,16},{56,24},{64... | collective-permute-start | bytes 1572872 | tf_op jit(solution)/shard_map/ppermute | solution.py:294
  69.3 1.5 %collective-permute-start.15 = (bf16[256,1024]{1,0:T(8,128)(2,1)S(1)}, bf16[256,1024]{1,0:T(8,128)(2,1)S(1)}, u32[]{:S(2)}, u32[]{:S(2)}) collective-permute-start(bf16[256,1024]{1,0:T(8,128)(2,1)S(1)} %get-tuple-element.42.a), channel_id=1, source_target_pairs={{0,24},{8,0},{16,8},{24,16},{32,56},{40,32},{48,40},{56,48},{64,88... | collective-permute-start | bytes 1572872 | tf_op jit(solution)/shard_map/ppermute | solution.py:292
  70.8 8.7 %shard_map.53.k = f32[2048,1024]{1,0:T(8,128)S(1)} custom-call(s32[4]{0:T(128)S(1)} %copy-done.7, bf16[1024,128]{1,0:T(8,128)(2,1)S(1)} %bitcast.24, bf16[1024,896]{1,0:T(8,128)(2,1)S(1)} %bitcast.17, bf16[2048,128]{1,0:T(8,128)(2,1)S(1)} %bitcast.22, bf16[2048,128]{1,0:T(8,128)(2,1)} %collective-permute-done.6.p1, ...), custom_call_target="tpu_custom_call" | custom-call | flops 4294967296 | bytes 14000000 | tf_op jit(solution)/shard_map/pallas_call | solution.py:303
  80.3 2.2 %collective-permute-done.16.c = bf16[256,1024]{1,0:T(8,128)(2,1)S(1)} collective-permute-done((bf16[256,1024]{1,0:T(8,128)(2,1)S(1)}, bf16[256,1024]{1,0:T(8,128)(2,1)S(1)}, u32[]{:S(2)}, u32[]{:S(2)}) %collective-permute-start.16) | collective-permute-done | bytes 524320 | tf_op jit(solution)/shard_map/ppermute | solution.py:293
  82.5 1.5 %collective-permute-done.15.b = bf16[256,1024]{1,0:T(8,128)(2,1)S(1)} collective-permute-done((bf16[256,1024]{1,0:T(8,128)(2,1)S(1)}, bf16[256,1024]{1,0:T(8,128)(2,1)S(1)}, u32[]{:S(2)}, u32[]{:S(2)}) %collective-permute-start.15) | collective-permute-done | bytes 524320 | tf_op jit(solution)/shard_map/ppermute | solution.py:292
  84.0 2.0 %shard_map.54 = (bf16[256,1024]{1,0:T(8,128)(2,1)S(1)}, bf16[1024,1024]{1,0:T(8,128)(2,1)S(1)}) custom-call(s32[4]{0:T(128)S(1)} %copy-done.7, bf16[256,1024]{1,0:T(8,128)(2,1)S(1)} %get-tuple-element.42.a, bf16[256,1024]{1,0:T(8,128)(2,1)S(1)} %collective-permute-done.15.b, bf16[256,1024]{1,0:T(8,128)(2,1)S(1)} %collective-permute-done.16.c, ...), custom_call_target="tpu_custom_call" | custom-call | flops 1073741824 | bytes 8000000 | tf_op jit(solution)/shard_map/pallas_call | solution.py:313
  87.3 1.7 %collective-permute-start.23 = (bf16[256,1024]{1,0:T(8,128)(2,1)S(1)}, bf16[256,1024]{1,0:T(8,128)(2,1)S(1)}, u32[]{:S(2)}, u32[]{:S(2)}) collective-permute-start(bf16[256,1024]{1,0:T(8,128)(2,1)S(1)} %get-tuple-element.51.a), channel_id=1, source_target_pairs={{0,24},{8,0},{16,8},{24,16},{32,56},{40,32},{48,40},{56,48},{64,88... | collective-permute-start | bytes 1572872 | tf_op jit(solution)/shard_map/ppermute | solution.py:292
  89.0 2.3 %shard_map.55.s0 = bf16[1024,1024]{1,0:T(8,128)(2,1)S(1)} custom-call(bf16[1024,1024]{1,0:T(8,128)(2,1)S(1)} %get-tuple-element.52.rhs, bf16[2,1024,1024]{2,1,0:T(8,128)(2,1)S(1)} %copy-done.1), custom_call_target="tpu_custom_call" | custom-call | flops 2147483648 | bytes 6000000 | tf_op jit(solution)/shard_map/pallas_call | solution.py:324
  91.4 6.0 %shard_map.56.res = f32[2048,1024]{1,0:T(8,128)S(1)} custom-call(bf16[1024,1024]{1,0:T(8,128)(2,1)S(1)} %shard_map.55.s0, bf16[2048,2048]{1,0:T(8,128)(2,1)S(1)} %bitcast.15, f32[2048,1024]{1,0:T(8,128)S(1)} %shard_map.53.k), custom_call_target="tpu_custom_call", output_to_operand_aliasing={{}: (2, {})} | custom-call | flops 4294967296 | bytes 22000000 | tf_op jit(solution)/shard_map/pallas_call | solution.py:334
  97.4 1.3 %collective-permute-done.25.d = bf16[256,1024]{1,0:T(8,128)(2,1)S(1)} collective-permute-done((bf16[256,1024]{1,0:T(8,128)(2,1)S(1)}, bf16[256,1024]{1,0:T(8,128)(2,1)S(1)}, u32[]{:S(2)}, u32[]{:S(2)}) %collective-permute-start.25) | collective-permute-done | bytes 524320 | tf_op jit(solution)/shard_map/ppermute | solution.py:294
  99.3 1.5 %collective-permute-done.23.b = bf16[256,1024]{1,0:T(8,128)(2,1)S(1)} collective-permute-done((bf16[256,1024]{1,0:T(8,128)(2,1)S(1)}, bf16[256,1024]{1,0:T(8,128)(2,1)S(1)}, u32[]{:S(2)}, u32[]{:S(2)}) %collective-permute-start.23) | collective-permute-done | bytes 524320 | tf_op jit(solution)/shard_map/ppermute | solution.py:292
  100.8 6.8 %shard_map.57 = bf16[2048,1024]{1,0:T(8,128)(2,1)} custom-call(s32[4]{0:T(128)S(1)} %copy-done.7, bf16[256,1024]{1,0:T(8,128)(2,1)S(1)} %get-tuple-element.51.a, bf16[256,1024]{1,0:T(8,128)(2,1)S(1)} %collective-permute-done.23.b, bf16[256,1024]{1,0:T(8,128)(2,1)S(1)} %collective-permute-done.24.c, bf16[256,1024]{1,0:T(8,128)(2,1)S(1)} %collective-permute-done.25.d, ...), custom_call_target="tpu_custom_call" | custom-call | flops 4294967296 | bytes 18000000 | tf_op jit(solution)/shard_map/pallas_call | solution.py:349
  (72 shorter events, 11.7 us)
Async XLA Ops:
  3.5 18.5 %collective-permute-start = (bf16[1024,128]{1,0:T(8,128)(2,1)}, bf16[1024,128]{1,0:T(8,128)(2,1)S(1)}, u32[]{:S(2)}, u32[]{:S(2)}) collective-permute-start(bf16[1024,128]{1,0:T(8,128)(2,1)} %get-tuple-element.29), channel_id=1, source_target_pairs={{0,24},{8,0},{1,25},{9,1},{2,26},{10,2},{3,27},{11,3},{4,28},{12,4... | collective-permute-start | bytes 786440 | tf_op jit(solution)/shard_map/ppermute | solution.py:228
  4.8 17.2 %collective-permute-start.1 = (bf16[1024,128]{1,0:T(8,128)(2,1)}, bf16[1024,128]{1,0:T(8,128)(2,1)S(1)}, u32[]{:S(2)}, u32[]{:S(2)}) collective-permute-start(bf16[1024,128]{1,0:T(8,128)(2,1)} %get-tuple-element.30), channel_id=1, source_target_pairs={{0,16},{8,24},{1,17},{9,25},{2,18},{10,26},{3,19},{11,27},{4,20},{... | collective-permute-start | bytes 786440 | tf_op jit(solution)/shard_map/ppermute | solution.py:228
  6.1 15.9 %collective-permute-start.2 = (bf16[1024,128]{1,0:T(8,128)(2,1)}, bf16[1024,128]{1,0:T(8,128)(2,1)S(1)}, u32[]{:S(2)}, u32[]{:S(2)}) collective-permute-start(bf16[1024,128]{1,0:T(8,128)(2,1)} %get-tuple-element.31), channel_id=1, source_target_pairs={{0,8},{8,16},{1,9},{9,17},{2,10},{10,18},{3,11},{11,19},{4,12},{12... | collective-permute-start | bytes 786440 | tf_op jit(solution)/shard_map/ppermute | solution.py:228
  6.8 31.9 %collective-permute-start.7 = (bf16[2048,128]{1,0:T(8,128)(2,1)S(1)}, bf16[2048,128]{1,0:T(8,128)(2,1)}, u32[]{:S(2)}, u32[]{:S(2)}) collective-permute-start(bf16[2048,128]{1,0:T(8,128)(2,1)S(1)} %bitcast.18), channel_id=1, source_target_pairs={{0,6},{1,7},{2,0},{3,1},{4,2},{5,3},{6,4},{7,5},{8,14},{9,15},{10,... | collective-permute-start | bytes 1572872 | tf_op jit(solution)/shard_map/ppermute | solution.py:225
  10.9 27.8 %collective-permute-start.6 = (bf16[2048,128]{1,0:T(8,128)(2,1)S(1)}, bf16[2048,128]{1,0:T(8,128)(2,1)}, u32[]{:S(2)}, u32[]{:S(2)}) collective-permute-start(bf16[2048,128]{1,0:T(8,128)(2,1)S(1)} %bitcast.19), channel_id=1, source_target_pairs={{0,2},{1,3},{2,4},{3,5},{4,6},{5,7},{6,0},{7,1},{8,10},{9,11},{10,... | collective-permute-start | bytes 1572872 | tf_op jit(solution)/shard_map/ppermute | solution.py:225
  12.6 20.4 %all-to-all-start = ((bf16[16,64,128]{2,1,0:T(8,128)(2,1)}), bf16[16,64,128]{2,1,0:T(8,128)(2,1)S(1)}, u32[]{:S(2)}, u32[]{:S(2)}) async-start(bf16[16,64,128]{2,1,0:T(8,128)(2,1)} %shard_map.50), calls=%async_computation | async-start | bytes 524288 | tf_op jit(solution)/shard_map/all_to_all | solution.py:219
  23.0 28.4 %copy-start.7 = (s32[4]{0:T(128)S(1)}, s32[4]{0:T(128)}, u32[]{:S(2)}) copy-start(s32[4]{0:T(128)} %pad_add_fusion.at) | copy-start | bytes 52
  23.1 15.5 %collective-permute-start.4 = (bf16[768,128]{1,0:T(8,128)(2,1)S(1)}, bf16[768,128]{1,0:T(8,128)(2,1)S(1)}, u32[]{:S(2)}, u32[]{:S(2)}) collective-permute-start(bf16[768,128]{1,0:T(8,128)(2,1)S(1)} %pad_maximum_fusion.1), channel_id=1, source_target_pairs={{0,64},{8,72},{16,80},{24,88},{1,65},{9,73},{17,81},{25,89},{2,66}... | collective-permute-start | bytes 589832 | tf_op jit(solution)/shard_map/ppermute | solution.py:237
  28.0 10.5 %collective-permute-start.5 = (bf16[768,128]{1,0:T(8,128)(2,1)S(1)}, bf16[768,128]{1,0:T(8,128)(2,1)S(1)}, u32[]{:S(2)}, u32[]{:S(2)}) collective-permute-start(bf16[768,128]{1,0:T(8,128)(2,1)S(1)} %pad_maximum_fusion), channel_id=1, source_target_pairs={{0,32},{8,40},{16,48},{24,56},{1,33},{9,41},{17,49},{25,57},{2,34}... | collective-permute-start | bytes 589832 | tf_op jit(solution)/shard_map/ppermute | solution.py:237
  29.4 9.2 %collective-permute-start.3 = (bf16[768,128]{1,0:T(8,128)(2,1)S(1)}, bf16[768,128]{1,0:T(8,128)(2,1)S(1)}, u32[]{:S(2)}, u32[]{:S(2)}) collective-permute-start(bf16[768,128]{1,0:T(8,128)(2,1)S(1)} %pad_maximum_fusion), channel_id=1, source_target_pairs={{0,96},{8,104},{16,112},{24,120},{1,97},{9,105},{17,113},{25,121},... | collective-permute-start | bytes 589832 | tf_op jit(solution)/shard_map/ppermute | solution.py:237
  33.7 28.2 %all-to-all-start.1 = ((bf16[16,64,896]{2,1,0:T(8,128)(2,1)}), bf16[16,64,896]{2,1,0:T(8,128)(2,1)S(1)}, u32[]{:S(2)}, u32[]{:S(2)}) async-start(bf16[16,64,896]{2,1,0:T(8,128)(2,1)} %shard_map.51), calls=%async_computation.1 | async-start | bytes 3670016 | tf_op jit(solution)/shard_map/all_to_all | solution.py:219
  38.6 15.5 %slice-start = ((s8[8388608]{0:T(1024)(128)(4,1)}), s8[4194304]{0:T(1024)(128)(4,1)S(1)}, s32[]{:S(2)}) async-start(s8[8388608]{0:T(1024)(128)(4,1)} %bitcast.10), calls=%async_computation.2 | async-start | bytes 8388608
  38.7 8.5 %collective-permute-start.10 = (bf16[768,128]{1,0:T(8,128)(2,1)S(1)}, bf16[768,128]{1,0:T(8,128)(2,1)S(1)}, u32[]{:S(2)}, u32[]{:S(2)}) collective-permute-start(bf16[768,128]{1,0:T(8,128)(2,1)S(1)} %select_select_fusion.2.p0), channel_id=1, source_target_pairs={{0,4},{1,5},{2,6},{3,7},{4,0},{5,1},{6,2},{7,3},{8,12},{9,13},{10,... | collective-permute-start | bytes 589832 | tf_op jit(solution)/shard_map/ppermute | solution.py:242
  40.7 8.9 %collective-permute-start.9 = (bf16[768,128]{1,0:T(8,128)(2,1)S(1)}, bf16[768,128]{1,0:T(8,128)(2,1)S(1)}, u32[]{:S(2)}, u32[]{:S(2)}) collective-permute-start(bf16[768,128]{1,0:T(8,128)(2,1)S(1)} %select_select_fusion.2.p0), channel_id=1, source_target_pairs={{0,6},{1,7},{2,0},{3,1},{4,2},{5,3},{6,4},{7,5},{8,14},{9,15},{10,... | collective-permute-start | bytes 589832 | tf_op jit(solution)/shard_map/ppermute | solution.py:242
  42.1 7.5 %collective-permute-start.8 = (bf16[768,128]{1,0:T(8,128)(2,1)S(1)}, bf16[768,128]{1,0:T(8,128)(2,1)S(1)}, u32[]{:S(2)}, u32[]{:S(2)}) collective-permute-start(bf16[768,128]{1,0:T(8,128)(2,1)S(1)} %select_select_fusion.2.p0), channel_id=1, source_target_pairs={{0,2},{1,3},{2,4},{3,5},{4,6},{5,7},{6,0},{7,1},{8,10},{9,11},{10,... | collective-permute-start | bytes 589832 | tf_op jit(solution)/shard_map/ppermute | solution.py:242
  42.9 8.5 %collective-permute-start.11 = (bf16[768,128]{1,0:T(8,128)(2,1)S(1)}, bf16[768,128]{1,0:T(8,128)(2,1)S(1)}, u32[]{:S(2)}, u32[]{:S(2)}) collective-permute-start(bf16[768,128]{1,0:T(8,128)(2,1)S(1)} %select_select_fusion.2.p0), channel_id=1, source_target_pairs={{0,1},{1,0},{2,3},{3,2},{4,5},{5,4},{6,7},{7,6},{8,9},{9,8},{10,11... | collective-permute-start | bytes 589832 | tf_op jit(solution)/shard_map/ppermute | solution.py:244
  47.2 4.1 %collective-permute-start.14 = (bf16[768,128]{1,0:T(8,128)(2,1)S(1)}, bf16[768,128]{1,0:T(8,128)(2,1)S(1)}, u32[]{:S(2)}, u32[]{:S(2)}) collective-permute-start(bf16[768,128]{1,0:T(8,128)(2,1)S(1)} %collective-permute-done.10.p3), channel_id=1, source_target_pairs={{0,1},{1,0},{2,3},{3,2},{4,5},{5,4},{6,7},{7,6},{8,9},{9,8},{10,11... | collective-permute-start | bytes 589832 | tf_op jit(solution)/shard_map/ppermute | solution.py:244
  49.6 1.8 %collective-permute-start.13 = (bf16[768,128]{1,0:T(8,128)(2,1)S(1)}, bf16[768,128]{1,0:T(8,128)(2,1)S(1)}, u32[]{:S(2)}, u32[]{:S(2)}) collective-permute-start(bf16[768,128]{1,0:T(8,128)(2,1)S(1)} %collective-permute-done.9.p2), channel_id=1, source_target_pairs={{0,1},{1,0},{2,3},{3,2},{4,5},{5,4},{6,7},{7,6},{8,9},{9,8},{10,11... | collective-permute-start | bytes 589832 | tf_op jit(solution)/shard_map/ppermute | solution.py:244
  49.6 1.8 %collective-permute-start.12 = (bf16[768,128]{1,0:T(8,128)(2,1)S(1)}, bf16[768,128]{1,0:T(8,128)(2,1)S(1)}, u32[]{:S(2)}, u32[]{:S(2)}) collective-permute-start(bf16[768,128]{1,0:T(8,128)(2,1)S(1)} %collective-permute-done.8.p1), channel_id=1, source_target_pairs={{0,1},{1,0},{2,3},{3,2},{4,5},{5,4},{6,7},{7,6},{8,9},{9,8},{10,11... | collective-permute-start | bytes 589832 | tf_op jit(solution)/shard_map/ppermute | solution.py:244
  50.1 15.6 %collective-permute-start.18 = (bf16[2048,128]{1,0:T(8,128)(2,1)S(1)}, bf16[2048,128]{1,0:T(8,128)(2,1)}, u32[]{:S(2)}, u32[]{:S(2)}) collective-permute-start(bf16[2048,128]{1,0:T(8,128)(2,1)S(1)} %bitcast.20), channel_id=1, source_target_pairs={{0,4},{1,5},{2,6},{3,7},{4,0},{5,1},{6,2},{7,3},{8,12},{9,13},{10,... | collective-permute-start | bytes 1572872 | tf_op jit(solution)/shard_map/ppermute | solution.py:243
  52.4 16.3 %collective-permute-start.19 = (bf16[2048,128]{1,0:T(8,128)(2,1)S(1)}, bf16[2048,128]{1,0:T(8,128)(2,1)}, u32[]{:S(2)}, u32[]{:S(2)}) collective-permute-start(bf16[2048,128]{1,0:T(8,128)(2,1)S(1)} %bitcast.21), channel_id=1, source_target_pairs={{0,1},{1,0},{2,3},{3,2},{4,5},{5,4},{6,7},{7,6},{8,9},{9,8},{10,11... | collective-permute-start | bytes 1572872 | tf_op jit(solution)/shard_map/ppermute | solution.py:298
  52.7 16.6 %collective-permute-start.20 = (bf16[2048,128]{1,0:T(8,128)(2,1)}, bf16[2048,128]{1,0:T(8,128)(2,1)}, u32[]{:S(2)}, u32[]{:S(2)}) collective-permute-start(bf16[2048,128]{1,0:T(8,128)(2,1)} %collective-permute-done.6.p1), channel_id=1, source_target_pairs={{0,1},{1,0},{2,3},{3,2},{4,5},{5,4},{6,7},{7,6},{8,9},{9,8},{10,11... | collective-permute-start | bytes 1572872 | tf_op jit(solution)/shard_map/ppermute | solution.py:298
  53.7 17.1 %collective-permute-start.21 = (bf16[2048,128]{1,0:T(8,128)(2,1)}, bf16[2048,128]{1,0:T(8,128)(2,1)}, u32[]{:S(2)}, u32[]{:S(2)}) collective-permute-start(bf16[2048,128]{1,0:T(8,128)(2,1)} %collective-permute-done.7.p2), channel_id=1, source_target_pairs={{0,1},{1,0},{2,3},{3,2},{4,5},{5,4},{6,7},{7,6},{8,9},{9,8},{10,11... | collective-permute-start | bytes 1572872 | tf_op jit(solution)/shard_map/ppermute | solution.py:298
  64.1 27.2 %slice-start.2 = ((s8[8388608]{0:T(1024)(128)(4,1)}), s8[4194304]{0:T(1024)(128)(4,1)S(1)}, s32[]{:S(2)}) async-start(s8[8388608]{0:T(1024)(128)(4,1)} %bitcast.13), calls=%async_computation.4 | async-start | bytes 8388608
  65.7 25.7 %slice-start.3 = ((s8[8388608]{0:T(1024)(128)(4,1)}), s8[4194304]{0:T(1024)(128)(4,1)S(1)}, s32[]{:S(2)}) async-start(s8[8388608]{0:T(1024)(128)(4,1)} %bitcast.13), calls=%async_computation.5 | async-start | bytes 8388608
  65.7 5.1 %collective-permute-start.22 = (bf16[2048,128]{1,0:T(8,128)(2,1)}, bf16[2048,128]{1,0:T(8,128)(2,1)S(1)}, u32[]{:S(2)}, u32[]{:S(2)}) collective-permute-start(bf16[2048,128]{1,0:T(8,128)(2,1)} %collective-permute-done.18.p3), channel_id=1, source_target_pairs={{0,1},{1,0},{2,3},{3,2},{4,5},{5,4},{6,7},{7,6},{8,9},{9,8},{10,11... | collective-permute-start | bytes 1572872 | tf_op jit(solution)/shard_map/ppermute | solution.py:298
  66.1 14.3 %collective-permute-start.17 = (bf16[256,1024]{1,0:T(8,128)(2,1)S(1)}, bf16[256,1024]{1,0:T(8,128)(2,1)S(1)}, u32[]{:S(2)}, u32[]{:S(2)}) collective-permute-start(bf16[256,1024]{1,0:T(8,128)(2,1)S(1)} %get-tuple-element.42.a), channel_id=1, source_target_pairs={{0,96},{8,104},{16,112},{24,120},{32,0},{40,8},{48,16},{56,24},{64... | collective-permute-start | bytes 1572872 | tf_op jit(solution)/shard_map/ppermute | solution.py:294
  68.8 13.8 %collective-permute-start.16 = (bf16[256,1024]{1,0:T(8,128)(2,1)S(1)}, bf16[256,1024]{1,0:T(8,128)(2,1)S(1)}, u32[]{:S(2)}, u32[]{:S(2)}) collective-permute-start(bf16[256,1024]{1,0:T(8,128)(2,1)S(1)} %get-tuple-element.42.a), channel_id=1, source_target_pairs={{0,8},{8,16},{16,24},{24,0},{32,40},{40,48},{48,56},{56,32},{64,72... | collective-permute-start | bytes 1572872 | tf_op jit(solution)/shard_map/ppermute | solution.py:293
  69.3 14.7 %collective-permute-start.15 = (bf16[256,1024]{1,0:T(8,128)(2,1)S(1)}, bf16[256,1024]{1,0:T(8,128)(2,1)S(1)}, u32[]{:S(2)}, u32[]{:S(2)}) collective-permute-start(bf16[256,1024]{1,0:T(8,128)(2,1)S(1)} %get-tuple-element.42.a), channel_id=1, source_target_pairs={{0,24},{8,0},{16,8},{24,16},{32,56},{40,32},{48,40},{56,48},{64,88... | collective-permute-start | bytes 1572872 | tf_op jit(solution)/shard_map/ppermute | solution.py:292
  86.1 12.7 %collective-permute-start.25 = (bf16[256,1024]{1,0:T(8,128)(2,1)S(1)}, bf16[256,1024]{1,0:T(8,128)(2,1)S(1)}, u32[]{:S(2)}, u32[]{:S(2)}) collective-permute-start(bf16[256,1024]{1,0:T(8,128)(2,1)S(1)} %get-tuple-element.51.a), channel_id=1, source_target_pairs={{0,96},{8,104},{16,112},{24,120},{32,0},{40,8},{48,16},{56,24},{64... | collective-permute-start | bytes 1572872 | tf_op jit(solution)/shard_map/ppermute | solution.py:294
  87.0 12.3 %collective-permute-start.24 = (bf16[256,1024]{1,0:T(8,128)(2,1)S(1)}, bf16[256,1024]{1,0:T(8,128)(2,1)S(1)}, u32[]{:S(2)}, u32[]{:S(2)}) collective-permute-start(bf16[256,1024]{1,0:T(8,128)(2,1)S(1)} %get-tuple-element.51.a), channel_id=1, source_target_pairs={{0,8},{8,16},{16,24},{24,0},{32,40},{40,48},{48,56},{56,32},{64,72... | collective-permute-start | bytes 1572872 | tf_op jit(solution)/shard_map/ppermute | solution.py:293
  87.3 13.6 %collective-permute-start.23 = (bf16[256,1024]{1,0:T(8,128)(2,1)S(1)}, bf16[256,1024]{1,0:T(8,128)(2,1)S(1)}, u32[]{:S(2)}, u32[]{:S(2)}) collective-permute-start(bf16[256,1024]{1,0:T(8,128)(2,1)S(1)} %get-tuple-element.51.a), channel_id=1, source_target_pairs={{0,24},{8,0},{16,8},{24,16},{32,56},{40,32},{48,40},{56,48},{64,88... | collective-permute-start | bytes 1572872 | tf_op jit(solution)/shard_map/ppermute | solution.py:292
  (10 other events, 61.3 us)
